TPU v7x, 32 devices: a whole 2x2x4 slice. The times are simulated.
32 devices in a mesh: dp: 8 (over y, x, core), tensor: 4 (over z).
Axes of the slice: x: 2, y: 2, z: 4, core: 2. Of those that a mesh axis runs over, the one named last changes fastest.
Arguments:
- tokens: bfloat16 [8192, 1536], P(('dp', 'tensor')), may hold values from -6 to 6
- clip_ids: int32 [8192], P('dp'), may hold values from 0 to 2, as said below
- positions: int32 [8192], P('dp'), may hold values from 0 to 2047, as said below
- timesteps: int32 [24], P('dp'), may hold values from 0 to 999
- text_states: bfloat16 [24, 128, 4096], P('dp'), may hold values from -6 to 6
- text_lengths: int32 [24], P('dp'), may hold values from 1 to 128
- out_grad: bfloat16 [8192, 1536], P(('dp', 'tensor')), may hold values from -6 to 6
- attn_gain: float32 [1536], replicated, may hold values from 0.5 to 1.5
- ffn_gain: float32 [1536], replicated, may hold values from 0.5 to 1.5
- query_gain: float32 [64], replicated, may hold values from 0.5 to 1.5
- key_gain: float32 [64], replicated, may hold values from 0.5 to 1.5
- cross_gate: float32 [24], replicated, may hold values from 0.3 to 1.5
- w_query: bfloat16 [1536, 1536], P(None, 'tensor'), may hold values from -0.15625 to 0.15625
- w_key: bfloat16 [1536, 1536], P(None, 'tensor'), may hold values from -0.15625 to 0.15625
- w_value: bfloat16 [1536, 1536], P(None, 'tensor'), may hold values from -0.15625 to 0.15625
- w_out: bfloat16 [1536, 1536], P('tensor'), may hold values from -1.25 to 1.25
- w_text_key: bfloat16 [4096, 1536], P(None, 'tensor'), may hold values from -0.09375 to 0.09375
- w_text_value: bfloat16 [4096, 1536], P(None, 'tensor'), may hold values from -0.09375 to 0.09375
- w_ada: bfloat16 [1024, 6144], P(None, 'tensor'), may hold values from -0.1875 to 0.1875
- w_gate: bfloat16 [1536, 4096], P(None, 'tensor'), may hold values from -0.15625 to 0.15625
- w_up: bfloat16 [1536, 4096], P(None, 'tensor'), may hold values from -0.15625 to 0.15625
- w_down: bfloat16 [4096, 1536], P('tensor'), may hold values from -0.09375 to 0.09375
Outputs:
- block_out: bfloat16 [8192, 1536], P(('dp', 'tensor'))
- input_grad: float32 [8192, 1536], P(('dp', 'tensor'))
- attn_gain_grad: float32 [1536], replicated
- ffn_gain_grad: float32 [1536], replicated
- query_gain_grad: float32 [64], replicated
- key_gain_grad: float32 [64], replicated
- cross_gate_grad: float32 [24], replicated
- w_query_grad: float32 [1536, 1536], P('dp', 'tensor')
- w_key_grad: float32 [1536, 1536], P('dp', 'tensor')
- w_value_grad: float32 [1536, 1536], P('dp', 'tensor')
- w_out_grad: float32 [1536, 1536], P('tensor', 'dp')
- w_text_key_grad: float32 [4096, 1536], P('dp', 'tensor')
- w_text_value_grad: float32 [4096, 1536], P('dp', 'tensor')
- w_ada_grad: float32 [1024, 6144], P('dp', 'tensor')
- w_gate_grad: float32 [1536, 4096], P('dp', 'tensor')
- w_up_grad: float32 [1536, 4096], P('dp', 'tensor')
- w_down_grad: float32 [4096, 1536], P('tensor', 'dp')
Inputs may be any that keep to these rules, and one draw needn't show every extreme that they name: `clip_ids`: in each aligned block of 1024 tokens the clip numbers never fall, and 0, 1 and 2 each occur; clips 0 and 2 each hold fewer than 256 tokens. Within a clip the positions rise by one from token to token.
All inputs are finite; a program needn't handle non-finite values.
Results may differ from a plain program's by a relative error of at most 0.015.
Values may be sent and summed in bfloat16 or wider, within the bound.
No kernel may reach another device: no remote copies, remote signals or barrier semaphores. Data moves between devices by JAX's collectives and lax.ppermute only.
A program may use at most 256 MiB of HBM per device.

v0:
```python
import math

import jax
import jax.numpy as jnp
from jax import lax
from jax.sharding import PartitionSpec as P

epsilon = 1e-06
masked_score = -1e30


def rms_scale(values):
    return lax.rsqrt(jnp.mean(values * values, axis=-1, keepdims=True) + epsilon)


def rms_backward(grad_hat, normed, scaling):
    return scaling * (grad_hat - normed * jnp.mean(grad_hat * normed, axis=-1, keepdims=True))


def time_embed(time_steps, embed_width):
    half_width = embed_width // 2
    frequency = jnp.exp(-math.log(10000.0) * jnp.arange(half_width, dtype=jnp.float32) / half_width)
    angles = time_steps.astype(jnp.float32)[:, None] * frequency[None, :]
    return jnp.concatenate([jnp.cos(angles), jnp.sin(angles)], axis=-1)


def rotary(values, places, direction):
    head_width = values.shape[-1]
    half_width = head_width // 2
    frequency = jnp.exp(
        -math.log(10000.0) * jnp.arange(half_width, dtype=jnp.float32) * 2.0 / head_width
    )
    angles = places.astype(jnp.float32)[:, None] * frequency[None, :]
    cosine = jnp.cos(angles)[:, None, :]
    sine_part = direction * jnp.sin(angles)[:, None, :]
    lead_part = values[..., :half_width]
    tail_part = values[..., half_width:]
    return jnp.concatenate(
        [lead_part * cosine - tail_part * sine_part, lead_part * sine_part + tail_part * cosine],
        axis=-1,
    )


def clip_table(clip_rows, clip_count):
    return (clip_rows[:, None] == jnp.arange(clip_count, dtype=jnp.int32)[None, :]).astype(
        jnp.float32
    )


def softmax_parts(scores):
    highest = jnp.max(scores, axis=-1, keepdims=True)
    exponent = jnp.exp(scores - highest)
    totals = jnp.sum(exponent, axis=-1, keepdims=True)
    return (exponent / totals, highest[..., 0] + jnp.log(totals[..., 0]))


def block_scores(
    query_blk, ids_blk, key_rot, clip_ids, text_key_low, text_owner, text_live, factor
):
    self_scores = (
        jnp.einsum("qhd,khd->hqk", query_blk, key_rot, preferred_element_type=jnp.float32) * factor
    )
    same_clip = ids_blk[:, None] == clip_ids[None, :]
    self_scores = jnp.where(same_clip[None], self_scores, masked_score)
    cross_scores = (
        jnp.einsum("qhd,thd->hqt", query_blk, text_key_low, preferred_element_type=jnp.float32)
        * factor
    )
    allowed = (ids_blk[:, None] == text_owner[None, :]) & text_live[None, :]
    cross_scores = jnp.where(allowed[None], cross_scores, masked_score)
    return (self_scores, cross_scores)


def on_device(
    tokens,
    clip_ids,
    positions,
    timesteps,
    text_states,
    text_lengths,
    out_grad,
    attn_gain,
    ffn_gain,
    query_gain,
    key_gain,
    cross_gate,
    w_query,
    w_key,
    w_value,
    w_out,
    w_text_key,
    w_text_value,
    w_ada,
    w_gate,
    w_up,
    w_down,
):
    tensor_size = lax.axis_size("tensor")
    my_rank = lax.axis_index("tensor")
    local_rows = tokens.shape[0]
    group_rows = local_rows * tensor_size
    model_width = tokens.shape[1]
    head_dim = query_gain.shape[0]
    local_heads = w_query.shape[1] // head_dim
    head_cols = local_heads * head_dim
    clip_count = timesteps.shape[0]
    text_len = text_states.shape[1]
    text_rows = clip_count * text_len
    factor = 1.0 / math.sqrt(head_dim)
    highest_precision = lax.Precision.HIGHEST
    my_ids = lax.dynamic_slice_in_dim(clip_ids, my_rank * local_rows, local_rows)
    my_table = clip_table(my_ids, clip_count)
    embedded = time_embed(timesteps, w_ada.shape[0])
    condition = (embedded * jax.nn.sigmoid(embedded)).astype(jnp.bfloat16)
    mod_part = jnp.dot(condition, w_ada, preferred_element_type=jnp.float32)
    modulation = lax.all_gather(mod_part, "tensor", axis=1, tiled=True)
    per_token = jnp.dot(my_table, modulation, precision=highest_precision)
    scale_attn = per_token[:, :model_width]
    gate_attn = jnp.tanh(per_token[:, model_width : 2 * model_width])
    scale_ffn = per_token[:, 2 * model_width : 3 * model_width]
    gate_ffn = jnp.tanh(per_token[:, 3 * model_width :])
    inputs = tokens.astype(jnp.float32)
    inv_first = rms_scale(inputs)
    normed_first = inputs * inv_first
    attn_rows = (normed_first * attn_gain * (1.0 + scale_attn)).astype(jnp.bfloat16)
    attn_all = lax.all_gather(attn_rows, "tensor", axis=0, tiled=True)
    head_shape = (group_rows, local_heads, head_dim)
    queries = jnp.dot(attn_all, w_query, preferred_element_type=jnp.float32).reshape(head_shape)
    key_raw = jnp.dot(attn_all, w_key, preferred_element_type=jnp.float32).reshape(head_shape)
    value_low = (
        jnp.dot(attn_all, w_value, preferred_element_type=jnp.float32)
        .astype(jnp.bfloat16)
        .reshape(head_shape)
    )
    inv_query = rms_scale(queries)
    query_hat = queries * inv_query
    query_rot = rotary(query_hat * query_gain, positions, 1.0).astype(jnp.bfloat16)
    inv_key = rms_scale(key_raw)
    key_hat = key_raw * inv_key
    key_rot = rotary(key_hat * key_gain, positions, 1.0).astype(jnp.bfloat16)
    text_flat = text_states.reshape(text_rows, text_states.shape[2])
    text_shape = (text_rows, local_heads, head_dim)
    text_keys = jnp.dot(text_flat, w_text_key, preferred_element_type=jnp.float32).reshape(
        text_shape
    )
    inv_text = rms_scale(text_keys)
    text_hat = text_keys * inv_text
    text_key_low = (text_hat * key_gain).astype(jnp.bfloat16)
    text_value_low = (
        jnp.dot(text_flat, w_text_value, preferred_element_type=jnp.float32)
        .astype(jnp.bfloat16)
        .reshape(text_shape)
    )
    text_owner = jnp.repeat(jnp.arange(clip_count, dtype=jnp.int32), text_len)
    text_live = jnp.tile(jnp.arange(text_len, dtype=jnp.int32), clip_count) < jnp.repeat(
        text_lengths, text_len
    )
    gate_tanh = jnp.tanh(lax.dynamic_slice_in_dim(cross_gate, my_rank * local_heads, local_heads))
    block_rows = min(512, group_rows)
    offsets = jnp.arange(group_rows // block_rows, dtype=jnp.int32) * block_rows

    def forward_block(offset):
        query_blk = lax.dynamic_slice_in_dim(query_rot, offset, block_rows, 0)
        ids_blk = lax.dynamic_slice_in_dim(clip_ids, offset, block_rows, 0)
        self_scores, cross_scores = block_scores(
            query_blk, ids_blk, key_rot, clip_ids, text_key_low, text_owner, text_live, factor
        )
        self_weights, self_stat = softmax_parts(self_scores)
        cross_weights, cross_stat = softmax_parts(cross_scores)
        self_out = jnp.einsum(
            "hqk,khd->qhd",
            self_weights.astype(jnp.bfloat16),
            value_low,
            preferred_element_type=jnp.float32,
        )
        cross_out = jnp.einsum(
            "hqt,thd->qhd",
            cross_weights.astype(jnp.bfloat16),
            text_value_low,
            preferred_element_type=jnp.float32,
        )
        mixed_blk = (self_out + gate_tanh[None, :, None] * cross_out).astype(jnp.bfloat16)
        return (mixed_blk.reshape(block_rows, head_cols), self_stat, cross_stat)

    mixed_blocks, self_stats, cross_stats = lax.map(forward_block, offsets)
    mixed_heads = mixed_blocks.reshape(group_rows, head_cols)
    attn_out = lax.psum_scatter(
        jnp.dot(mixed_heads, w_out, preferred_element_type=jnp.float32),
        "tensor",
        scatter_dimension=0,
        tiled=True,
    )
    middle = inputs + gate_attn * attn_out
    inv_second = rms_scale(middle)
    normed_second = middle * inv_second
    ffn_rows = (normed_second * ffn_gain * (1.0 + scale_ffn)).astype(jnp.bfloat16)
    ffn_all = lax.all_gather(ffn_rows, "tensor", axis=0, tiled=True)
    gate_pre = jnp.dot(ffn_all, w_gate, preferred_element_type=jnp.float32)
    up_pre = jnp.dot(ffn_all, w_up, preferred_element_type=jnp.float32)
    sigmoid_gate = jax.nn.sigmoid(gate_pre)
    silu_gate = gate_pre * sigmoid_gate
    hidden = (silu_gate * up_pre).astype(jnp.bfloat16)
    ffn_out = lax.psum_scatter(
        jnp.dot(hidden, w_down, preferred_element_type=jnp.float32).astype(jnp.bfloat16),
        "tensor",
        scatter_dimension=0,
        tiled=True,
    ).astype(jnp.float32)
    block_out = (middle + gate_ffn * ffn_out).astype(jnp.bfloat16)
    grad_output = out_grad.astype(jnp.float32)
    grad_ffn_low = (grad_output * gate_ffn).astype(jnp.bfloat16)
    grad_gate_ffn = grad_output * ffn_out * (1.0 - gate_ffn * gate_ffn)
    grad_ffn_all = lax.all_gather(grad_ffn_low, "tensor", axis=0, tiled=True)
    down_grad_t = jnp.dot(grad_ffn_all.T, hidden, preferred_element_type=jnp.float32)
    grad_hidden = jnp.dot(grad_ffn_all, w_down.T, preferred_element_type=jnp.float32)
    grad_gate_low = (
        grad_hidden * up_pre * sigmoid_gate * (1.0 + gate_pre * (1.0 - sigmoid_gate))
    ).astype(jnp.bfloat16)
    grad_up_low = (grad_hidden * silu_gate).astype(jnp.bfloat16)
    gate_grad_w = jnp.dot(ffn_all.T, grad_gate_low, preferred_element_type=jnp.float32)
    up_grad_w = jnp.dot(ffn_all.T, grad_up_low, preferred_element_type=jnp.float32)
    grad_ffn_rows = lax.psum_scatter(
        jnp.dot(grad_gate_low, w_gate.T, preferred_element_type=jnp.float32)
        + jnp.dot(grad_up_low, w_up.T, preferred_element_type=jnp.float32),
        "tensor",
        scatter_dimension=0,
        tiled=True,
    )
    ffn_gain_part = jnp.sum(grad_ffn_rows * normed_second * (1.0 + scale_ffn), axis=0)
    grad_scale_ffn = grad_ffn_rows * normed_second * ffn_gain
    grad_middle = grad_output + rms_backward(
        grad_ffn_rows * ffn_gain * (1.0 + scale_ffn), normed_second, inv_second
    )
    grad_attn_low = (grad_middle * gate_attn).astype(jnp.bfloat16)
    grad_gate_attn = grad_middle * attn_out * (1.0 - gate_attn * gate_attn)
    grad_attn_all = lax.all_gather(grad_attn_low, "tensor", axis=0, tiled=True)
    out_grad_t = jnp.dot(grad_attn_all.T, mixed_heads, preferred_element_type=jnp.float32)
    grad_heads = jnp.dot(grad_attn_all, w_out.T, preferred_element_type=jnp.float32).reshape(
        head_shape
    )
    derivative_gate = 1.0 - gate_tanh * gate_tanh

    def backward_block(totals_carry, block_inputs):
        grad_key_rot, grad_value, grad_text_key, grad_text_value, grad_cross = totals_carry
        offset, self_stat, cross_stat = block_inputs
        query_blk = lax.dynamic_slice_in_dim(query_rot, offset, block_rows, 0)
        ids_blk = lax.dynamic_slice_in_dim(clip_ids, offset, block_rows, 0)
        grad_blk = lax.dynamic_slice_in_dim(grad_heads, offset, block_rows, 0)
        self_scores, cross_scores = block_scores(
            query_blk, ids_blk, key_rot, clip_ids, text_key_low, text_owner, text_live, factor
        )
        self_weights = jnp.exp(self_scores - self_stat[..., None])
        cross_weights = jnp.exp(cross_scores - cross_stat[..., None])
        self_grad_low = grad_blk.astype(jnp.bfloat16)
        cross_grad_low = (grad_blk * gate_tanh[None, :, None]).astype(jnp.bfloat16)
        cross_weights_low = cross_weights.astype(jnp.bfloat16)
        cross_out = jnp.einsum(
            "hqt,thd->qhd", cross_weights_low, text_value_low, preferred_element_type=jnp.float32
        )
        grad_cross = grad_cross + jnp.sum(grad_blk * cross_out, axis=(0, 2)) * derivative_gate
        self_dots = jnp.einsum(
            "qhd,khd->hqk", self_grad_low, value_low, preferred_element_type=jnp.float32
        )
        self_ds = (
            self_weights * (self_dots - jnp.sum(self_weights * self_dots, axis=-1, keepdims=True))
        ).astype(jnp.bfloat16)
        cross_dots = jnp.einsum(
            "qhd,thd->hqt", cross_grad_low, text_value_low, preferred_element_type=jnp.float32
        )
        cross_ds = (
            cross_weights
            * (cross_dots - jnp.sum(cross_weights * cross_dots, axis=-1, keepdims=True))
        ).astype(jnp.bfloat16)
        grad_query_blk = (
            jnp.einsum("hqk,khd->qhd", self_ds, key_rot, preferred_element_type=jnp.float32)
            + jnp.einsum("hqt,thd->qhd", cross_ds, text_key_low, preferred_element_type=jnp.float32)
        ) * factor
        grad_key_rot = (
            grad_key_rot
            + jnp.einsum("hqk,qhd->khd", self_ds, query_blk, preferred_element_type=jnp.float32)
            * factor
        )
        grad_value = grad_value + jnp.einsum(
            "hqk,qhd->khd",
            self_weights.astype(jnp.bfloat16),
            self_grad_low,
            preferred_element_type=jnp.float32,
        )
        grad_text_key = (
            grad_text_key
            + jnp.einsum("hqt,qhd->thd", cross_ds, query_blk, preferred_element_type=jnp.float32)
            * factor
        )
        grad_text_value = grad_text_value + jnp.einsum(
            "hqt,qhd->thd", cross_weights_low, cross_grad_low, preferred_element_type=jnp.float32
        )
        return (
            (grad_key_rot, grad_value, grad_text_key, grad_text_value, grad_cross),
            grad_query_blk,
        )

    initial = (
        jnp.zeros(head_shape, jnp.float32),
        jnp.zeros(head_shape, jnp.float32),
        jnp.zeros(text_shape, jnp.float32),
        jnp.zeros(text_shape, jnp.float32),
        jnp.zeros((local_heads,), jnp.float32),
    )
    final_totals, grad_query_blocks = lax.scan(
        backward_block, initial, (offsets, self_stats, cross_stats)
    )
    grad_key_rot, grad_value, grad_text_key, grad_text_value, grad_cross = final_totals
    grad_query_norm = rotary(grad_query_blocks.reshape(head_shape), positions, -1.0)
    grad_key_norm = rotary(grad_key_rot, positions, -1.0)
    query_gain_part = jnp.sum(grad_query_norm * query_hat, axis=(0, 1))
    key_gain_part = jnp.sum(grad_key_norm * key_hat, axis=(0, 1)) + jnp.sum(
        grad_text_key * text_hat, axis=(0, 1)
    )
    grad_queries = (
        rms_backward(grad_query_norm * query_gain, query_hat, inv_query)
        .astype(jnp.bfloat16)
        .reshape(group_rows, head_cols)
    )
    grad_keys = (
        rms_backward(grad_key_norm * key_gain, key_hat, inv_key)
        .astype(jnp.bfloat16)
        .reshape(group_rows, head_cols)
    )
    grad_values = grad_value.astype(jnp.bfloat16).reshape(group_rows, head_cols)
    grad_text_keys = (
        rms_backward(grad_text_key * key_gain, text_hat, inv_text)
        .astype(jnp.bfloat16)
        .reshape(text_rows, head_cols)
    )
    grad_text_values = grad_text_value.astype(jnp.bfloat16).reshape(text_rows, head_cols)
    query_grad_w = jnp.dot(attn_all.T, grad_queries, preferred_element_type=jnp.float32)
    key_grad_w = jnp.dot(attn_all.T, grad_keys, preferred_element_type=jnp.float32)
    value_grad_w = jnp.dot(attn_all.T, grad_values, preferred_element_type=jnp.float32)
    text_key_grad_w = jnp.dot(text_flat.T, grad_text_keys, preferred_element_type=jnp.float32)
    text_value_grad_w = jnp.dot(text_flat.T, grad_text_values, preferred_element_type=jnp.float32)
    grad_attn_rows = lax.psum_scatter(
        jnp.dot(grad_queries, w_query.T, preferred_element_type=jnp.float32)
        + jnp.dot(grad_keys, w_key.T, preferred_element_type=jnp.float32)
        + jnp.dot(grad_values, w_value.T, preferred_element_type=jnp.float32),
        "tensor",
        scatter_dimension=0,
        tiled=True,
    )
    attn_gain_part = jnp.sum(grad_attn_rows * normed_first * (1.0 + scale_attn), axis=0)
    grad_scale_attn = grad_attn_rows * normed_first * attn_gain
    input_grad = grad_middle + rms_backward(
        grad_attn_rows * attn_gain * (1.0 + scale_attn), normed_first, inv_first
    )
    token_mod_grad = jnp.concatenate(
        [grad_scale_attn, grad_gate_attn, grad_scale_ffn, grad_gate_ffn], axis=1
    )
    clip_mod_grad = jnp.dot(my_table.T, token_mod_grad, precision=highest_precision)
    mod_grad_part = lax.psum_scatter(clip_mod_grad, "tensor", scatter_dimension=1, tiled=True)
    ada_grad_w = jnp.dot(
        condition.T, mod_grad_part.astype(jnp.bfloat16), preferred_element_type=jnp.float32
    )
    gate_full = lax.dynamic_update_slice_in_dim(
        jnp.zeros((cross_gate.shape[0],), jnp.float32), grad_cross, my_rank * local_heads, 0
    )
    attn_gain_grad, ffn_gain_grad, query_gain_grad, key_gain_grad, cross_gate_grad = lax.psum(
        (attn_gain_part, ffn_gain_part, query_gain_part, key_gain_part, gate_full), ("dp", "tensor")
    )
    (
        query_sum,
        key_sum,
        value_sum,
        text_key_sum,
        text_value_sum,
        ada_sum,
        out_sum,
        gate_sum,
        up_sum,
        down_sum,
    ) = (
        lax.psum_scatter(query_grad_w, "dp", scatter_dimension=0, tiled=True),
        lax.psum_scatter(key_grad_w, "dp", scatter_dimension=0, tiled=True),
        lax.psum_scatter(value_grad_w, "dp", scatter_dimension=0, tiled=True),
        lax.psum_scatter(text_key_grad_w, "dp", scatter_dimension=0, tiled=True),
        lax.psum_scatter(text_value_grad_w, "dp", scatter_dimension=0, tiled=True),
        lax.psum_scatter(ada_grad_w, "dp", scatter_dimension=0, tiled=True),
        lax.psum_scatter(out_grad_t, "dp", scatter_dimension=0, tiled=True),
        lax.psum_scatter(gate_grad_w, "dp", scatter_dimension=0, tiled=True),
        lax.psum_scatter(up_grad_w, "dp", scatter_dimension=0, tiled=True),
        lax.psum_scatter(down_grad_t, "dp", scatter_dimension=0, tiled=True),
    )
    return (
        block_out,
        input_grad,
        attn_gain_grad,
        ffn_gain_grad,
        query_gain_grad,
        key_gain_grad,
        cross_gate_grad,
        query_sum,
        key_sum,
        value_sum,
        out_sum.T,
        text_key_sum,
        text_value_sum,
        ada_sum,
        gate_sum,
        up_sum,
        down_sum.T,
    )


def solution(mesh):
    return jax.shard_map(
        on_device,
        mesh=mesh,
        in_specs=(
            P(("dp", "tensor"), None),
            P("dp"),
            P("dp"),
            P("dp"),
            P("dp", None, None),
            P("dp"),
            P(("dp", "tensor"), None),
            P(),
            P(),
            P(),
            P(),
            P(),
            P(None, "tensor"),
            P(None, "tensor"),
            P(None, "tensor"),
            P("tensor", None),
            P(None, "tensor"),
            P(None, "tensor"),
            P(None, "tensor"),
            P(None, "tensor"),
            P(None, "tensor"),
            P("tensor", None),
        ),
        out_specs=(
            P(("dp", "tensor"), None),
            P(("dp", "tensor"), None),
            P(),
            P(),
            P(),
            P(),
            P(),
            P("dp", "tensor"),
            P("dp", "tensor"),
            P("dp", "tensor"),
            P("tensor", "dp"),
            P("dp", "tensor"),
            P("dp", "tensor"),
            P("dp", "tensor"),
            P("dp", "tensor"),
            P("dp", "tensor"),
            P("tensor", "dp"),
        ),
        check_vma=False,
    )
```

profile of v0, /device:TPU:0, one launch (start us, length us, event | category | flops | bytes accessed | tf_op | source)
XLA Modules:
  0.0 1585.0 jit_solution(5213669864479055442)
XLA Ops:
  12.1 15.0 all_gather.15
  47.9 51.2 %all-gather.5.cloned.1.call-done = bf16[1024,1536]{1,0:T(8,128)(2,1)} async-done(((bf16[256,1536]{1,0:T(8,128)(2,1)}), bf16[1024,1536]{1,0:T(8,128)(2,1)}) %all-gather.5.cloned.1.call-update) | async-done | bytes 3145744 | tf_op jit(solution)/shard_map/all_gather | solution.py:126
  111.4 47.8 %while.36 = (s32[]{:T(128)}, bf16[2,512,384]{2,1,0:T(8,128)(2,1)}, f32[2,6,512]{2,1,0:T(8,128)}, f32[2,6,512]{2,1,0:T(8,128)S(1)}, s32[2]{0:T(128)S(1)}, /*index...) while((s32[]{:T(128)}, bf16[2,512,384]{2,1,0:T(8,128)(2,1)}, ...), condition=%wide.region_9.10_spmd.clone, body=%wide.region_4.9_spmd.clone.sunk | while | flops 1160702336 | bytes 72130664 | solution.py:185
  165.7 109.1 %reduce-scatter.18.cloned.1.call-done = f32[256,1536]{1,0:T(8,128)} async-done(((f32[1024,1536]{1,0:T(8,128)}), f32[256,1536]{1,0:T(8,128)}) %reduce-scatter.18.cloned.1.call-update) | async-done | bytes 1572880 | tf_op jit(solution)/shard_map/reduce_scatter | solution.py:187
  282.3 63.5 %all-gather.7.cloned.1.call-done = bf16[1024,1536]{1,0:T(8,128)(2,1)} async-done(((bf16[256,1536]{1,0:T(8,128)(2,1)}), bf16[1024,1536]{1,0:T(8,128)(2,1)}) %all-gather.7.cloned.1.call-update) | async-done | bytes 3145744 | tf_op jit(solution)/shard_map/all_gather | solution.py:197
  359.2 50.8 %all-gather.9.cloned.1.call-done = bf16[1024,1536]{1,0:T(8,128)(2,1)} async-done(((bf16[256,1536]{1,0:T(8,128)(2,1)}), bf16[1024,1536]{1,0:T(8,128)(2,1)}) %all-gather.9.cloned.1.call-update) | async-done | bytes 3145744 | tf_op jit(solution)/shard_map/all_gather | solution.py:213
  438.7 101.6 %reduce-scatter.22.cloned.1.call-done = f32[256,1536]{1,0:T(8,128)} async-done(((f32[1024,1536]{1,0:T(8,128)}), f32[256,1536]{1,0:T(8,128)}) %reduce-scatter.22.cloned.1.call-update) | async-done | bytes 1572880 | tf_op jit(solution)/shard_map/reduce_scatter | solution.py:222
  543.9 59.4 %reduce-scatter.20.cloned.1.call-done = bf16[256,1536]{1,0:T(8,128)(2,1)} async-done(((bf16[1024,1536]{1,0:T(8,128)(2,1)}), bf16[256,1536]{1,0:T(8,128)(2,1)}) %reduce-scatter.20.cloned.1.call-update) | async-done | bytes 786448 | tf_op jit(solution)/shard_map/reduce_scatter | solution.py:203
  615.1 62.2 %all-gather.11.cloned.1.call-done = bf16[1024,1536]{1,0:T(8,128)(2,1)} async-done(((bf16[256,1536]{1,0:T(8,128)(2,1)}), bf16[1024,1536]{1,0:T(8,128)(2,1)}) %all-gather.11.cloned.1.call-update) | async-done | bytes 3145744 | tf_op jit(solution)/shard_map/all_gather | solution.py:236
  682.2 114.7 %while.37 = (s32[]{:T(128)}, f32[1024,6,64]{0,2,1:T(8,128)}, f32[1024,6,64]{0,2,1:T(8,128)}, f32[384,6,64]{0,2,1:T(8,128)}, f32[384,6,64]{0,2,1:T(8,128)}, /*ind...) while((s32[]{:T(128)}, f32[1024,6,64]{0,2,1:T(8,128)}, ...), condition=%wide.region_19.20_spmd.clone, body=%wide.region_15.19_spmd.clone.sunk | while | flops 2994022912 | bytes 212489872 | solution.py:309
  723.9 15.0 dynamic_update_slice.31
  781.4 15.0 dynamic_update_slice.31
  817.7 108.4 %reduce-scatter.24.cloned.1.call-done = f32[256,1536]{1,0:T(8,128)} async-done(((f32[1024,1536]{1,0:T(8,128)}), f32[256,1536]{1,0:T(8,128)}) %reduce-scatter.24.cloned.1.call-update) | async-done | bytes 1572880 | tf_op jit(solution)/shard_map/reduce_scatter | solution.py:341
  1003.9 58.9 %reduce-scatter.36.cloned.1.call-done = f32[512,384]{0,1:T(8,128)} async-done(((f32[4096,384]{0,1:T(8,128)}), f32[512,384]{0,1:T(8,128)}) %reduce-scatter.36.cloned.1.call-update) | async-done | bytes 786448 | tf_op jit(solution)/shard_map/reduce_scatter | solution.py:384
  1065.1 63.2 %reduce-scatter.34.cloned.1.call-done = f32[512,384]{0,1:T(8,128)} async-done(((f32[4096,384]{0,1:T(8,128)}), f32[512,384]{0,1:T(8,128)}) %reduce-scatter.34.cloned.1.call-update) | async-done | bytes 786448 | tf_op jit(solution)/shard_map/reduce_scatter | solution.py:383
  1130.6 39.9 %all-reduce = (f32[1536]{0:T(1024)}, f32[1536]{0:T(1024)}, f32[64]{0:T(128)}, f32[64]{0:T(128)}, f32[24]{0:T(128)}) all-reduce(f32[1536]{0:T(1024)S(1)} %get-tuple-element.380, f32[1536]{0:T(1024)S(1)} %copy-done.59, f32[64]{0:T(128)S(1)} %reduce_sum.207, f32[64]{0:T(128)S(1)} %add.233, ...), channel_id=1, replica_groups=mesh['dp'=8,'tensor'=4] {'dp','tensor'}, use_global_device_ids=true, to_apply=%region_25.26 | all-reduce | flops 3224 | bytes 25792 | tf_op jit(solution)/shard_map/psum | solution.py:365
  1174.7 19.8 %reduce-scatter.44.cloned.1.call-done = f32[192,1024]{1,0:T(8,128)} async-done(((f32[1536,1024]{1,0:T(8,128)}), f32[192,1024]{1,0:T(8,128)}) %reduce-scatter.44.cloned.1.call-update) | async-done | bytes 786448 | tf_op jit(solution)/shard_map/reduce_scatter | solution.py:389
  1194.5 66.1 %reduce-scatter.42.cloned.1.call-done = f32[192,1024]{1,0:T(8,128)} async-done(((f32[1536,1024]{1,0:T(8,128)}), f32[192,1024]{1,0:T(8,128)}) %reduce-scatter.42.cloned.1.call-update) | async-done | bytes 786448 | tf_op jit(solution)/shard_map/reduce_scatter | solution.py:388
  1260.6 65.6 %reduce-scatter.40.cloned.1.call-done = f32[192,1024]{1,0:T(8,128)} async-done(((f32[1536,1024]{1,0:T(8,128)}), f32[192,1024]{1,0:T(8,128)}) %reduce-scatter.40.cloned.1.call-update) | async-done | bytes 786448 | tf_op jit(solution)/shard_map/reduce_scatter | solution.py:387
  1326.2 46.6 %reduce-scatter.32.cloned.1.call-done = f32[192,384]{1,0:T(8,128)} async-done(((f32[1536,384]{1,0:T(8,128)}), f32[192,384]{1,0:T(8,128)}) %reduce-scatter.32.cloned.1.call-update) | async-done | bytes 294928 | tf_op jit(solution)/shard_map/reduce_scatter | solution.py:386
  1372.8 46.3 %reduce-scatter.26.cloned.1.call-done = f32[192,384]{1,0:T(8,128)} async-done(((f32[1536,384]{1,0:T(8,128)}), f32[192,384]{1,0:T(8,128)}) %reduce-scatter.26.cloned.1.call-update) | async-done | bytes 294928 | tf_op jit(solution)/shard_map/reduce_scatter | solution.py:380
  1419.1 46.7 %reduce-scatter.28.cloned.1.call-done = f32[192,384]{1,0:T(8,128)} async-done(((f32[1536,384]{1,0:T(8,128)}), f32[192,384]{1,0:T(8,128)}) %reduce-scatter.28.cloned.1.call-update) | async-done | bytes 294928 | tf_op jit(solution)/shard_map/reduce_scatter | solution.py:381
  1465.8 46.3 %reduce-scatter.30.cloned.1.call-done = f32[192,384]{1,0:T(8,128)} async-done(((f32[1536,384]{1,0:T(8,128)}), f32[192,384]{1,0:T(8,128)}) %reduce-scatter.30.cloned.1.call-update) | async-done | bytes 294928 | tf_op jit(solution)/shard_map/reduce_scatter | solution.py:382
  1512.1 66.1 %reduce-scatter.38.cloned.1.call-done = f32[128,1536]{1,0:T(8,128)} async-done(((f32[1024,1536]{1,0:T(8,128)}), f32[128,1536]{1,0:T(8,128)}) %reduce-scatter.38.cloned.1.call-update) | async-done | bytes 786448 | tf_op jit(solution)/shard_map/reduce_scatter | solution.py:385
  (423 shorter events, 343.8 us)
Async XLA Ops:
  7.2 91.9 %all-gather.5.cloned.1.call-start = ((), (), s32[]{:S(2)}) async-start(), calls=%async_computation.15 | async-start | bytes 3932160 | tf_op jit(solution)/shard_map/all_gather | solution.py:126
  34.4 240.4 %reduce-scatter.18.cloned.1.call-start = ((), (), s32[]{:S(2)}) async-start(), calls=%async_computation.16 | async-start | bytes 7864320 | tf_op jit(solution)/shard_map/reduce_scatter | solution.py:187
  165.3 112.1 %copy-start.52 = (f32[1536]{0:T(1024)S(1)}, f32[1536]{0:T(1024)}, u32[]{:S(2)}) copy-start(f32[1536]{0:T(1024)} %param.34) | copy-start | bytes 18436
  165.3 180.6 %all-gather.7.cloned.1.call-start = ((), (), s32[]{:S(2)}) async-start(), calls=%async_computation.17 | async-start | bytes 3932160 | tf_op jit(solution)/shard_map/all_gather | solution.py:197
  281.7 128.4 %all-gather.9.cloned.1.call-start = ((), (), s32[]{:S(2)}) async-start(), calls=%async_computation.19 | async-start | bytes 3932160 | tf_op jit(solution)/shard_map/all_gather | solution.py:213
  282.2 258.1 %reduce-scatter.22.cloned.1.call-start = ((), (), s32[]{:S(2)}) async-start(), calls=%async_computation.20 | async-start | bytes 7864320 | tf_op jit(solution)/shard_map/reduce_scatter | solution.py:222
  430.7 172.5 %reduce-scatter.20.cloned.1.call-start = ((), (), s32[]{:S(2)}) async-start(), calls=%async_computation.18 | async-start | bytes 3932160 | tf_op jit(solution)/shard_map/reduce_scatter | solution.py:203
  438.6 238.7 %all-gather.11.cloned.1.call-start = ((), (), s32[]{:S(2)}) async-start(), calls=%async_computation.21 | async-start | bytes 3932160 | tf_op jit(solution)/shard_map/all_gather | solution.py:236
  613.6 312.5 %reduce-scatter.24.cloned.1.call-start = ((), (), s32[]{:S(2)}) async-start(), calls=%async_computation.22 | async-start | bytes 7864320 | tf_op jit(solution)/shard_map/reduce_scatter | solution.py:341
  816.5 109.6 %copy-start.54 = (f32[1536]{0:T(1024)S(1)}, f32[1536]{0:T(1024)}, u32[]{:S(2)}) copy-start(f32[1536]{0:T(1024)} %param.33) | copy-start | bytes 18436
  816.5 109.6 %copy-start.65 = (f32[256]{0:T(256)S(1)}, f32[256]{0:T(256)}, u32[]{:S(2)}) copy-start(f32[256]{0:T(256)} %copy-done.64) | copy-start | bytes 3076
  816.6 181.8 %reduce-scatter.46.cloned.1.call-start = ((), (), s32[]{:S(2)}) async-start(), calls=%async_computation.33 | async-start | bytes 3932160
  817.7 111.4 %copy-start.73 = (s32[256]{0:T(256)S(1)}, s32[256]{0:T(256)}, u32[]{:S(2)}) copy-start(s32[256]{0:T(256)} %copy-done.72) | copy-start | bytes 3076
  936.8 126.0 %reduce-scatter.36.cloned.1.call-start = ((), (), s32[]{:S(2)}) async-start(), calls=%async_computation.28 | async-start | bytes 7077888 | tf_op jit(solution)/shard_map/reduce_scatter | solution.py:384
  941.3 187.0 %reduce-scatter.34.cloned.1.call-start = ((), (), s32[]{:S(2)}) async-start(), calls=%async_computation.27 | async-start | bytes 7077888 | tf_op jit(solution)/shard_map/reduce_scatter | solution.py:383
  949.5 245.0 %reduce-scatter.44.cloned.1.call-start = ((), (), s32[]{:S(2)}) async-start(), calls=%async_computation.32 | async-start | bytes 7077888 | tf_op jit(solution)/shard_map/reduce_scatter | solution.py:389
  958.4 302.2 %reduce-scatter.42.cloned.1.call-start = ((), (), s32[]{:S(2)}) async-start(), calls=%async_computation.31 | async-start | bytes 7077888 | tf_op jit(solution)/shard_map/reduce_scatter | solution.py:388
  967.4 358.8 %reduce-scatter.40.cloned.1.call-start = ((), (), s32[]{:S(2)}) async-start(), calls=%async_computation.30 | async-start | bytes 7077888 | tf_op jit(solution)/shard_map/reduce_scatter | solution.py:387
  976.3 396.6 %reduce-scatter.32.cloned.1.call-start = ((), (), s32[]{:S(2)}) async-start(), calls=%async_computation.26 | async-start | bytes 2654208 | tf_op jit(solution)/shard_map/reduce_scatter | solution.py:386
  981.6 437.5 %reduce-scatter.26.cloned.1.call-start = ((), (), s32[]{:S(2)}) async-start(), calls=%async_computation.23 | async-start | bytes 2654208 | tf_op jit(solution)/shard_map/reduce_scatter | solution.py:380
  987.1 478.7 %reduce-scatter.28.cloned.1.call-start = ((), (), s32[]{:S(2)}) async-start(), calls=%async_computation.24 | async-start | bytes 2654208 | tf_op jit(solution)/shard_map/reduce_scatter | solution.py:381
  992.6 519.5 %reduce-scatter.30.cloned.1.call-start = ((), (), s32[]{:S(2)}) async-start(), calls=%async_computation.25 | async-start | bytes 2654208 | tf_op jit(solution)/shard_map/reduce_scatter | solution.py:382
  998.2 580.0 %reduce-scatter.38.cloned.1.call-start = ((), (), s32[]{:S(2)}) async-start(), calls=%async_computation.29 | async-start | bytes 7077888 | tf_op jit(solution)/shard_map/reduce_scatter | solution.py:385
  1003.4 127.2 %copy-start.59 = (f32[1536]{0:T(1024)S(1)}, f32[1536]{0:T(1024)}, u32[]{:S(2)}) copy-start(f32[1536]{0:T(1024)} %get-tuple-element.378) | copy-start | bytes 18436
  (101 other events, 586.1 us)
Sparse Core Ops, SparseCore 0:
  34.5 64.5 all-gather.4
  165.4 109.3 reduce-scatter.17
  281.8 64.0 all-gather.6
  347.8 62.1 all-gather.8
  430.9 109.3 reduce-scatter.21
  542.5 60.7 reduce-scatter.19
  613.8 63.5 all-gather.10
  816.7 109.3 reduce-scatter.23
  936.9 60.7 reduce-scatter.45
  1000.9 61.8 reduce-scatter.35
  1066.5 61.7 reduce-scatter.33
  1132.1 62.3 reduce-scatter.43
  1198.8 61.7 reduce-scatter.41
  1264.4 61.7 reduce-scatter.39
  1330.3 42.4 reduce-scatter.31
  1376.6 42.4 reduce-scatter.25
  1423.3 42.4 reduce-scatter.27
  1469.6 42.4 reduce-scatter.29
  1516.4 61.7 reduce-scatter.37
where the time goes:
time: 1590 us
  waiting for transfers between devices  1130 us (71%)
  matrix products  223 us (14%)
  other arithmetic  75.4 us (5%)
  local copies, waits for them, and re-layouts  72.1 us (5%)
  blocking collectives  54.9 us (3%)
    reduce_scatter x1, waiting for transfers between devices, on_device(): lax.psum_scatter(jnp.dot(mixed_heads, w_out, preferred_element_type=jnp.f...  109 us
    reduce_scatter x1, waiting for transfers between devices, on_device(): lax.psum_scatter(jnp.dot(grad_queries, w_query.T, preferred_element_type=...  108 us
    reduce_scatter x1, waiting for transfers between devices, on_device(): lax.psum_scatter(jnp.dot(grad_gate_low, w_gate.T, preferred_element_type=...  102 us
    reduce_scatter x1, waiting for transfers between devices, on_device(): lax.psum_scatter(ada_grad_w, 'dp', scatter_dimension=0, tiled=True)  66.1 us
    reduce_scatter x1, waiting for transfers between devices, on_device(): lax.psum_scatter(up_grad_w, 'dp', scatter_dimension=0, tiled=True)  66.1 us
    reduce_scatter x1, waiting for transfers between devices, on_device(): lax.psum_scatter(gate_grad_w, 'dp', scatter_dimension=0, tiled=True)  65.6 us
    all_gather x1, waiting for transfers between devices, on_device(): ffn_all = lax.all_gather(ffn_rows, 'tensor', axis=0, tiled=True)  63.5 us
    reduce_scatter x1, waiting for transfers between devices, on_device(): lax.psum_scatter(text_key_grad_w, 'dp', scatter_dimension=0, tiled=True)  63.2 us
  transfers between devices with their start and end apart: 19, of which 18 were waited for; matrix products, arithmetic and copies ran while one was open for 7% of the time, Pallas kernels for 0%

commit v1 on v0

v1 whole, which is shorter than its diff:
```python
import functools
import math

import jax
import jax.numpy as jnp
from jax import lax
from jax.experimental import pallas as pl
from jax.experimental.pallas import tpu as pltpu
from jax.sharding import PartitionSpec as P

epsilon = 1e-06
edge_rows = 256
apart = 2048.0


def rms_scale(values):
    return lax.rsqrt(jnp.mean(values * values, axis=-1, keepdims=True) + epsilon)


def rms_backward(grad_hat, normed, scaling):
    return scaling * (grad_hat - normed * jnp.mean(grad_hat * normed, axis=-1, keepdims=True))


def time_embed(time_steps, embed_width):
    half_width = embed_width // 2
    frequency = jnp.exp(-math.log(10000.0) * jnp.arange(half_width, dtype=jnp.float32) / half_width)
    angles = time_steps.astype(jnp.float32)[:, None] * frequency[None, :]
    return jnp.concatenate([jnp.cos(angles), jnp.sin(angles)], axis=-1)


def clip_table(clip_rows, clip_count):
    return (clip_rows[:, None] == jnp.arange(clip_count, dtype=jnp.int32)[None, :]).astype(
        jnp.float32
    )


def exchange(values, axis_name, distance):
    count = lax.axis_size(axis_name)
    return lax.ppermute(values, axis_name, [(i, i ^ distance) for i in range(count)])


def butterfly_sum(values):
    for axis_name in ("tensor", "dp"):
        count = lax.axis_size(axis_name)
        distance = 1
        while distance < count:
            values = values + exchange(values, axis_name, distance)
            distance *= 2
    return values


def halve(blocks, bit, axis_at):
    mine = (lax.axis_index("dp") >> bit) & 1
    given = lax.dynamic_index_in_dim(blocks, 1 - mine, axis_at, keepdims=False)
    kept = lax.dynamic_index_in_dim(blocks, mine, axis_at, keepdims=False)
    taken = exchange(given, "dp", 1 << bit)
    return kept.astype(jnp.float32) + taken.astype(jnp.float32)


def scatter_groups(partial_sum):
    count = lax.axis_size("dp")
    bits = count.bit_length() - 1
    rows, columns = partial_sum.shape
    blocks = partial_sum.reshape((2,) * bits + (rows // count, columns))
    blocks = halve(blocks, 0, bits - 1).astype(jnp.bfloat16)
    middle_col = columns // 2
    results = []
    for order, low_col in ((range(1, bits), 0), (range(bits - 1, 0, -1), middle_col)):
        part = blocks[..., low_col : low_col + middle_col]
        left = list(range(bits - 1, 0, -1))
        for step, bit in enumerate(order):
            part = halve(part, bit, left.index(bit))
            left.remove(bit)
            if step < bits - 2:
                part = part.astype(jnp.bfloat16)
        results.append(part)
    return jnp.concatenate(results, axis=-1)


def spread_groups(rows):
    count = lax.axis_size("dp")
    distance = 1
    rows = rows[None]
    while distance < count:
        other = exchange(rows, "dp", distance)
        mine = (lax.axis_index("dp") // distance) % 2
        first = jnp.where(mine == 0, rows, other)
        second = jnp.where(mine == 0, other, rows)
        rows = jnp.concatenate([first, second], axis=0)
        distance *= 2
    return rows


def scatter_rows(values):
    return lax.psum_scatter(
        values.astype(jnp.bfloat16), "tensor", scatter_dimension=0, tiled=True
    ).astype(jnp.float32)


def product(left, right, contract=((1,), (0,))):
    return lax.dot_general(left, right, (contract, ((), ())), preferred_element_type=jnp.float32)


def head_norm(raw):
    return lax.rsqrt(jnp.mean(raw * raw, axis=0, keepdims=True) + epsilon)


def turn(values, cosine, sine):
    half = values.shape[0] // 2
    lead, tail = values[:half], values[half:]
    return jnp.concatenate([lead * cosine - tail * sine, lead * sine + tail * cosine], axis=0)


def turn_back(values, cosine, sine):
    half = values.shape[0] // 2
    lead, tail = values[:half], values[half:]
    return jnp.concatenate([lead * cosine + tail * sine, tail * cosine - lead * sine], axis=0)


def widen(values, extra):
    rows = values.shape[0] + extra.shape[0]
    pad = jnp.zeros((128 - rows, values.shape[1]), values.dtype)
    return jnp.concatenate([values, extra.astype(values.dtype), pad], axis=0)


def text_range(block, blocks, clips, slots):
    first = 0 if block == 0 else slots
    last = (clips if block == blocks - 1 else clips - 1) * slots
    return first, last


def attend_forward(
    clips, slots, gates, query, key, value, text_key, text_value, table, text_table, cosine, sine,
    query_gain, key_gain, mixed, self_out, cross_out, self_inverse, cross_inverse,
):
    head_dim, rows = query.shape
    scale = math.log2(math.e) / math.sqrt(head_dim)
    gate = gates[pl.program_id(0)]
    raw = query[...]
    query_rot = turn(raw * head_norm(raw) * query_gain[...], cosine[...], sine[...])
    query_wide = widen(query_rot, table[0]).astype(jnp.bfloat16)
    raw = key[...]
    key_rot = turn(raw * head_norm(raw) * key_gain[...], cosine[...], sine[...])
    key_wide = widen(key_rot, table[1]).T.astype(jnp.bfloat16)
    raw = text_key[...]
    text_wide = widen(raw * head_norm(raw) * key_gain[...], text_table[...]).T.astype(jnp.bfloat16)
    ones_row = (lax.broadcasted_iota(jnp.int32, (16, rows), 0) == 0).astype(jnp.float32)
    value_wide = jnp.concatenate([value[...], ones_row], axis=0).astype(jnp.bfloat16)
    text_value_wide = jnp.concatenate(
        [text_value[...], ones_row[:, : text_value.shape[1]]], axis=0
    ).astype(jnp.bfloat16)
    blocks = rows // edge_rows
    for block in range(blocks):
        cols = slice(block * edge_rows, (block + 1) * edge_rows)
        query_blk = query_wide[:, cols]
        weights = jnp.exp2(product(key_wide, query_blk) * scale).astype(jnp.bfloat16)
        total = product(value_wide, weights)
        inverse = 1.0 / total[head_dim : head_dim + 1]
        own = total[:head_dim] * inverse
        first, last = text_range(block, blocks, clips, slots)
        weights = jnp.exp2(product(text_wide[first:last], query_blk) * scale).astype(jnp.bfloat16)
        total = product(text_value_wide[:, first:last], weights)
        text_inverse = 1.0 / total[head_dim : head_dim + 1]
        other = total[:head_dim] * text_inverse
        mixed[:, cols] = (own + gate * other).astype(jnp.bfloat16)
        self_out[:, cols] = own
        cross_out[:, cols] = other
        self_inverse[0, :, cols] = inverse
        cross_inverse[0, :, cols] = text_inverse


def attend_backward(
    clips, slots, gates, query, key, value, text_key, text_value, table, text_table, cosine, sine,
    query_gain, key_gain, grad, self_out, cross_out, self_inverse, cross_inverse,
    grad_qkv, grad_text, gain_sums, grad_key_sum, grad_value_sum, grad_query_all, text_key_sum, text_value_sum,
):
    head_dim, rows = query.shape
    scale = math.log2(math.e) / math.sqrt(head_dim)
    factor = 1.0 / math.sqrt(head_dim)
    gate = gates[pl.program_id(0)]
    raw = query[...]
    query_inv = head_norm(raw)
    query_rot = turn(raw * query_inv * query_gain[...], cosine[...], sine[...])
    query_wide = widen(query_rot, table[0]).astype(jnp.bfloat16)
    raw = key[...]
    key_inv = head_norm(raw)
    key_rot = turn(raw * key_inv * key_gain[...], cosine[...], sine[...])
    key_low = key_rot.astype(jnp.bfloat16)
    key_wide = widen(key_rot, table[1]).T.astype(jnp.bfloat16)
    raw = text_key[...]
    text_inv = head_norm(raw)
    text_norm = raw * text_inv * key_gain[...]
    text_low = text_norm.astype(jnp.bfloat16)
    text_wide = widen(text_norm, text_table[...]).T.astype(jnp.bfloat16)
    two_rows = (lax.broadcasted_iota(jnp.int32, (16, rows), 0) < 2).astype(jnp.float32)
    value_wide = widen(value[...], two_rows).T.astype(jnp.bfloat16)
    text_value_wide = widen(text_value[...], two_rows[:, : text_value.shape[1]]).T.astype(jnp.bfloat16)

    grads = grad[...].astype(jnp.float32)

    def with_dots(weighted, out):
        low = weighted.astype(jnp.bfloat16)
        dots = jnp.sum(low.astype(jnp.float32) * out, axis=0, keepdims=True)
        high = dots.astype(jnp.bfloat16).astype(jnp.float32)
        rows_at = lax.broadcasted_iota(jnp.int32, (16, rows), 0)
        extra = jnp.where(rows_at == 0, -high, jnp.where(rows_at == 1, high - dots, 0.0))
        return widen(low.astype(jnp.float32), extra).astype(jnp.bfloat16)

    self_wide = with_dots(grads * self_inverse[0], self_out[...])
    cross_wide = with_dots(grads * (gate * cross_inverse[0]), cross_out[...])
    blocks = rows // edge_rows
    text_key_sum[...] = jnp.zeros_like(text_key_sum)
    text_value_sum[...] = jnp.zeros_like(text_value_sum)
    for block in range(blocks):
        cols = slice(block * edge_rows, (block + 1) * edge_rows)
        query_blk = query_wide[:, cols]
        grad_blk = self_wide[:, cols]
        weights = jnp.exp2(product(key_wide, query_blk) * scale)
        slopes = (weights * product(value_wide, grad_blk)).astype(jnp.bfloat16)
        value_term = product(grad_blk[:head_dim], weights.astype(jnp.bfloat16), ((1,), (1,)))
        key_term = product(query_blk[:head_dim], slopes, ((1,), (1,)))
        if block == 0:
            grad_value_sum[...] = value_term
            grad_key_sum[...] = key_term
        else:
            grad_value_sum[...] += value_term
            grad_key_sum[...] += key_term
        query_term = product(key_low, slopes)
        first, last = text_range(block, blocks, clips, slots)
        grad_blk = cross_wide[:, cols]
        weights = jnp.exp2(product(text_wide[first:last], query_blk) * scale)
        slopes = (weights * product(text_value_wide[first:last], grad_blk)).astype(jnp.bfloat16)
        text_value_sum[:, first:last] += product(
            grad_blk[:head_dim], weights.astype(jnp.bfloat16), ((1,), (1,))
        )
        text_key_sum[:, first:last] += product(query_blk[:head_dim], slopes, ((1,), (1,)))
        grad_query_all[:, cols] = query_term + product(text_low[:, first:last], slopes)

    def through_norm(incoming, raw, inverse, gain):
        normed = raw * inverse
        scaled = incoming * gain
        mean = jnp.mean(scaled * normed, axis=0, keepdims=True)
        gain_part = jnp.sum(incoming * normed, axis=1, keepdims=True)
        return inverse * (scaled - normed * mean), gain_part

    incoming = turn_back(grad_query_all[...] * factor, cosine[...], sine[...])
    result, query_part = through_norm(incoming, query[...], query_inv, query_gain[...])
    grad_qkv[0] = result.astype(jnp.bfloat16)
    incoming = turn_back(grad_key_sum[...] * factor, cosine[...], sine[...])
    result, key_part = through_norm(incoming, key[...], key_inv, key_gain[...])
    grad_qkv[1] = result.astype(jnp.bfloat16)
    grad_qkv[2] = grad_value_sum[...].astype(jnp.bfloat16)
    result, text_part = through_norm(
        text_key_sum[...] * factor, text_key[...], text_inv, key_gain[...]
    )
    grad_text[0] = result.astype(jnp.bfloat16)
    grad_text[1] = text_value_sum[...].astype(jnp.bfloat16)
    gate_part = jnp.sum(grads * cross_out[...], axis=1, keepdims=True)
    lane = lax.broadcasted_iota(jnp.int32, (head_dim, 128), 1)
    gain_sums[0] = jnp.where(
        lane == 0, query_part, jnp.where(lane == 1, key_part + text_part, gate_part)
    )


def attention_specs(heads, head_dim, rows, text_rows):
    def head_block(part, width):
        return pl.BlockSpec((head_dim, width), lambda h, part=part: (part * heads + h, 0))
    def whole(shape):
        return pl.BlockSpec(shape, lambda h: (0,) * len(shape))
    return [
        pl.BlockSpec(memory_space=pltpu.SMEM),
        head_block(0, rows), head_block(1, rows), head_block(2, rows),
        head_block(0, text_rows), head_block(1, text_rows),
        whole((2, 16, rows)), whole((16, text_rows)),
        whole((head_dim // 2, rows)), whole((head_dim // 2, rows)),
        whole((head_dim, 1)), whole((head_dim, 1)),
    ]


def attention_forward(shared, heads, head_dim, clips):
    qkv, text = shared[1], shared[4]
    rows = qkv.shape[1]; text_rows = text.shape[1]
    cols = heads * head_dim
    out = lambda dt: jax.ShapeDtypeStruct((cols, rows), dt)
    hb = pl.BlockSpec((head_dim, rows), lambda h: (h, 0))
    stat = pl.BlockSpec((1, 1, rows), lambda h: (h, 0, 0))
    return pl.pallas_call(
        functools.partial(attend_forward, clips, text_rows // clips),
        grid=(heads,),
        in_specs=attention_specs(heads, head_dim, rows, text_rows),
        out_specs=[hb, hb, hb, stat, stat],
        out_shape=[out(jnp.bfloat16), out(jnp.float32), out(jnp.float32)]
        + [jax.ShapeDtypeStruct((heads, 1, rows), jnp.float32)] * 2,
        compiler_params=pltpu.CompilerParams(vmem_limit_bytes=48 << 20),
        cost_estimate=pl.CostEstimate(flops=4*cols*rows*rows*2, bytes_accessed=cols*rows*24, transcendentals=heads*rows*rows),
    )(*shared)


def attention_backward(shared, grad, kept, heads, head_dim, clips):
    qkv, text = shared[1], shared[4]
    rows = qkv.shape[1]; text_rows = text.shape[1]
    cols = heads * head_dim
    hb = pl.BlockSpec((head_dim, rows), lambda h: (h, 0))
    stat = pl.BlockSpec((1, 1, rows), lambda h: (h, 0, 0))
    return pl.pallas_call(
        functools.partial(attend_backward, clips, text_rows // clips),
        grid=(heads,),
        in_specs=attention_specs(heads, head_dim, rows, text_rows) + [hb, hb, hb, stat, stat],
        out_specs=[
            pl.BlockSpec((3, head_dim, rows), lambda h: (0, h, 0)),
            pl.BlockSpec((2, head_dim, text_rows), lambda h: (0, h, 0)),
            pl.BlockSpec((1, head_dim, 128), lambda h: (h, 0, 0)),
        ],
        out_shape=[
            jax.ShapeDtypeStruct((3, cols, rows), jnp.bfloat16),
            jax.ShapeDtypeStruct((2, cols, text_rows), jnp.bfloat16),
            jax.ShapeDtypeStruct((heads, head_dim, 128), jnp.float32),
        ],
        scratch_shapes=[pltpu.VMEM((head_dim, rows), jnp.float32)] * 3
        + [pltpu.VMEM((head_dim, text_rows), jnp.float32)] * 2,
        compiler_params=pltpu.CompilerParams(vmem_limit_bytes=48 << 20),
        cost_estimate=pl.CostEstimate(flops=10*cols*rows*rows*2, bytes_accessed=cols*rows*30, transcendentals=heads*rows*rows),
    )(*shared, grad, *kept)


def clip_tables(clip_ids, text_lengths, clips, slots):
    rows = clip_ids.shape[0]
    feature = jnp.arange(16, dtype=jnp.int32)[:, None]
    member = feature == clip_ids[None, :]
    query_part = jnp.where(feature < clips, jnp.where(member, 0.0, -apart), jnp.where(feature == clips, -apart, 0.0))
    key_part = member.astype(jnp.float32)
    owner = jnp.repeat(jnp.arange(clips, dtype=jnp.int32), slots)
    slot = jnp.tile(jnp.arange(slots, dtype=jnp.int32), clips)
    dead = slot >= jnp.repeat(text_lengths, slots)
    text_part = jnp.where(feature == clips, dead[None, :], feature == owner[None, :]).astype(jnp.float32)
    return jnp.stack([query_part, key_part]), text_part


def rotary_tables(positions, head_dim):
    half = head_dim // 2
    frequency = jnp.exp(-math.log(10000.0) * jnp.arange(half, dtype=jnp.float32) * 2.0 / head_dim)
    angles = frequency[:, None] * positions.astype(jnp.float32)[None, :]
    return jnp.cos(angles), jnp.sin(angles)


def on_device(
    tokens,
    clip_ids,
    positions,
    timesteps,
    text_states,
    text_lengths,
    out_grad,
    attn_gain,
    ffn_gain,
    query_gain,
    key_gain,
    cross_gate,
    w_query,
    w_key,
    w_value,
    w_out,
    w_text_key,
    w_text_value,
    w_ada,
    w_gate,
    w_up,
    w_down,
):
    tensor_size = lax.axis_size("tensor")
    my_rank = lax.axis_index("tensor")
    local_rows = tokens.shape[0]
    group_rows = local_rows * tensor_size
    model_width = tokens.shape[1]
    head_dim = query_gain.shape[0]
    local_heads = w_query.shape[1] // head_dim
    head_cols = local_heads * head_dim
    clip_count = timesteps.shape[0]
    text_len = text_states.shape[1]
    text_rows = clip_count * text_len
    highest_precision = lax.Precision.HIGHEST
    def my_rows(values):
        return lax.dynamic_slice_in_dim(values, my_rank * local_rows, local_rows)

    tokens_all = lax.all_gather(tokens, "tensor", axis=0, tiled=True)
    group_table = clip_table(clip_ids, clip_count)
    my_table = my_rows(group_table)
    embedded = time_embed(timesteps, w_ada.shape[0])
    condition = (embedded * jax.nn.sigmoid(embedded)).astype(jnp.bfloat16)
    mod_part = jnp.dot(condition, w_ada, preferred_element_type=jnp.float32)
    modulation = lax.all_gather(mod_part, "tensor", axis=1, tiled=True)
    per_token = jnp.dot(my_table, modulation[:, model_width:], precision=highest_precision)
    gate_attn = jnp.tanh(per_token[:, :model_width])
    scale_ffn = per_token[:, model_width : 2 * model_width]
    gate_ffn = jnp.tanh(per_token[:, 2 * model_width :])
    grad_output = out_grad.astype(jnp.float32)
    grad_ffn_low = (grad_output * gate_ffn).astype(jnp.bfloat16)
    grad_ffn_all = lax.all_gather(grad_ffn_low, "tensor", axis=0, tiled=True)
    scale_clips = modulation[:, :model_width]
    scale_all = jnp.dot(group_table, scale_clips, precision=highest_precision)
    inputs_all = tokens_all.astype(jnp.float32)
    normed_all = inputs_all * rms_scale(inputs_all)
    attn_all = (normed_all * attn_gain * (1.0 + scale_all)).astype(jnp.bfloat16)
    inputs = tokens.astype(jnp.float32)
    inv_first = rms_scale(inputs)
    normed_first = inputs * inv_first
    scale_attn = my_rows(scale_all)
    w_qkv = jnp.concatenate([w_query, w_key, w_value], axis=1)
    qkv = product(w_qkv, attn_all, ((0,), (1,)))
    text_flat = text_states.reshape(text_rows, text_states.shape[2])
    text_pair = jnp.concatenate(
        [product(w_text_key, text_flat, ((0,), (1,))), product(w_text_value, text_flat, ((0,), (1,)))],
        axis=0,
    )
    gate_tanh = jnp.tanh(lax.dynamic_slice_in_dim(cross_gate, my_rank * local_heads, local_heads))
    table, text_table = clip_tables(clip_ids, text_lengths, clip_count, text_len)
    cosine, sine = rotary_tables(positions, head_dim)
    shared = (
        gate_tanh, qkv, qkv, qkv, text_pair, text_pair, table, text_table, cosine, sine,
        query_gain[:, None], key_gain[:, None],
    )
    mixed_heads, *kept = attention_forward(shared, local_heads, head_dim, clip_count)
    attn_out = scatter_rows(product(mixed_heads, w_out, ((0,), (0,))))
    middle = inputs + gate_attn * attn_out
    inv_second = rms_scale(middle)
    normed_second = middle * inv_second
    ffn_rows = (normed_second * ffn_gain * (1.0 + scale_ffn)).astype(jnp.bfloat16)
    ffn_all = lax.all_gather(ffn_rows, "tensor", axis=0, tiled=True)
    w_pair = jnp.concatenate([w_gate, w_up], axis=1)
    hidden_cols = w_gate.shape[1]
    pair_pre = jnp.dot(ffn_all, w_pair, preferred_element_type=jnp.float32)
    gate_pre = pair_pre[:, :hidden_cols]
    up_pre = pair_pre[:, hidden_cols:]
    sigmoid_gate = jax.nn.sigmoid(gate_pre)
    silu_gate = gate_pre * sigmoid_gate
    hidden = (silu_gate * up_pre).astype(jnp.bfloat16)
    grad_hidden = jnp.dot(grad_ffn_all, w_down.T, preferred_element_type=jnp.float32)
    grad_gate_low = (
        grad_hidden * up_pre * sigmoid_gate * (1.0 + gate_pre * (1.0 - sigmoid_gate))
    ).astype(jnp.bfloat16)
    grad_up_low = (grad_hidden * silu_gate).astype(jnp.bfloat16)
    grad_pair = jnp.concatenate([grad_gate_low, grad_up_low], axis=1)
    grad_ffn_rows = scatter_rows(jnp.dot(grad_pair, w_pair.T, preferred_element_type=jnp.float32))
    down_sum = scatter_groups(
        jnp.dot(grad_ffn_all.T, hidden, preferred_element_type=jnp.float32).astype(jnp.bfloat16)
    )
    pair_sum = scatter_groups(
        jnp.dot(ffn_all.T, grad_pair, preferred_element_type=jnp.float32).astype(jnp.bfloat16)
    )
    ffn_out = scatter_rows(jnp.dot(hidden, w_down, preferred_element_type=jnp.float32))
    block_out = (middle + gate_ffn * ffn_out).astype(jnp.bfloat16)
    grad_gate_ffn = grad_output * ffn_out * (1.0 - gate_ffn * gate_ffn)
    ffn_gain_part = jnp.sum(grad_ffn_rows * normed_second * (1.0 + scale_ffn), axis=0)
    grad_scale_ffn = grad_ffn_rows * normed_second * ffn_gain
    grad_middle = grad_output + rms_backward(
        grad_ffn_rows * ffn_gain * (1.0 + scale_ffn), normed_second, inv_second
    )
    grad_attn_low = (grad_middle * gate_attn).astype(jnp.bfloat16)
    grad_gate_attn = grad_middle * attn_out * (1.0 - gate_attn * gate_attn)
    grad_attn_all = lax.all_gather(grad_attn_low, "tensor", axis=0, tiled=True)
    out_sum = scatter_groups(
        product(grad_attn_all, mixed_heads, ((0,), (1,))).astype(jnp.bfloat16)
    )
    grad_heads = product(w_out, grad_attn_all, ((1,), (1,))).astype(jnp.bfloat16)
    grad_qkv, grad_text, gain_sums = attention_backward(
        shared, grad_heads, kept, local_heads, head_dim, clip_count
    )
    grad_qkv = grad_qkv.reshape(3 * head_cols, group_rows)
    grad_text = grad_text.reshape(2 * head_cols, text_rows)
    query_gain_part = jnp.sum(gain_sums[:, :, 0], axis=0)
    key_gain_part = jnp.sum(gain_sums[:, :, 1], axis=0)
    grad_cross = jnp.sum(gain_sums[:, :, 2], axis=1) * (1.0 - gate_tanh * gate_tanh)
    rows_part = product(grad_qkv, w_qkv, ((0,), (1,)))
    grad_attn_rows = scatter_rows(rows_part)
    text_sum = scatter_groups(
        product(text_flat, grad_text, ((0,), (1,))).astype(jnp.bfloat16)
    )
    qkv_sum = scatter_groups(
        product(attn_all, grad_qkv, ((0,), (1,))).astype(jnp.bfloat16)
    )
    scaled_part = jnp.dot(group_table.T, rows_part * normed_all, precision=highest_precision)
    attn_gain_part = jnp.sum(scaled_part * (1.0 + scale_clips), axis=0)
    own_mod_grad = jnp.dot(
        my_table.T,
        jnp.concatenate([grad_gate_attn, grad_scale_ffn, grad_gate_ffn], axis=1),
        precision=highest_precision,
    )
    clip_mod_grad = jnp.concatenate([scaled_part * attn_gain, own_mod_grad], axis=1)
    part_cols = mod_part.shape[1]

    def mod_block(rank):
        return lax.dynamic_slice_in_dim(clip_mod_grad, (rank % tensor_size) * part_cols, part_cols, 1)

    mod_grad = mod_block(my_rank)
    for shift in range(1, tensor_size):
        mod_grad = mod_grad + lax.ppermute(
            mod_block(my_rank + shift),
            "tensor",
            [(i, (i + shift) % tensor_size) for i in range(tensor_size)],
        )
    mod_grad_groups = spread_groups(mod_grad.astype(jnp.bfloat16))
    mod_grad_groups = mod_grad_groups.reshape(-1, part_cols)
    condition_groups = spread_groups(condition).reshape(-1, condition.shape[1])
    ada_rows = condition.shape[1] // lax.axis_size("dp")
    my_condition = lax.dynamic_slice_in_dim(
        condition_groups, lax.axis_index("dp") * ada_rows, ada_rows, 1
    )
    ada_sum = jnp.dot(my_condition.T, mod_grad_groups, preferred_element_type=jnp.float32)
    gate_full = lax.dynamic_update_slice_in_dim(
        jnp.zeros((cross_gate.shape[0],), jnp.float32), grad_cross, my_rank * local_heads, 0
    )
    small_parts = (attn_gain_part, ffn_gain_part, query_gain_part, key_gain_part, gate_full)
    small_sum = butterfly_sum(jnp.concatenate(small_parts))
    small_sums = []
    start = 0
    for part in small_parts:
        small_sums.append(small_sum[start : start + part.shape[0]])
        start += part.shape[0]
    input_grad = grad_middle + rms_backward(
        grad_attn_rows * attn_gain * (1.0 + scale_attn), normed_first, inv_first
    )
    return (
        block_out,
        input_grad,
        *small_sums,
        qkv_sum[:, :head_cols],
        qkv_sum[:, head_cols : 2 * head_cols],
        qkv_sum[:, 2 * head_cols :],
        out_sum.T,
        text_sum[:, :head_cols],
        text_sum[:, head_cols:],
        ada_sum,
        pair_sum[:, :hidden_cols],
        pair_sum[:, hidden_cols:],
        down_sum.T,
    )


def solution(mesh):
    return jax.shard_map(
        on_device,
        mesh=mesh,
        in_specs=(
            P(("dp", "tensor"), None),
            P("dp"),
            P("dp"),
            P("dp"),
            P("dp", None, None),
            P("dp"),
            P(("dp", "tensor"), None),
            P(),
            P(),
            P(),
            P(),
            P(),
            P(None, "tensor"),
            P(None, "tensor"),
            P(None, "tensor"),
            P("tensor", None),
            P(None, "tensor"),
            P(None, "tensor"),
            P(None, "tensor"),
            P(None, "tensor"),
            P(None, "tensor"),
            P("tensor", None),
        ),
        out_specs=(
            P(("dp", "tensor"), None),
            P(("dp", "tensor"), None),
            P(),
            P(),
            P(),
            P(),
            P(),
            P("dp", "tensor"),
            P("dp", "tensor"),
            P("dp", "tensor"),
            P("tensor", "dp"),
            P("dp", "tensor"),
            P("dp", "tensor"),
            P("dp", "tensor"),
            P("dp", "tensor"),
            P("dp", "tensor"),
            P("tensor", "dp"),
        ),
        check_vma=False,
    )
```

time: 1590 us -> 760 us (0.48)
  waiting for transfers between devices: 1130 us -> 364 us
  matrix products: 223 us -> 120 us
  Pallas kernels: 0 us -> 43.8 us
  blocking collectives: 54.9 us -> 16.2 us
  starting transfers between devices: 2 us -> 38.4 us
  local copies, waits for them, and re-layouts: 72.1 us -> 99.2 us
  other arithmetic: 75.4 us -> 55.7 us
    reduce_scatter x14 -> x4, waiting for transfers between devices: 904 us -> 134 us  [scatter_rows(): lax.psum_scatter(values.astype(jnp.bfloat16), 'tensor', scatter_dimension...]
    dot_general x54 -> x17, matrix products: 186 us -> 92.5 us  [the longest x9 43.8 us: product(): lax.dot_general(left, right, (contract, ((), ())), preferred_element_type...]
    ppermute x0 -> x39, waiting for transfers between devices: none -> 78.1 us  [the longest x36 78.1 us: exchange(): lax.ppermute(values, axis_name, [(i, i ^ distance) for i in range(count)])]
    all_gather x1, waiting for transfers between devices: 62.2 us -> 4.86 us  [on_device(): grad_attn_all = lax.all_gather(grad_attn_low, 'tensor', axis=0, tiled=True)]
    pallas_call x0 -> x2, Pallas kernels: none -> 43.8 us  [the longest x1 25.7 us: attention_backward(): pl.pallas_call(functools.partial(attend_backward, clips, text_rows // cli...]
    dynamic_update_slice x9 -> x0, local copies, waits for them, and re-layouts: 40.9 us -> none  [the longest x4 33.3 us: on_device(): lax.scan(backward_block, initial, (offsets, self_stats, cross_stats))]
    psum x1 -> x0, blocking collectives: 39.9 us -> none  [on_device(): lax.psum((attn_gain_part, ffn_gain_part, query_gain_part, key_gain_part,...]
    ppermute x0 -> x39, starting transfers between devices: none -> 37.6 us  [the longest x36 33.6 us: exchange(): lax.ppermute(values, axis_name, [(i, i ^ distance) for i in range(count)])]
  transfers between devices with their start and end apart: 19 -> 47, of which waited for: 18 -> 26; matrix products, arithmetic and copies ran while one was open for 7% -> 24% of each run, Pallas kernels for 0% -> 0%
where the time goes in v1:
time: 760 us; the launch traced here: 753 us
  waiting for transfers between devices  364 us (48%)
  matrix products  120 us (16%)
  local copies, waits for them, and re-layouts  99.2 us (13%)
  other arithmetic  55.7 us (7%)
  Pallas kernels  43.8 us (6%)
  starting transfers between devices  38.4 us (5%)
  blocking collectives  16.2 us (2%)
  between operations  15.5 us (2%)
    reduce_scatter x4, waiting for transfers between devices, scatter_rows(): lax.psum_scatter(values.astype(jnp.bfloat16), 'tensor', scatter_dimension...  134 us
    ppermute x36, waiting for transfers between devices, exchange(): lax.ppermute(values, axis_name, [(i, i ^ distance) for i in range(count)])  78.1 us
    all_gather x1, waiting for transfers between devices, on_device(): ffn_all = lax.all_gather(ffn_rows, 'tensor', axis=0, tiled=True)  56.9 us
    all_gather x1, waiting for transfers between devices, on_device(): grad_ffn_all = lax.all_gather(grad_ffn_low, 'tensor', axis=0, tiled=True)  52.4 us
    dot_general x9, matrix products, product(): lax.dot_general(left, right, (contract, ((), ())), preferred_element_type...  43.8 us
    all_gather x1, waiting for transfers between devices, on_device(): tokens_all = lax.all_gather(tokens, 'tensor', axis=0, tiled=True)  36.4 us
    unnamed x128, local copies, waits for them, and re-layouts  35.2 us
    ppermute x36, starting transfers between devices, exchange(): lax.ppermute(values, axis_name, [(i, i ^ distance) for i in range(count)])  33.6 us
  transfers between devices with their start and end apart: 47, of which 26 were waited for; matrix products, arithmetic and copies ran while one was open for 24% of the time, Pallas kernels for 0%

profile of v1, /device:TPU:0, one launch (start us, length us, event | category | flops | bytes accessed | tf_op | source)
XLA Modules:
  0.0 753.1 jit_solution(6595530909325046624)
XLA Ops:
  13.7 16.2 %all_gather.15 = f32[3,6144]{1,0:T(4,128)} all-gather(f32[3,1536]{1,0:T(4,128)S(1)} %fusion.70), channel_id=1, replica_groups=mesh['dp'=8,'tensor'=4] {'tensor'}, dimensions={1}, use_global_device_ids=true | all-gather | bytes 92160 | tf_op jit(solution)/shard_map/all_gather | solution.py:391
  40.2 36.4 %all-gather.5.cloned.1.call-done = bf16[1024,1536]{1,0:T(8,128)(2,1)} async-done(((bf16[256,1536]{1,0:T(8,128)(2,1)}), bf16[1024,1536]{1,0:T(8,128)(2,1)}) %all-gather.5.cloned.1.call-update) | async-done | bytes 3145744 | tf_op jit(solution)/shard_map/all_gather | solution.py:385
  79.4 6.8 fusion.3
  86.3 8.8 %fusion.91.query.key.value = f32[1152,1024]{1,0:T(8,128)} fusion(bf16[1536,1152]{1,0:T(8,128)(2,1)} %constant_dynamic-update-slice_fusion, bf16[1024,1536]{1,0:T(8,128)(2,1)S(1)} %get-tuple-element.95), kind=kOutput, calls=%fused_computation.247 | convolution fusion | flops 3623878656 | bytes 11403264 | tf_op jit(solution)/shard_map/dot_general | solution.py:101
  95.1 18.1 %shard_map.341 = (bf16[384,1024]{1,0:T(8,128)(2,1)S(1)}, f32[384,1024]{1,0:T(8,128)S(1)}, f32[384,1024]{1,0:T(8,128)S(1)}, f32[6,1,1024]{2,1,0:T(1,128)S(1)}, f32[6,1,1024]{2,1,0:T(1,128)S(1)}) custom-call(f32[6]{0:T(128)S(1)} %dynamic-slice_tanh_fusion.gates, f32[1152,1024]{1,0:T(8,128)} %fusion.91.query.key.value, f32[1152,1024]{1,0:T(8,128)} %fusion.91.query.key.value, ...), custom_call_target="tpu_custom_call" | custom-call | flops 3221225472 | bytes 9437184 | tf_op jit(solution)/shard_map/pallas_call | solution.py:287
  126.3 54.0 %reduce-scatter.5.cloned.1.call-done = bf16[256,1536]{1,0:T(8,128)(2,1)} async-done(((bf16[1024,1536]{1,0:T(8,128)(2,1)}), bf16[256,1536]{1,0:T(8,128)(2,1)}) %reduce-scatter.5.cloned.1.call-update) | async-done | bytes 786448 | tf_op jit(solution)/shard_map/reduce_scatter | solution.py:95
  193.4 56.9 %all-gather.7.cloned.1.call-done = bf16[1024,1536]{1,0:T(8,128)(2,1)} async-done(((bf16[256,1536]{1,0:T(8,128)(2,1)}), bf16[1024,1536]{1,0:T(8,128)(2,1)}) %all-gather.7.cloned.1.call-update) | async-done | bytes 3145744 | tf_op jit(solution)/shard_map/all_gather | solution.py:428
  250.3 11.8 %fusion.94 = f32[1024,2048]{1,0:T(8,128)} fusion(bf16[1024,1536]{1,0:T(8,128)(2,1)} %all-gather.7.cloned.1.call-done, bf16[1536,2048]{1,0:T(8,128)(2,1)} %constant_dynamic-update-slice_fusion.3), kind=kOutput, calls=%fused_computation.250 | convolution fusion | flops 6442450944 | bytes 17825792 | tf_op jit(solution)/shard_map/dot_general | solution.py:431
  262.1 52.4 %all-gather.9.cloned.1.call-done = bf16[1024,1536]{1,0:T(8,128)(2,1)} async-done(((bf16[256,1536]{1,0:T(8,128)(2,1)}), bf16[1024,1536]{1,0:T(8,128)(2,1)}) %all-gather.9.cloned.1.call-update) | async-done | bytes 3145744 | tf_op jit(solution)/shard_map/all_gather | solution.py:398
  314.5 11.6 %multiply_convert_fusion.1 = (bf16[1024,1024]{1,0:T(8,128)(2,1)S(1)}, bf16[1024,1024]{1,0:T(8,128)(2,1)S(1)}, bf16[1024,1024]{1,0:T(8,128)(2,1)}) fusion(f32[1024,2048]{1,0:T(8,128)} %fusion.94, bf16[1024,1536]{1,0:T(8,128)(2,1)} %all-gather.9.cloned.1.call-done, bf16[1024,1536]{1,0:T(8,128)(2,1)} %param.43), kind=kOutput, calls=%fused_computation.24 | convolution fusion | flops 3236954112 | bytes 20971520 | tf_op jit(solution)/shard_map/dot_general | solution.py:437
  328.1 10.0 %convolution_convert_fusion.3 = bf16[1024,1536]{1,0:T(8,128)(2,1)} fusion(bf16[1536,2048]{1,0:T(8,128)(2,1)} %constant_dynamic-update-slice_fusion.3, bf16[1024,1024]{1,0:T(8,128)(2,1)S(1)} %get-tuple-element.43, bf16[1024,1024]{1,0:T(8,128)(2,1)S(1)} %get-tuple-element.42), kind=kOutput, calls=%fused_computation.28 | convolution fusion | flops 6452412416 | bytes 13631488 | tf_op jit(solution)/shard_map/dot_general | solution.py:443
  338.1 7.7 %convolution_convert_fusion.6 = bf16[1024,1536]{1,0:T(8,128)(2,1)} fusion(bf16[1024,1024]{1,0:T(8,128)(2,1)} %get-tuple-element.44, bf16[1024,1536]{1,0:T(8,128)(2,1)} %param.43), kind=kOutput, calls=%fused_computation.31 | convolution fusion | flops 3222798336 | bytes 8388608 | tf_op jit(solution)/shard_map/dot_general | solution.py:450
  363.4 7.3 convolution_convert_fusion.1
  376.3 20.8 %reduce-scatter.9.cloned.1.call-done = bf16[256,1536]{1,0:T(8,128)(2,1)} async-done(((bf16[1024,1536]{1,0:T(8,128)(2,1)}), bf16[256,1536]{1,0:T(8,128)(2,1)}) %reduce-scatter.9.cloned.1.call-update) | async-done | bytes 786448 | tf_op jit(solution)/shard_map/reduce_scatter | solution.py:95
  400.6 59.0 %reduce-scatter.7.cloned.1.call-done = bf16[256,1536]{1,0:T(8,128)(2,1)} async-done(((bf16[1024,1536]{1,0:T(8,128)(2,1)}), bf16[256,1536]{1,0:T(8,128)(2,1)}) %reduce-scatter.7.cloned.1.call-update) | async-done | bytes 786448 | tf_op jit(solution)/shard_map/reduce_scatter | solution.py:95
  495.3 17.9 %collective-permute-done.36 = bf16[192,512]{1,0:T(8,128)(2,1)S(1)} collective-permute-done((bf16[192,512]{1,0:T(8,128)(2,1)S(1)}, bf16[192,512]{1,0:T(8,128)(2,1)S(1)}, u32[]{:S(2)}, u32[]{:S(2)}) %collective-permute-start.36) | collective-permute-done | bytes 196640 | tf_op jit(solution)/shard_map/ppermute | solution.py:39
  537.1 25.7 %shard_map.342 = (bf16[3,384,1024]{2,1,0:T(8,128)(2,1)}, bf16[2,384,384]{2,1,0:T(8,128)(2,1)S(1)}, f32[6,64,128]{2,1,0:T(8,128)S(1)}) custom-call(f32[6]{0:T(128)S(1)} %dynamic-slice_tanh_fusion.gates, f32[1152,1024]{1,0:T(8,128)} %fusion.91.query.key.value, f32[1152,1024]{1,0:T(8,128)} %fusion.91.query.key.value, f32[1152,1024]{1,0:T(8,128)} %fusion.91.query.key.value, ...), custom_call_target="tpu_custom_call" | custom-call | flops 8053063680 | bytes 11796480 | tf_op jit(solution)/shard_map/pallas_call | solution.py:305
  562.9 8.9 %fusion.90 = (bf16[1024,1536]{1,0:T(8,128)(2,1)}, f32[1024,1536]{1,0:T(8,128)S(1)}) fusion(bf16[1152,1024]{1,0:T(8,128)(2,1)} %bitcast.206, bf16[1536,1152]{1,0:T(8,128)(2,1)} %constant_dynamic-update-slice_fusion), kind=kOutput, calls=%fused_computation.246 | convolution fusion | flops 3625451520 | bytes 15335424 | tf_op jit(solution)/shard_map/dot_general | solution.py:101
  591.4 11.2 %reshape.450 = bf16[2,2,2,512,768]{3,2,1,0,4:T(2,128)(2,1)} reshape(bf16[4096,768]{0,1:T(8,128)(2,1)} %fusion.9) | data formatting | bytes 12582912 | tf_op jit(solution)/shard_map/reshape | solution.py:64
  602.5 15.7 %constant_dynamic-slice_fusion.2 = (bf16[2,2,1,512,768]{3,2,1,0,4:T(2,128)(2,1)}, bf16[2,2,1,512,768]{3,2,1,0,4:T(2,128)(2,1)}) fusion(bf16[2,2,2,512,768]{3,2,1,0,4:T(2,128)(2,1)} %reshape.450, s32[]{:T(128)S(6)} %select_n.266, s32[]{:T(128)S(6)} %select_n.267), kind=kLoop, calls=%fused_computation.196 | loop fusion | bytes 12582920 | tf_op jit(solution)/shard_map/jit(dynamic_index_in_dim)/dynamic_slice | solution.py:55
  618.3 15.2 %copy.64 = bf16[2,2,1,512,768]{4,3,1,0,2:T(8,128)(2,1)} copy(bf16[2,2,1,512,768]{3,2,1,0,4:T(2,128)(2,1)} %get-tuple-element.46) | data formatting | bytes 6291456 | tf_op jit(solution)/shard_map/jit(dynamic_index_in_dim)/dynamic_slice | solution.py:54
  642.0 15.4 %copy.71 = bf16[2,2,1,512,768]{4,3,1,0,2:T(8,128)(2,1)} copy(bf16[2,2,1,512,768]{3,2,1,0,4:T(2,128)(2,1)} %get-tuple-element.45) | data formatting | bytes 6291456
  692.7 7.8 %collective-permute-done.6 = bf16[2,192,576]{2,1,0:T(8,128)(2,1)S(1)} collective-permute-done((bf16[2,192,576]{2,1,0:T(8,128)(2,1)S(1)}, bf16[2,192,576]{2,1,0:T(8,128)(2,1)S(1)}, u32[]{:S(2)}, u32[]{:S(2)}) %collective-permute-start.6) | collective-permute-done | bytes 442400 | tf_op jit(solution)/shard_map/ppermute | solution.py:39
  715.2 8.6 %collective-permute-done.18 = bf16[2,512,384]{2,1,0:T(8,128)(2,1)S(1)} collective-permute-done((bf16[2,512,384]{2,1,0:T(8,128)(2,1)S(1)}, bf16[2,512,384]{2,1,0:T(8,128)(2,1)S(1)}, u32[]{:S(2)}, u32[]{:S(2)}) %collective-permute-start.18) | collective-permute-done | bytes 786464 | tf_op jit(solution)/shard_map/ppermute | solution.py:39
  (355 shorter events, 233.3 us)
Async XLA Ops:
  7.2 69.4 %all-gather.5.cloned.1.call-start = ((), (), s32[]{:S(2)}) async-start(), calls=%async_computation.4 | async-start | bytes 3932160 | tf_op jit(solution)/shard_map/all_gather | solution.py:385
  8.0 172.3 %reduce-scatter.5.cloned.1.call-start = ((), (), s32[]{:S(2)}) async-start(), calls=%async_computation.5 | async-start | bytes 3932160 | tf_op jit(solution)/shard_map/reduce_scatter | solution.py:95
  121.1 129.1 %all-gather.7.cloned.1.call-start = ((), (), s32[]{:S(2)}) async-start(), calls=%async_computation.6 | async-start | bytes 3932160 | tf_op jit(solution)/shard_map/all_gather | solution.py:428
  186.6 127.9 %all-gather.9.cloned.1.call-start = ((), (), s32[]{:S(2)}) async-start(), calls=%async_computation.8 | async-start | bytes 3932160 | tf_op jit(solution)/shard_map/all_gather | solution.py:398
  187.2 209.9 %reduce-scatter.9.cloned.1.call-start = ((), (), s32[]{:S(2)}) async-start(), calls=%async_computation.9 | async-start | bytes 3932160 | tf_op jit(solution)/shard_map/reduce_scatter | solution.py:95
  338.1 121.5 %reduce-scatter.7.cloned.1.call-start = ((), (), s32[]{:S(2)}) async-start(), calls=%async_computation.7 | async-start | bytes 3932160 | tf_op jit(solution)/shard_map/reduce_scatter | solution.py:95
  345.8 187.4 %all-gather.11.cloned.1.call-start = ((), (), s32[]{:S(2)}) async-start(), calls=%async_computation.10 | async-start | bytes 3932160 | tf_op jit(solution)/shard_map/all_gather | solution.py:460
  374.5 111.6 %collective-permute-start.29 = (bf16[2,2,192,2048]{3,2,1,0:T(8,128)(2,1)}, bf16[2,2,192,2048]{3,2,1,0:T(8,128)(2,1)}, u32[]{:S(2)}, u32[]{:S(2)}) collective-permute-start(bf16[2,2,192,2048]{3,2,1,0:T(8,128)(2,1)} %dynamic-slice_bitcast_fusion), channel_id=1, source_target_pairs={{0,4},{4,0},{8,12},{12,8},{16,20},{20,16},{24,28},{28,24},{1,5},{5... | collective-permute-start | bytes 9437192 | tf_op jit(solution)/shard_map/ppermute | solution.py:39
  469.6 270.5 %reduce-scatter.11.cloned.1.call-start = ((), (), s32[]{:S(2)}) async-start(), calls=%async_computation.11 | async-start | bytes 3932160 | tf_op jit(solution)/shard_map/reduce_scatter | solution.py:95
  477.7 16.9 %collective-permute-start.37 = (bf16[2,192,512]{2,1,0:T(8,128)(2,1)S(1)}, bf16[2,192,512]{2,1,0:T(8,128)(2,1)S(1)}, u32[]{:S(2)}, u32[]{:S(2)}) collective-permute-start(bf16[2,192,512]{2,1,0:T(8,128)(2,1)S(1)} %dynamic-slice_bitcast_fusion.9), channel_id=1, source_target_pairs={{0,16},{4,20},{8,24},{12,28},{16,0},{20,4},{24,8},{28,12},{1,17},{... | collective-permute-start | bytes 1179656 | tf_op jit(solution)/shard_map/ppermute | solution.py:39
  490.7 22.5 %collective-permute-start.32 = (bf16[2,192,1024]{2,1,0:T(8,128)(2,1)S(1)}, bf16[2,192,1024]{2,1,0:T(8,128)(2,1)S(1)}, u32[]{:S(2)}, u32[]{:S(2)}) collective-permute-start(bf16[2,192,1024]{2,1,0:T(8,128)(2,1)S(1)} %dynamic-slice_bitcast_fusion.2), channel_id=1, source_target_pairs={{0,16},{4,20},{8,24},{12,28},{16,0},{20,4},{24,8},{28,12},{1,17},{... | collective-permute-start | bytes 2359304 | tf_op jit(solution)/shard_map/ppermute | solution.py:39
  492.3 20.9 %collective-permute-start.36 = (bf16[192,512]{1,0:T(8,128)(2,1)S(1)}, bf16[192,512]{1,0:T(8,128)(2,1)S(1)}, u32[]{:S(2)}, u32[]{:S(2)}) collective-permute-start(bf16[192,512]{1,0:T(8,128)(2,1)S(1)} %dynamic-slice_bitcast_fusion.18), channel_id=1, source_target_pairs={{0,16},{4,20},{8,24},{12,28},{16,0},{20,4},{24,8},{28,12},{1,17},{... | collective-permute-start | bytes 589832 | tf_op jit(solution)/shard_map/ppermute | solution.py:39
  493.0 22.2 %collective-permute-start.30 = (bf16[2,192,1024]{2,1,0:T(8,128)(2,1)S(1)}, bf16[2,192,1024]{2,1,0:T(8,128)(2,1)S(1)}, u32[]{:S(2)}, u32[]{:S(2)}) collective-permute-start(bf16[2,192,1024]{2,1,0:T(8,128)(2,1)S(1)} %dynamic-slice_bitcast_fusion.3), channel_id=1, source_target_pairs={{0,8},{4,12},{8,0},{12,4},{16,24},{20,28},{24,16},{28,20},{1,9},{5... | collective-permute-start | bytes 2359304 | tf_op jit(solution)/shard_map/ppermute | solution.py:39
  494.7 22.5 %collective-permute-start.38 = (bf16[192,512]{1,0:T(8,128)(2,1)S(1)}, bf16[192,512]{1,0:T(8,128)(2,1)S(1)}, u32[]{:S(2)}, u32[]{:S(2)}) collective-permute-start(bf16[192,512]{1,0:T(8,128)(2,1)S(1)} %dynamic-slice_bitcast_fusion.17), channel_id=1, source_target_pairs={{0,8},{4,12},{8,0},{12,4},{16,24},{20,28},{24,16},{28,20},{1,9},{5... | collective-permute-start | bytes 589832 | tf_op jit(solution)/shard_map/ppermute | solution.py:39
  582.1 57.9 %collective-permute-start.23 = (f32[3,1536]{1,0:T(4,128)}, f32[3,1536]{1,0:T(4,128)S(1)}, u32[]{:S(2)}, u32[]{:S(2)}) collective-permute-start(f32[3,1536]{1,0:T(4,128)} %get-tuple-element.70), channel_id=1, source_target_pairs={{0,1},{1,2},{2,3},{3,0},{4,5},{5,6},{6,7},{7,4},{8,9},{9,10},{10,1... | collective-permute-start | bytes 55304 | tf_op jit(solution)/shard_map/ppermute | solution.py:496
  582.1 57.9 %collective-permute-start.24 = (f32[3,1536]{1,0:T(4,128)}, f32[3,1536]{1,0:T(4,128)}, u32[]{:S(2)}, u32[]{:S(2)}) collective-permute-start(f32[3,1536]{1,0:T(4,128)} %get-tuple-element.71), channel_id=1, source_target_pairs={{0,2},{1,3},{2,0},{3,1},{4,6},{5,7},{6,4},{7,5},{8,10},{9,11},{10,... | collective-permute-start | bytes 55304 | tf_op jit(solution)/shard_map/ppermute | solution.py:496
  583.3 56.6 %collective-permute-start.25 = (f32[3,1536]{1,0:T(4,128)S(1)}, f32[3,1536]{1,0:T(4,128)}, u32[]{:S(2)}, u32[]{:S(2)}) collective-permute-start(f32[3,1536]{1,0:T(4,128)S(1)} %get-tuple-element.72), channel_id=1, source_target_pairs={{0,3},{1,0},{2,1},{3,2},{4,7},{5,4},{6,5},{7,6},{8,11},{9,8},{10,9... | collective-permute-start | bytes 55304 | tf_op jit(solution)/shard_map/ppermute | solution.py:496
  633.5 68.3 %collective-permute-start.15 = (bf16[2,2,512,768]{3,2,1,0:T(8,128)(2,1)}, bf16[2,2,512,768]{3,2,1,0:T(8,128)(2,1)}, u32[]{:S(2)}, u32[]{:S(2)}) collective-permute-start(bf16[2,2,512,768]{3,2,1,0:T(8,128)(2,1)} %bitcast.201), channel_id=1, source_target_pairs={{0,4},{4,0},{8,12},{12,8},{16,20},{20,16},{24,28},{28,24},{1,5},{5... | collective-permute-start | bytes 9437192 | tf_op jit(solution)/shard_map/ppermute | solution.py:39
  638.4 19.2 %collective-permute-start.1 = (f32[3224]{0:T(1024)S(1)}, f32[3224]{0:T(1024)S(1)}, u32[]{:S(2)}, u32[]{:S(2)}) collective-permute-start(f32[3224]{0:T(1024)S(1)} %add.348), channel_id=1, source_target_pairs={{0,2},{1,3},{2,0},{3,1},{4,6},{5,7},{6,4},{7,5},{8,10},{9,11},{10,... | collective-permute-start | bytes 38696 | tf_op jit(solution)/shard_map/ppermute | solution.py:39
  640.8 17.2 %collective-permute-start.26 = (bf16[1,3,1536]{2,1,0:T(4,128)(2,1)S(1)}, bf16[1,3,1536]{2,1,0:T(4,128)(2,1)S(1)}, u32[]{:S(2)}, u32[]{:S(2)}) collective-permute-start(bf16[1,3,1536]{2,1,0:T(4,128)(2,1)S(1)} %fusion.69), channel_id=1, source_target_pairs={{0,4},{4,0},{8,12},{12,8},{16,20},{20,16},{24,28},{28,24},{1,5},{5... | collective-permute-start | bytes 27656 | tf_op jit(solution)/shard_map/ppermute | solution.py:39
  657.4 16.8 %collective-permute-start.10 = (bf16[2,2,192,384]{3,2,1,0:T(8,128)(2,1)}, bf16[2,2,192,384]{3,2,1,0:T(8,128)(2,1)}, u32[]{:S(2)}, u32[]{:S(2)}) collective-permute-start(bf16[2,2,192,384]{3,2,1,0:T(8,128)(2,1)} %dynamic-slice_bitcast_fusion.6), channel_id=1, source_target_pairs={{0,4},{4,0},{8,12},{12,8},{16,20},{20,16},{24,28},{28,24},{1,5},{5... | collective-permute-start | bytes 1769480 | tf_op jit(solution)/shard_map/ppermute | solution.py:39
  664.4 22.0 %collective-permute-start.5 = (bf16[2,2,192,1152]{3,2,0,1:T(8,128)(2,1)}, bf16[2,2,192,1152]{3,2,0,1:T(8,128)(2,1)}, u32[]{:S(2)}, u32[]{:S(2)}) collective-permute-start(bf16[2,2,192,1152]{3,2,0,1:T(8,128)(2,1)} %bitcast.191), channel_id=1, source_target_pairs={{0,4},{4,0},{8,12},{12,8},{16,20},{20,16},{24,28},{28,24},{1,5},{5... | collective-permute-start | bytes 5308424 | tf_op jit(solution)/shard_map/ppermute | solution.py:39
  705.0 18.8 %collective-permute-start.18 = (bf16[2,512,384]{2,1,0:T(8,128)(2,1)S(1)}, bf16[2,512,384]{2,1,0:T(8,128)(2,1)S(1)}, u32[]{:S(2)}, u32[]{:S(2)}) collective-permute-start(bf16[2,512,384]{2,1,0:T(8,128)(2,1)S(1)} %dynamic-slice_bitcast_fusion.4), channel_id=1, source_target_pairs={{0,16},{4,20},{8,24},{12,28},{16,0},{20,4},{24,8},{28,12},{1,17},{... | collective-permute-start | bytes 2359304 | tf_op jit(solution)/shard_map/ppermute | solution.py:39
  707.0 24.0 %collective-permute-start.16 = (bf16[2,512,384]{2,1,0:T(8,128)(2,1)S(1)}, bf16[2,512,384]{2,1,0:T(8,128)(2,1)S(1)}, u32[]{:S(2)}, u32[]{:S(2)}) collective-permute-start(bf16[2,512,384]{2,1,0:T(8,128)(2,1)S(1)} %dynamic-slice_bitcast_fusion.5), channel_id=1, source_target_pairs={{0,8},{4,12},{8,0},{12,4},{16,24},{20,28},{24,16},{28,20},{1,9},{5... | collective-permute-start | bytes 2359304 | tf_op jit(solution)/shard_map/ppermute | solution.py:39
  (85 other events, 759.9 us)
Sparse Core Ops, SparseCore 0:
  9.6 66.9 all-gather.4
  121.3 58.9 reduce-scatter.4
  186.7 63.5 all-gather.6
  252.3 62.1 all-gather.8
  338.2 58.8 reduce-scatter.8
  399.3 60.2 reduce-scatter.6
  469.7 63.5 all-gather.10
  664.6 59.4 reduce-scatter.10

commit v2 on v1

v2 whole, which is shorter than its diff:
```python
import functools
import math

import jax
import jax.numpy as jnp
from jax import lax
from jax.experimental import pallas as pl
from jax.experimental.pallas import tpu as pltpu
from jax.sharding import PartitionSpec as P

epsilon = 1e-06


def rms_scale(values):
    return lax.rsqrt(jnp.mean(values * values, axis=-1, keepdims=True) + epsilon)


def rms_backward(grad_hat, normed, scaling):
    return scaling * (grad_hat - normed * jnp.mean(grad_hat * normed, axis=-1, keepdims=True))


def time_embed(time_steps, embed_width):
    half_width = embed_width // 2
    frequency = jnp.exp(-math.log(10000.0) * jnp.arange(half_width, dtype=jnp.float32) / half_width)
    angles = time_steps.astype(jnp.float32)[:, None] * frequency[None, :]
    return jnp.concatenate([jnp.cos(angles), jnp.sin(angles)], axis=-1)


def time_columns(time_steps, first, width, embed_width):
    half_width = embed_width // 2
    columns = first + jnp.arange(width, dtype=jnp.int32)
    frequency = jnp.exp(
        -math.log(10000.0) * (columns % half_width).astype(jnp.float32) / half_width
    )
    angles = time_steps[:, None] * frequency[None, :]
    embedded = jnp.where((columns < half_width)[None, :], jnp.cos(angles), jnp.sin(angles))
    return (embedded * jax.nn.sigmoid(embedded)).astype(jnp.bfloat16)


def exchange(values, axis_name, distance):
    count = lax.axis_size(axis_name)
    return lax.ppermute(values, axis_name, [(i, i ^ distance) for i in range(count)])


def product(left, right, contract=((1,), (0,))):
    return lax.dot_general(left, right, (contract, ((), ())), preferred_element_type=jnp.float32)


def head_norm(raw):
    return lax.rsqrt(jnp.mean(raw * raw, axis=0, keepdims=True) + epsilon)


def turn(values, cosine, sine):
    half = values.shape[0] // 2
    lead, tail = values[:half], values[half:]
    return jnp.concatenate([lead * cosine - tail * sine, lead * sine + tail * cosine], axis=0)


def turn_back(values, cosine, sine):
    half = values.shape[0] // 2
    lead, tail = values[:half], values[half:]
    return jnp.concatenate([lead * cosine + tail * sine, tail * cosine - lead * sine], axis=0)


def widen(values, extra):
    rows = values.shape[0] + extra.shape[0]
    pad = jnp.zeros((128 - rows, values.shape[1]), values.dtype)
    return jnp.concatenate([values, extra.astype(values.dtype), pad], axis=0)


def text_range(block, blocks, clips, slots):
    first = 0 if block == 0 else slots
    last = (clips if block == blocks - 1 else clips - 1) * slots
    return first, last


def total(terms):
    result = terms[0].astype(jnp.float32)
    for term in terms[1:]:
        result = result + term.astype(jnp.float32)
    return result


edge_rows = 256
apart = 2048.0
vmem_bytes = 56 << 20


def params():
    return pltpu.CompilerParams(vmem_limit_bytes=vmem_bytes)


def costs(flops, moved, transcendentals=0):
    return pl.CostEstimate(flops=flops // 64, bytes_accessed=moved // 64, transcendentals=0)


def struct(shape, kind=jnp.float32):
    return jax.ShapeDtypeStruct(shape, kind)


smem_spec = pl.BlockSpec(memory_space=pltpu.SMEM)


def whole_spec(shape):
    return pl.BlockSpec(shape, lambda *at: (0,) * len(shape))


def modulation_rows(mod, rank, which):
    count = mod.shape[0]
    per = count // 4
    shares = [mod[lax.rem(which * per + i - rank + count, count)] for i in range(per)]
    return shares[0] if per == 1 else jnp.concatenate(shares, axis=1)


def by_clip(vectors, ids):
    result = vectors[0:1]
    for clip in range(1, vectors.shape[0]):
        result = jnp.where(ids == clip, vectors[clip : clip + 1], result)
    return result


def sums_by_clip(values, ids, clips):
    return jnp.concatenate(
        [
            jnp.sum(jnp.where(ids == clip, values, 0.0), axis=0, keepdims=True)
            for clip in range(clips)
        ],
        axis=0,
    )


def gate_kernel(rank, mod, ids, out_grad, result):
    gate = by_clip(jnp.tanh(modulation_rows(mod, rank[0], 3)), ids[...])
    result[...] = (out_grad[...].astype(jnp.float32) * gate).astype(jnp.bfloat16)


def gated_gradient(rank, mod, ids, out_grad):
    return pl.pallas_call(
        gate_kernel,
        in_specs=[smem_spec] + [pl.BlockSpec(memory_space=pltpu.VMEM)] * 3,
        out_shape=struct(out_grad.shape, jnp.bfloat16),
        compiler_params=params(),
        cost_estimate=costs(out_grad.size * 4, out_grad.size * 4),
    )(rank, mod, ids, out_grad)


def project_kernel(rank, mod, ids, gain, tokens, w_query, w_key, w_value, rows_out, qkv):
    inputs = tokens[...].astype(jnp.float32)
    scaled = gain[...] * (1.0 + modulation_rows(mod, rank[0], 0))
    rows = (inputs * rms_scale(inputs) * by_clip(scaled, ids[...])).astype(jnp.bfloat16)
    rows_out[...] = rows
    for part, weight in enumerate((w_query, w_key, w_value)):
        qkv[part] = product(rows, weight[...]).T


def project(rank, mod, ids, gain, tokens_all, w_query, w_key, w_value):
    rows, width = tokens_all.shape
    cols = w_query.shape[1]
    step = edge_rows
    return pl.pallas_call(
        project_kernel,
        grid=(rows // step,),
        in_specs=[
            smem_spec, whole_spec(mod.shape), pl.BlockSpec((step, 1), lambda i: (i, 0)),
            whole_spec(gain.shape), pl.BlockSpec((step, width), lambda i: (i, 0)),
            whole_spec((width, cols)), whole_spec((width, cols)), whole_spec((width, cols)),
        ],
        out_specs=[
            pl.BlockSpec((step, width), lambda i: (i, 0)),
            pl.BlockSpec((3, cols, step), lambda i: (0, 0, i)),
        ],
        out_shape=[struct((rows, width), jnp.bfloat16), struct((3, cols, rows))],
        compiler_params=params(),
        cost_estimate=costs(6 * rows * width * cols, rows * width * 4 + 3 * cols * (width * 2 + rows * 4)),
    )(rank, mod, ids, gain, tokens_all, w_query, w_key, w_value)


def assemble_kernel(mine, held, arrived, out):
    core = mine[0] & 1
    out[:, core] = held[0]
    out[:, 1 - core] = arrived[0]


def assemble(held, arrived):
    half, ranks, rows, width = held.shape
    bits = half.bit_length() - 1

    def place(i, mine):
        pair = sum(((i >> k) & 1) << (bits - 1 - k) for k in range(bits))
        return 0, (mine[0] >> 1) ^ pair, 0, 0

    spec = pl.BlockSpec((1, ranks, rows, width), lambda i, mine: (i, 0, 0, 0))
    return pl.pallas_call(
        assemble_kernel,
        grid_spec=pltpu.PrefetchScalarGridSpec(
            num_scalar_prefetch=1,
            grid=(half,),
            in_specs=[spec, spec],
            out_specs=pl.BlockSpec((ranks, 2, rows, width), place),
        ),
        out_shape=struct((ranks, 2 * half, rows, width), held.dtype),
        compiler_params=params(),
        cost_estimate=costs(0, 0),
    )(lax.axis_index("dp")[None], held, arrived)


def middle_kernel(count, rank, mod, ids, gain, tokens, w_out, *refs):
    mixed, (attn_out, middle, *rows_out) = refs[:count], refs[count:]
    total = product(mixed[0][...], w_out[0], ((0,), (0,)))
    for m in range(1, count):
        total += product(mixed[m][...], w_out[m], ((0,), (0,)))
    attn_out[...] = total
    where_clip = ids[...]
    gate = by_clip(jnp.tanh(modulation_rows(mod, rank[0], 1)), where_clip)
    values = tokens[...].astype(jnp.float32) + gate * total
    middle[...] = values
    scaled = gain[...] * (1.0 + modulation_rows(mod, rank[0], 2))
    rows = (values * rms_scale(values) * by_clip(scaled, where_clip)).astype(jnp.bfloat16)
    step = rows.shape[0] // len(rows_out)
    for cut, ref in enumerate(rows_out):
        ref[...] = rows[cut * step : (cut + 1) * step]


def middle_forward(rank, mod, ids, gain, tokens, w_out_all, mixed, cuts):
    rows, width = tokens.shape
    vmem = pl.BlockSpec(memory_space=pltpu.VMEM)
    return pl.pallas_call(
        functools.partial(middle_kernel, len(mixed)),
        in_specs=[smem_spec] + [vmem] * (5 + len(mixed)),
        out_shape=[struct((rows, width))] * 2
        + [struct((rows // cuts, width), jnp.bfloat16)] * cuts,
        compiler_params=params(),
        cost_estimate=costs(2 * rows * w_out_all.size // 1, w_out_all.size * 2 + rows * width * 14),
    )(rank, mod, ids, gain, tokens, w_out_all, *mixed)


def middle_back_kernel(cuts, count, rank, mod, ids, gain, middle, attn_out, out_grad, w_out, *refs):
    pieces = []
    at = 0
    for terms in cuts:
        pieces.append(total([ref[...] for ref in refs[at : at + terms]]))
        at += terms
    grad_middle, grad_low, scale_sums, gate_sums = refs[at : at + 4]
    grad_mixed = refs[at + 4 :]
    clips = mod.shape[1]
    where_clip = ids[...]
    values = middle[...]
    inverse = rms_scale(values)
    normed = values * inverse
    grads = jnp.concatenate(pieces, axis=0)
    scale_sums[...] = sums_by_clip(grads * normed, where_clip, clips)
    scaled = gain[...] * (1.0 + modulation_rows(mod, rank[0], 2))
    result = out_grad[...].astype(jnp.float32) + rms_backward(
        grads * by_clip(scaled, where_clip), normed, inverse
    )
    grad_middle[...] = result
    gate = jnp.tanh(modulation_rows(mod, rank[0], 1))
    gate_sums[...] = sums_by_clip(result * attn_out[...], where_clip, clips)
    low = (result * by_clip(gate, where_clip)).astype(jnp.bfloat16)
    grad_low[...] = low
    for m in range(count):
        grad_mixed[m][...] = product(w_out[m], low, ((1,), (1,))).astype(jnp.bfloat16)


def middle_backward(rank, mod, ids, gain, middle, attn_out, out_grad, w_out_all, pieces):
    rows, width = middle.shape
    count, cols, _ = w_out_all.shape
    clips = mod.shape[1]
    vmem = pl.BlockSpec(memory_space=pltpu.VMEM)
    return pl.pallas_call(
        functools.partial(middle_back_kernel, [len(terms) for terms in pieces], count),
        in_specs=[smem_spec] + [vmem] * (7 + sum(len(terms) for terms in pieces)),
        out_shape=[
            struct((rows, width)), struct((rows, width), jnp.bfloat16),
            struct((clips, width)), struct((clips, width)),
        ]
        + [struct((cols, rows), jnp.bfloat16)] * count,
        compiler_params=params(),
        cost_estimate=costs(2 * rows * w_out_all.size, w_out_all.size * 2 + rows * width * 20),
    )(rank, mod, ids, gain, middle, attn_out, out_grad, w_out_all, *sum(pieces, []))


def ffn_kernel(rows, grads, w_gate, w_up, w_down, hidden, grad_gate, grad_up, back, out):
    gate_pre = product(rows[...], w_gate[...])
    up_pre = product(rows[...], w_up[...])
    grad_hidden = product(grads[...], w_down[...], ((1,), (1,)))
    sigmoid = 1.0 / (1.0 + jnp.exp(-gate_pre))
    silu = gate_pre * sigmoid
    hidden_low = (silu * up_pre).astype(jnp.bfloat16)
    gate_low = (grad_hidden * up_pre * (sigmoid + silu * (1.0 - sigmoid))).astype(jnp.bfloat16)
    up_low = (grad_hidden * silu).astype(jnp.bfloat16)
    hidden[...] = hidden_low
    grad_gate[...] = gate_low
    grad_up[...] = up_low
    back[...] = (
        product(gate_low, w_gate[...], ((1,), (1,))) + product(up_low, w_up[...], ((1,), (1,)))
    ).astype(jnp.bfloat16)
    out[...] = product(hidden_low, w_down[...]).astype(jnp.bfloat16)


def feed_forward(rows, grads, w_gate, w_up, w_down):
    count, width = rows.shape
    hidden = w_gate.shape[1]
    step = edge_rows
    wide = pl.BlockSpec((step, width), lambda i: (i, 0))
    inner = pl.BlockSpec((step, hidden), lambda i: (i, 0))
    return pl.pallas_call(
        ffn_kernel,
        grid=(count // step,),
        in_specs=[
            wide, wide, whole_spec(w_gate.shape), whole_spec(w_up.shape), whole_spec(w_down.shape),
        ],
        out_specs=[inner] * 3 + [wide] * 2,
        out_shape=[struct((count, hidden), jnp.bfloat16)] * 3
        + [struct((count, width), jnp.bfloat16)] * 2,
        compiler_params=params(),
        cost_estimate=costs(12 * count * width * hidden, 6 * width * hidden + 8 * count * width, count * hidden),
    )(rows, grads, w_gate, w_up, w_down)


def input_kernel(ids, tokens, grad_qkv, w_query, w_key, w_value, result, sums):
    clips = sums.shape[0]
    total = None
    for part, weight in enumerate((w_query, w_key, w_value)):
        term = lax.dot_general(
            grad_qkv[part], weight[...], (((0,), (1,)), ((), ())), preferred_element_type=jnp.float32
        )
        total = term if total is None else total + term
    result[...] = total.astype(jnp.bfloat16)
    inputs = tokens[...].astype(jnp.float32)
    found = sums_by_clip(total * (inputs * rms_scale(inputs)), ids[...], clips)

    @pl.when(pl.program_id(0) == 0)
    def _():
        sums[...] = found

    @pl.when(pl.program_id(0) > 0)
    def _():
        sums[...] += found


def input_rows(ids, tokens_all, grad_qkv, w_query, w_key, w_value, clips):
    rows, width = tokens_all.shape
    cols = w_query.shape[1]
    step = edge_rows
    return pl.pallas_call(
        input_kernel,
        grid=(rows // step,),
        in_specs=[
            pl.BlockSpec((step, 1), lambda i: (i, 0)), pl.BlockSpec((step, width), lambda i: (i, 0)),
            pl.BlockSpec((3, cols, step), lambda i: (0, 0, i)),
            whole_spec((width, cols)), whole_spec((width, cols)), whole_spec((width, cols)),
        ],
        out_specs=[pl.BlockSpec((step, width), lambda i: (i, 0)), whole_spec((clips, width))],
        out_shape=[struct((rows, width), jnp.bfloat16), struct((clips, width))],
        compiler_params=params(),
        cost_estimate=costs(6 * rows * width * cols, rows * width * 4 + 6 * cols * (width + rows)),
    )(ids, tokens_all, grad_qkv, w_query, w_key, w_value)


def block_kernel(cuts, rank, mod, ids, middle, out_grad, *refs):
    block_out, sums = refs[cuts:]
    where_clip = ids[...]
    ffn_out = jnp.concatenate([ref[...] for ref in refs[:cuts]], axis=0).astype(jnp.float32)
    gate = by_clip(jnp.tanh(modulation_rows(mod, rank[0], 3)), where_clip)
    block_out[...] = (middle[...] + gate * ffn_out).astype(jnp.bfloat16)
    sums[...] = sums_by_clip(out_grad[...].astype(jnp.float32) * ffn_out, where_clip, mod.shape[1])


def block_result(rank, mod, ids, middle, out_grad, pieces):
    vmem = pl.BlockSpec(memory_space=pltpu.VMEM)
    return pl.pallas_call(
        functools.partial(block_kernel, len(pieces)),
        in_specs=[smem_spec] + [vmem] * (4 + len(pieces)),
        out_shape=[struct(middle.shape, jnp.bfloat16), struct((mod.shape[1], middle.shape[1]))],
        compiler_params=params(),
        cost_estimate=costs(middle.size * 8, middle.size * 10),
    )(rank, mod, ids, middle, out_grad, *pieces)


def last_kernel(rank, mod, ids, gain, tokens, grad_middle, grads, result):
    inputs = tokens[...].astype(jnp.float32)
    inverse = rms_scale(inputs)
    scaled = by_clip(gain[...] * (1.0 + modulation_rows(mod, rank[0], 0)), ids[...])
    result[...] = grad_middle[...] + rms_backward(
        grads[...].astype(jnp.float32) * scaled, inputs * inverse, inverse
    )


def input_result(rank, mod, ids, gain, tokens, grad_middle, grads):
    vmem = pl.BlockSpec(memory_space=pltpu.VMEM)
    return pl.pallas_call(
        last_kernel,
        in_specs=[smem_spec] + [vmem] * 6,
        out_shape=struct(tokens.shape),
        compiler_params=params(),
        cost_estimate=costs(tokens.size * 12, tokens.size * 12),
    )(rank, mod, ids, gain, tokens, grad_middle, grads)


def weight_kernel(lefts, rights, block, mine, *refs):
    left = refs[: len(lefts)]
    right = refs[len(lefts) : len(lefts) + sum(rights)]
    given, kept, left_turned, whole = refs[-4:]
    step = pl.program_id(0)

    @pl.when(step == 0)
    def _():
        at = 0
        for ref, relative in zip(left, lefts):
            if relative:
                count = ref.shape[0]
                places = [lax.rem(mine[1] + m, count) for m in range(count)]
                values = jnp.concatenate([ref[place, 0] for place in places], axis=0)
            else:
                values = ref[...]
                values = values.reshape(-1, values.shape[-1])
            left_turned[:, at : at + values.shape[0]] = values.T
            at += values.shape[0]

    tiles = pl.num_programs(0) // len(rights)
    first = 0
    for share, count in enumerate(rights):
        chosen = right[first : first + count]
        first += count

        @pl.when(step // tiles == share)
        def _(chosen=chosen):
            at = 0
            result = None
            for ref in chosen:
                values = ref[...]
                term = product(left_turned[:, at : at + values.shape[0]], values)
                result = term if result is None else result + term
                at += values.shape[0]
            whole[...] = result.astype(jnp.bfloat16)

    for pair in range(given.shape[0]):
        for ref, side in ((given, 1 - mine[0]), (kept, mine[0])):
            start = pl.multiple_of((2 * pair + side) * block, 16)
            ref[pair] = whole[pl.ds(start, block)]


def weight_gradient(lefts, left_specs, relative, rights, depth, width, columns, tile, place, before):
    count = lax.axis_size("dp")
    mine = jnp.stack([lax.axis_index("dp") & 1, lax.axis_index("tensor")])
    block = width // count
    tiles = rights[0][0].shape[1] // tile
    out_spec = pl.BlockSpec((count // 2, block, tile), lambda i: (0, 0, place(i)))
    right_specs = [
        pl.BlockSpec(
            (ref.shape[0], tile), lambda i, share=share: (0, jnp.clip(i - share * tiles, 0, tiles - 1))
        )
        for share, refs in enumerate(rights)
        for ref in refs
    ]
    operands = [mine, *lefts, *sum(rights, []), *before]
    first = len(operands) - len(before)
    return pl.pallas_call(
        functools.partial(weight_kernel, relative, [len(refs) for refs in rights], block),
        grid=(tiles * len(rights),),
        in_specs=[smem_spec]
        + left_specs
        + right_specs
        + [pl.BlockSpec(memory_space=pl.ANY)] * len(before),
        out_specs=[out_spec] * 2,
        out_shape=[struct((count // 2, block, columns), jnp.bfloat16)] * 2,
        scratch_shapes=[pltpu.VMEM((width, depth), jnp.bfloat16), pltpu.VMEM((width, tile), jnp.bfloat16)],
        input_output_aliases={first + k: k for k in range(len(before))},
        compiler_params=params(),
        cost_estimate=costs(2 * depth * width * columns, 2 * (depth + columns) * (width + depth)),
    )(*operands)


def text_kernel(places, grads, first, second, out):
    half = grads.shape[1]
    out[0] = product(grads[0], first[...]).astype(jnp.bfloat16)
    out[1] = product(grads[1], second[...]).astype(jnp.bfloat16)


def text_gradient(grads, text_flat, side):
    count = lax.axis_size("dp")
    mine = lax.axis_index("dp")
    bits = count.bit_length() - 1
    length = text_flat.shape[1] // count
    half = count // 2
    places = []
    for order in bit_orders():
        for place in range(half):
            j = side + sum(
                1 << bit for at, bit in enumerate(order[1:]) if (place >> (bits - 2 - at)) & 1
            )
            places.append(mine ^ j)
    places = jnp.stack(places)
    cols = grads.shape[1]
    rows = text_flat.shape[0]
    return pl.pallas_call(
        text_kernel,
        grid_spec=pltpu.PrefetchScalarGridSpec(
            num_scalar_prefetch=1,
            grid=(half,),
            in_specs=[
                pl.BlockSpec(grads.shape, lambda i, at: (0, 0, 0)),
                pl.BlockSpec((rows, length), lambda i, at: (0, at[i])),
                pl.BlockSpec((rows, length), lambda i, at: (0, at[half + i])),
            ],
            out_specs=pl.BlockSpec((2, cols, length), lambda i, at: (0, 0, i)),
        ),
        out_shape=struct((2, cols, half * length), jnp.bfloat16),
        compiler_params=params(),
        cost_estimate=costs(4 * cols * rows * half * length, 4 * rows * half * length),
    )(places, grads, text_flat, text_flat)


def attend_forward(
    clips, slots, ranks, gates, query, key, value, text_key, text_value, table, text_table, cosine, sine,
    query_gain, key_gain, mixed, self_out, cross_out, self_inverse, cross_inverse,
):
    head_dim, rows = query.shape
    scale = math.log2(math.e) / math.sqrt(head_dim)
    gate = gates[pl.program_id(0)]
    raw = query[...]
    query_rot = turn(raw * head_norm(raw) * query_gain[...], cosine[...], sine[...])
    query_wide = widen(query_rot, table[0]).astype(jnp.bfloat16)
    raw = key[...]
    key_rot = turn(raw * head_norm(raw) * key_gain[...], cosine[...], sine[...])
    key_wide = widen(key_rot, table[1]).T.astype(jnp.bfloat16)
    raw = text_key[...]
    text_wide = widen(raw * head_norm(raw) * key_gain[...], text_table[...]).T.astype(jnp.bfloat16)
    ones_row = (lax.broadcasted_iota(jnp.int32, (16, rows), 0) == 0).astype(jnp.float32)
    value_wide = jnp.concatenate([value[...], ones_row], axis=0).astype(jnp.bfloat16)
    text_value_wide = jnp.concatenate(
        [text_value[...], ones_row[:, : text_value.shape[1]]], axis=0
    ).astype(jnp.bfloat16)
    blocks = rows // edge_rows
    for block in range(blocks):
        cols = slice(block * edge_rows, (block + 1) * edge_rows)
        query_blk = query_wide[:, cols]
        weights = jnp.exp2(product(key_wide, query_blk) * scale).astype(jnp.bfloat16)
        total = product(value_wide, weights)
        inverse = 1.0 / total[head_dim : head_dim + 1]
        own = total[:head_dim] * inverse
        first, last = text_range(block, blocks, clips, slots)
        weights = jnp.exp2(product(text_wide[first:last], query_blk) * scale).astype(jnp.bfloat16)
        total = product(text_value_wide[:, first:last], weights)
        text_inverse = 1.0 / total[head_dim : head_dim + 1]
        other = total[:head_dim] * text_inverse
        pieces = mixed.shape[0]
        mixed[lax.rem(block - ranks[0] + pieces, pieces)] = (own + gate * other).astype(jnp.bfloat16)
        self_out[:, cols] = own
        cross_out[:, cols] = other
        self_inverse[0, :, cols] = inverse
        cross_inverse[0, :, cols] = text_inverse


def through_norm(incoming, raw, inverse, gain):
    normed = raw * inverse
    scaled = incoming * gain
    mean = jnp.mean(scaled * normed, axis=0, keepdims=True)
    gain_part = jnp.sum(incoming * normed, axis=1, keepdims=True)
    return inverse * (scaled - normed * mean), gain_part


def rank_pieces(ranks, grads, held):
    count = len(grads)
    for m, ref in enumerate(grads):
        held[m] = ref[...].astype(jnp.float32)
    return jnp.concatenate(
        [held[lax.rem(piece - ranks[0] + count, count)] for piece in range(count)], axis=1
    )


def with_dots(weighted, out):
    rows = out.shape[1]
    low = weighted.astype(jnp.bfloat16)
    dots = jnp.sum(low.astype(jnp.float32) * out, axis=0, keepdims=True)
    high = dots.astype(jnp.bfloat16).astype(jnp.float32)
    rows_at = lax.broadcasted_iota(jnp.int32, (16, rows), 0)
    extra = jnp.where(rows_at == 0, -high, jnp.where(rows_at == 1, high - dots, 0.0))
    return widen(low.astype(jnp.float32), extra).astype(jnp.bfloat16)


def two_ones(rows):
    return (lax.broadcasted_iota(jnp.int32, (16, rows), 0) < 2).astype(jnp.float32)


def cross_backward(
    clips, slots, count, ranks, gates, query, text_key, text_value, table, text_table, cosine, sine,
    query_gain, key_gain, cross_out, cross_inverse, *refs,
):
    grad_pieces = refs[:count]
    grad_text, grad_query, gain_sums, held, text_key_sum, text_value_sum = refs[count:]
    head_dim, rows = query.shape
    scale = math.log2(math.e) / math.sqrt(head_dim)
    factor = 1.0 / math.sqrt(head_dim)
    gate = gates[pl.program_id(0)]
    raw = query[...]
    query_rot = turn(raw * head_norm(raw) * query_gain[...], cosine[...], sine[...])
    query_wide = widen(query_rot, table[0]).astype(jnp.bfloat16)
    raw = text_key[...]
    text_inv = head_norm(raw)
    text_norm = raw * text_inv * key_gain[...]
    text_low = text_norm.astype(jnp.bfloat16)
    text_wide = widen(text_norm, text_table[...]).T.astype(jnp.bfloat16)
    text_value_wide = widen(text_value[...], two_ones(text_value.shape[1])).T.astype(jnp.bfloat16)
    grads = rank_pieces(ranks, grad_pieces, held)
    cross_wide = with_dots(grads * (gate * cross_inverse[0]), cross_out[...])
    blocks = rows // edge_rows
    text_key_sum[...] = jnp.zeros_like(text_key_sum)
    text_value_sum[...] = jnp.zeros_like(text_value_sum)
    for block in range(blocks):
        cols = slice(block * edge_rows, (block + 1) * edge_rows)
        query_blk = query_wide[:, cols]
        first, last = text_range(block, blocks, clips, slots)
        grad_blk = cross_wide[:, cols]
        weights = jnp.exp2(product(text_wide[first:last], query_blk) * scale)
        slopes = (weights * product(text_value_wide[first:last], grad_blk)).astype(jnp.bfloat16)
        text_value_sum[:, first:last] += product(
            grad_blk[:head_dim], weights.astype(jnp.bfloat16), ((1,), (1,))
        )
        text_key_sum[:, first:last] += product(query_blk[:head_dim], slopes, ((1,), (1,)))
        grad_query[:, cols] = product(text_low[:, first:last], slopes)
    result, text_part = through_norm(
        text_key_sum[...] * factor, text_key[...], text_inv, key_gain[...]
    )
    grad_text[0] = result.astype(jnp.bfloat16)
    grad_text[1] = text_value_sum[...].astype(jnp.bfloat16)
    gate_part = jnp.sum(grads * cross_out[...], axis=1, keepdims=True)
    lane = lax.broadcasted_iota(jnp.int32, (head_dim, 128), 1)
    gain_sums[0] = jnp.where(lane == 0, text_part, gate_part)


def self_backward(
    count, ranks, query, key, value, table, cosine, sine, query_gain, key_gain,
    self_out, self_inverse, grad_query, *refs,
):
    grad_pieces = refs[:count]
    grad_qkv, gain_sums, held, grad_key_sum, grad_value_sum, grad_query_all = refs[count:]
    head_dim, rows = query.shape
    scale = math.log2(math.e) / math.sqrt(head_dim)
    factor = 1.0 / math.sqrt(head_dim)
    raw = query[...]
    query_inv = head_norm(raw)
    query_rot = turn(raw * query_inv * query_gain[...], cosine[...], sine[...])
    query_wide = widen(query_rot, table[0]).astype(jnp.bfloat16)
    raw = key[...]
    key_inv = head_norm(raw)
    key_rot = turn(raw * key_inv * key_gain[...], cosine[...], sine[...])
    key_low = key_rot.astype(jnp.bfloat16)
    key_wide = widen(key_rot, table[1]).T.astype(jnp.bfloat16)
    value_wide = widen(value[...], two_ones(rows)).T.astype(jnp.bfloat16)
    self_wide = with_dots(
        rank_pieces(ranks, grad_pieces, held) * self_inverse[0], self_out[...]
    )
    for block in range(rows // edge_rows):
        cols = slice(block * edge_rows, (block + 1) * edge_rows)
        query_blk = query_wide[:, cols]
        grad_blk = self_wide[:, cols]
        weights = jnp.exp2(product(key_wide, query_blk) * scale)
        slopes = (weights * product(value_wide, grad_blk)).astype(jnp.bfloat16)
        value_term = product(grad_blk[:head_dim], weights.astype(jnp.bfloat16), ((1,), (1,)))
        key_term = product(query_blk[:head_dim], slopes, ((1,), (1,)))
        if block == 0:
            grad_value_sum[...] = value_term
            grad_key_sum[...] = key_term
        else:
            grad_value_sum[...] += value_term
            grad_key_sum[...] += key_term
        grad_query_all[:, cols] = grad_query[:, cols] + product(key_low, slopes)

    incoming = turn_back(grad_query_all[...] * factor, cosine[...], sine[...])
    result, query_part = through_norm(incoming, query[...], query_inv, query_gain[...])
    grad_qkv[0] = result.astype(jnp.bfloat16)
    incoming = turn_back(grad_key_sum[...] * factor, cosine[...], sine[...])
    result, key_part = through_norm(incoming, key[...], key_inv, key_gain[...])
    grad_qkv[1] = result.astype(jnp.bfloat16)
    grad_qkv[2] = grad_value_sum[...].astype(jnp.bfloat16)
    lane = lax.broadcasted_iota(jnp.int32, (head_dim, 128), 1)
    gain_sums[0] = jnp.where(lane == 0, query_part, key_part)


def attention_specs(heads, head_dim, rows, text_rows):
    def head_block(part, width):
        return pl.BlockSpec((head_dim, width), lambda h, part=part: (part * heads + h, 0))

    return [
        smem_spec, smem_spec,
        head_block(0, rows), head_block(1, rows), head_block(2, rows),
        head_block(0, text_rows), head_block(0, text_rows),
        whole_spec((2, 16, rows)), whole_spec((16, text_rows)),
        whole_spec((head_dim // 2, rows)), whole_spec((head_dim // 2, rows)),
        whole_spec((head_dim, 1)), whole_spec((head_dim, 1)),
    ]


def attention_forward(shared, heads, head_dim, clips, ranks):
    qkv, text = shared[2], shared[5]
    rows = qkv.shape[1]
    text_rows = text.shape[1]
    cols = heads * head_dim
    hb = pl.BlockSpec((head_dim, rows), lambda h: (h, 0))
    stat = pl.BlockSpec((1, 1, rows), lambda h: (h, 0, 0))
    return pl.pallas_call(
        functools.partial(attend_forward, clips, text_rows // clips),
        grid=(heads,),
        in_specs=attention_specs(heads, head_dim, rows, text_rows),
        out_specs=[
            pl.BlockSpec((ranks, head_dim, rows // ranks), lambda h: (0, h, 0)), hb, hb, stat, stat,
        ],
        out_shape=[struct((ranks, cols, rows // ranks), jnp.bfloat16)]
        + [struct((cols, rows))] * 2
        + [struct((heads, 1, rows))] * 2,
        compiler_params=params(),
        cost_estimate=costs(8 * cols * rows * rows, cols * rows * 24, heads * rows * rows),
    )(*shared)


def attention_backward(shared, grads, kept, heads, head_dim, clips, between):
    (rank, gates, qkv, _, _, text_key, text_value, table, text_table, cosine, sine, query_gain,
     key_gain) = shared
    self_out, cross_out, self_inverse, cross_inverse = kept
    rows = qkv.shape[1]
    text_rows = text_key.shape[1]
    cols = heads * head_dim
    count = len(grads)
    (smem, _, query_s, key_s, value_s, text_key_s, text_value_s, table_s, text_table_s, cos_s,
     sin_s, query_gain_s, key_gain_s) = attention_specs(heads, head_dim, rows, text_rows)
    hb = pl.BlockSpec((head_dim, rows), lambda h: (h, 0))
    stat = pl.BlockSpec((1, 1, rows), lambda h: (h, 0, 0))
    sums = pl.BlockSpec((1, head_dim, 128), lambda h: (h, 0, 0))
    grad_specs = [pl.BlockSpec((head_dim, rows // count), lambda h: (h, 0))] * count
    held = pltpu.VMEM((count, head_dim, rows // count), jnp.float32)
    grad_text, grad_query, cross_sums = pl.pallas_call(
        functools.partial(cross_backward, clips, text_rows // clips, count),
        grid=(heads,),
        in_specs=[
            smem, smem, query_s, text_key_s, text_value_s, table_s, text_table_s, cos_s, sin_s,
            query_gain_s, key_gain_s, hb, stat, *grad_specs,
        ],
        out_specs=[pl.BlockSpec((2, head_dim, text_rows), lambda h: (0, h, 0)), hb, sums],
        out_shape=[
            struct((2, cols, text_rows), jnp.bfloat16), struct((cols, rows)),
            struct((heads, head_dim, 128)),
        ],
        scratch_shapes=[held] + [pltpu.VMEM((head_dim, text_rows), jnp.float32)] * 2,
        compiler_params=params(),
        cost_estimate=costs(6 * cols * rows * text_rows, cols * rows * 14, heads * rows * text_rows // 2),
    )(rank, gates, qkv, text_key, text_value, table, text_table, cosine, sine, query_gain, key_gain,
      cross_out, cross_inverse, *grads)
    grad_query, passed = between(grad_query, grad_text)
    grad_qkv, self_sums = pl.pallas_call(
        functools.partial(self_backward, count),
        grid=(heads,),
        in_specs=[
            smem, query_s, key_s, value_s, table_s, cos_s, sin_s, query_gain_s, key_gain_s,
            hb, stat, hb, *grad_specs,
        ],
        out_specs=[pl.BlockSpec((3, head_dim, rows), lambda h: (0, h, 0)), sums],
        out_shape=[struct((3, cols, rows), jnp.bfloat16), struct((heads, head_dim, 128))],
        scratch_shapes=[held] + [pltpu.VMEM((head_dim, rows), jnp.float32)] * 3,
        compiler_params=params(),
        cost_estimate=costs(20 * cols * rows * rows, cols * rows * 24, heads * rows * rows),
    )(rank, qkv, qkv, qkv, table, cosine, sine, query_gain, key_gain, self_out, self_inverse,
      grad_query, *grads)
    return grad_qkv, grad_text, cross_sums, self_sums, passed


def clip_tables(clip_ids, text_lengths, clips, slots):
    rows = clip_ids.shape[0]
    feature = jnp.arange(16, dtype=jnp.int32)[:, None]
    member = feature == clip_ids[None, :]
    query_part = jnp.where(feature < clips, jnp.where(member, 0.0, -apart), jnp.where(feature == clips, -apart, 0.0))
    key_part = member.astype(jnp.float32)
    owner = jnp.repeat(jnp.arange(clips, dtype=jnp.int32), slots)
    slot = jnp.tile(jnp.arange(slots, dtype=jnp.int32), clips)
    dead = slot >= jnp.repeat(text_lengths, slots)
    text_part = jnp.where(feature == clips, dead[None, :], feature == owner[None, :]).astype(jnp.float32)
    return jnp.stack([query_part, key_part]), text_part


def rotary_tables(positions, head_dim):
    half = head_dim // 2
    frequency = jnp.exp(-math.log(10000.0) * jnp.arange(half, dtype=jnp.float32) * 2.0 / head_dim)
    angles = frequency[:, None] * positions.astype(jnp.float32)[None, :]
    return jnp.cos(angles), jnp.sin(angles)


def sum_kernel(jobs, mine, *refs):
    at = 0
    outs = refs[sum(count for count, _ in jobs) :]
    for (count, turned), out in zip(jobs, outs):
        value = total([ref[0] for ref in refs[at : at + count]])
        value = value.T if turned else value
        if len(out.shape) == 3:
            out[0] = value.astype(out.dtype)
        else:
            out[...] = value.astype(out.dtype)
        at += count


def sum_stage(jobs, steps):
    mine = lax.axis_index("dp")[None]
    terms = [term for job in jobs for term, _ in job[0]]
    return pl.pallas_call(
        functools.partial(sum_kernel, [(len(job[0]), job[3]) for job in jobs]),
        grid_spec=pltpu.PrefetchScalarGridSpec(
            num_scalar_prefetch=1,
            grid=(steps,),
            in_specs=[spec for job in jobs for _, spec in job[0]],
            out_specs=[job[2] for job in jobs],
        ),
        out_shape=[job[1] for job in jobs],
        compiler_params=params(),
        cost_estimate=costs(0, 0),
    )(mine, *terms)


class Scatter:
    def __init__(self, kept, taken, order, column, columns, turned=False):
        bits = lax.axis_size("dp").bit_length() - 1
        self.every = list(range(bits - 1, 0, -1))
        self.order = list(order)
        self.done = []
        self.terms = [(term, self.every, column) for term in (kept, taken)]
        self.rows, self.columns, self.turned = kept.shape[1], columns, turned

    def last_job(self, width, first, moving, turned):
        offset = self.columns // width

        def spec(held, column):
            def place(i, mine):
                at = 0
                for bit in held:
                    at = at * 2 + ((mine[0] >> bit) & 1)
                return at, 0, column * offset + first + (i if moving else 0)

            return pl.BlockSpec((1, self.rows, width), place)

        terms = [(term, spec(held, column)) for term, held, column in self.terms]
        shape = (self.rows, width * (2 if moving else 1))
        block = (self.rows, width)
        if turned:
            shape, block = shape[::-1], block[::-1]
        out_spec = pl.BlockSpec(block, lambda i, mine: (0, i if moving else 0))
        return terms, struct(shape), out_spec, turned

    def job(self):
        current = self.order[len(self.done)] if len(self.done) < len(self.order) else None
        done = list(self.done)

        def spec(held, column):
            left = [bit for bit in held if bit not in done and bit != current]

            def place(i, mine):
                at = 0
                for bit in held:
                    own = (mine[0] >> bit) & 1
                    if bit in done:
                        side = own
                    elif bit == current:
                        side = 1 - own
                    else:
                        side = (i >> (len(left) - 1 - left.index(bit))) & 1
                    at = at * 2 + side
                return at, 0, column

            return pl.BlockSpec((1, self.rows, self.columns), place)

        terms = [(term, spec(held, column)) for term, held, column in self.terms]
        shape = (self.rows, self.columns)
        if current is None:
            shape = shape[::-1] if self.turned else shape
            return terms, struct(shape), pl.BlockSpec(shape, lambda i, mine: (0, 0)), self.turned
        count = 2 ** (len(self.every) - len(done) - 1)
        out_spec = pl.BlockSpec((1, *shape), lambda i, mine: (i, 0, 0))
        return terms, struct((count, *shape), jnp.bfloat16), out_spec, False

    def steps(self):
        return max(1, 2 ** (len(self.every) - len(self.done) - 1))

    def send(self, given):
        bit = self.order[len(self.done)]
        arrived = exchange(given, "dp", 1 << bit)
        self.done.append(bit)
        self.terms.append((arrived, [b for b in self.every if b not in self.done], 0))


class TextScatter:
    def __init__(self, kept, taken, part):
        self.order = bit_orders()[part][1:]
        self.done = []
        self.terms = [(kept, part), (taken, part)]
        self.length = kept.shape[2]

    def job(self):
        cols = self.terms[0][0].shape[1]
        last = len(self.done) == len(self.order)
        width = self.length if last else self.length // 2

        def spec(part):
            return pl.BlockSpec((1, cols, width), lambda i, mine: (part, 0, 0 if last else 1))

        terms = [(term, spec(part)) for term, part in self.terms]
        if last:
            shape = (width, cols)
            return terms, struct(shape), pl.BlockSpec(shape, lambda i, mine: (0, 0)), True
        out_spec = pl.BlockSpec((1, cols, width), lambda i, mine: (0, 0, 0))
        return terms, struct((1, cols, width), jnp.bfloat16), out_spec, False

    def steps(self):
        return 1

    def send(self, given):
        arrived = exchange(given, "dp", 1 << self.order[len(self.done)])
        self.done.append(self.order[len(self.done)])
        self.terms.append((arrived, 0))
        self.length //= 2


def next_sums(scatters):
    results = [None] * len(scatters)
    for steps in sorted({scatter.steps() for scatter in scatters}):
        chosen = [i for i, scatter in enumerate(scatters) if scatter.steps() == steps]
        for i, result in zip(chosen, sum_stage([scatters[i].job() for i in chosen], steps)):
            results[i] = result
    return results


def send_all(scatters, given):
    for scatter, values in zip(scatters, given):
        scatter.send(values)


def bit_orders():
    bits = lax.axis_size("dp").bit_length() - 1
    return [list(range(bits)), [0] + list(range(bits - 1, 0, -1))]


def shift_ranks(pieces):
    count = lax.axis_size("tensor")
    arrived = [pieces[0]] + [None] * (count - 1)
    for m in range(1, count):
        arrived[count - m] = lax.ppermute(
            pieces[m], "tensor", [(i, (i + m) % count) for i in range(count)]
        )
    return arrived


def in_rank_order(relative):
    count = relative.shape[0]
    start = (count - lax.axis_index("tensor")) % count
    return lax.dynamic_slice_in_dim(jnp.concatenate([relative, relative], axis=0), start, count, 0)


def scatter_rows(values):
    return lax.psum_scatter(values, "tensor", scatter_dimension=0, tiled=True)


def after(values, *others):
    return lax.optimization_barrier((values, *others))[0]


def after_all(values, *others):
    return lax.optimization_barrier((values, others))[0]


def weight_gradient_plain(left, right):
    groups = lax.axis_size("dp")
    grads = right.reshape(-1, right.shape[-1])
    blocks = product(left, grads, ((0,), (1,))).astype(jnp.bfloat16)
    blocks = blocks.reshape(groups // 2, 2, -1, grads.shape[0])
    mine = lax.axis_index("dp") & 1
    return [
        lax.dynamic_index_in_dim(blocks, side, 1, keepdims=False) for side in (1 - mine, mine)
    ]


def on_device(
    tokens,
    clip_ids,
    positions,
    timesteps,
    text_states,
    text_lengths,
    out_grad,
    attn_gain,
    ffn_gain,
    query_gain,
    key_gain,
    cross_gate,
    w_query,
    w_key,
    w_value,
    w_out,
    w_text_key,
    w_text_value,
    w_ada,
    w_gate,
    w_up,
    w_down,
):
    tensor_size = lax.axis_size("tensor")
    my_rank = lax.axis_index("tensor")
    my_group = lax.axis_index("dp")
    groups = lax.axis_size("dp")
    bits = groups.bit_length() - 1
    rank = my_rank[None]
    local_rows, model_width = tokens.shape
    group_rows = local_rows * tensor_size
    head_dim = query_gain.shape[0]
    head_cols = w_query.shape[1]
    local_heads = head_cols // head_dim
    clip_count = timesteps.shape[0]
    text_len = text_states.shape[1]
    text_rows = clip_count * text_len
    hidden_cols = w_gate.shape[1]
    orders = [list(range(1, bits)), list(range(bits - 1, 0, -1))]

    tokens_all = lax.all_gather(tokens, "tensor", axis=0, tiled=True)
    embedded = time_embed(timesteps, w_ada.shape[0])
    condition = (embedded * jax.nn.sigmoid(embedded)).astype(jnp.bfloat16)
    mod_part = jnp.dot(condition, w_ada, preferred_element_type=jnp.float32)
    mod = jnp.stack(shift_ranks([mod_part] * tensor_size))
    share_rows = head_cols // groups
    share = lax.dynamic_slice_in_dim(w_out, my_group * share_rows, share_rows, 0)
    shares = jnp.stack(shift_ranks([share] * tensor_size))[None]
    shares = [shares, exchange(shares, "dp", groups // 2)]

    ids = clip_ids[:, None]
    my_ids = lax.dynamic_slice_in_dim(ids, my_rank * local_rows, local_rows)
    attn_gain_row, ffn_gain_row = attn_gain[None], ffn_gain[None]
    grad_ffn_low = gated_gradient(rank, mod, my_ids, out_grad)
    text_flat = text_states.reshape(text_rows, text_states.shape[2])
    text_key = product(w_text_key, text_flat, ((0,), (1,)))
    text_value = product(w_text_value, text_flat, ((0,), (1,)))
    gate_tanh = jnp.tanh(lax.dynamic_slice_in_dim(cross_gate, my_rank * local_heads, local_heads))
    table, text_table = clip_tables(clip_ids, text_lengths, clip_count, text_len)
    cosine, sine = rotary_tables(positions, head_dim)
    tokens_all = after(
        tokens_all, grad_ffn_low, text_key, text_value, table, text_table, cosine, sine
    )
    tokens_all, *shares = lax.optimization_barrier((tokens_all, *shares))
    shares = jnp.concatenate(shares)
    for bit in range(bits - 2, 0, -1):
        arrived = exchange(shares, "dp", 1 << bit)
        if bit > 1:
            shares = jnp.concatenate([shares, arrived])
    grad_ffn_all = lax.all_gather(grad_ffn_low, "tensor", axis=0, tiled=True)
    attn_all, qkv = project(rank, mod, ids, attn_gain_row, tokens_all, w_query, w_key, w_value)
    qkv = qkv.reshape(3 * head_cols, group_rows)
    shared = (
        rank, gate_tanh, qkv, qkv, qkv, text_key, text_value, table, text_table, cosine, sine,
        query_gain[:, None], key_gain[:, None],
    )
    mixed_heads, *kept = attention_forward(
        shared, local_heads, head_dim, clip_count, tensor_size
    )
    shares, arrived, mixed_heads = lax.optimization_barrier((shares, arrived, mixed_heads))
    shares = jnp.concatenate([shares, arrived])
    w_out_all = assemble(shares, exchange(shares, "dp", 1))
    w_out_all = w_out_all.reshape(tensor_size, head_cols, model_width)
    mixed_pieces = shift_ranks([mixed_heads[m] for m in range(tensor_size)])
    attn_out, middle, ffn_rows = middle_forward(
        rank, mod, my_ids, ffn_gain_row, tokens, w_out_all, mixed_pieces, 1
    )
    ffn_rows, grad_ffn_all = lax.optimization_barrier((ffn_rows, grad_ffn_all))
    ffn_all = lax.all_gather(ffn_rows, "tensor", axis=0, tiled=True)
    hidden, grad_gate, grad_up, back, ffn_part = feed_forward(
        ffn_all, grad_ffn_all, w_gate, w_up, w_down
    )
    grad_ffn_rows = scatter_rows(back)
    tile = min(256, hidden_cols)
    tiles = hidden_cols // tile
    rows_spec = whole_spec((group_rows, model_width))
    ffn_given, ffn_held = weight_gradient(
        [grad_ffn_all], [rows_spec], [False], [[hidden]], group_rows, model_width, 3 * hidden_cols,
        tile, lambda i: jnp.where(i < tiles // 2, tiles + i, 2 * tiles + i), [],
    )
    ffn_given, ffn_held = weight_gradient(
        [ffn_all], [rows_spec], [False], [[grad_gate], [grad_up]],
        group_rows, model_width, 3 * hidden_cols, tile,
        lambda i: jnp.where(i < tiles, i, tiles // 2 + i), [ffn_given, ffn_held],
    )
    ffn_taken = exchange(ffn_given, "dp", 1)
    ffn_scatters = [
        Scatter(ffn_held, ffn_taken, orders[part], part, 3 * hidden_cols // 2) for part in range(2)
    ]
    ffn_next = next_sums(ffn_scatters)
    grad_ffn_rows, *late = lax.optimization_barrier((grad_ffn_rows, *ffn_next))
    send_all(ffn_scatters, ffn_next)
    rows_cuts = [[grad_ffn_rows]]

    grad_middle, grad_attn_low, scale_ffn_sums, gate_attn_sums, *grad_mixed = middle_backward(
        rank, mod, my_ids, ffn_gain_row, middle, attn_out, out_grad, w_out_all, rows_cuts
    )
    grad_heads = shift_ranks(grad_mixed)
    ffn_part = after(ffn_part.reshape(group_rows, model_width), *grad_heads)
    out_cuts = [scatter_rows(ffn_part)]
    mixed_all = jnp.stack(mixed_pieces)
    out_given, out_held = weight_gradient_plain(grad_attn_low, mixed_all)
    ffn_next = next_sums(ffn_scatters)
    grad_heads, out_given, out_held, *late = lax.optimization_barrier(
        (grad_heads, out_given, out_held, *ffn_next)
    )
    send_all(ffn_scatters, ffn_next)
    out_taken = exchange(out_given, "dp", 1)
    out_scatter = Scatter(out_held, out_taken, orders[1], 0, tensor_size * head_cols)

    def send_text(grad_query, grad_text):
        given = text_gradient(grad_text, text_flat, 1)
        (out_next,) = next_sums([out_scatter])
        grad_query, given, out_next = lax.optimization_barrier((grad_query, given, out_next))
        out_scatter.send(out_next)
        return grad_query, exchange(given, "dp", 1)

    grad_qkv, grad_text, cross_sums, self_sums, text_taken = attention_backward(
        shared, grad_heads, kept, local_heads, head_dim, clip_count, send_text
    )
    rows_part, scale_attn_sums = input_rows(
        ids, tokens_all, grad_qkv, w_query, w_key, w_value, clip_count
    )
    grad_attn_rows = scatter_rows(rows_part)
    grad_text = after(grad_text, rows_part)
    text_held = text_gradient(grad_text, text_flat, 0)
    text_scatters = [TextScatter(text_held, text_taken, part) for part in range(2)]
    text_next = next_sums(text_scatters)
    grad_qkv, *text_next = lax.optimization_barrier((grad_qkv, *text_next))
    send_all(text_scatters, text_next)
    qkv_given, qkv_held = weight_gradient_plain(attn_all, grad_qkv)
    scale_attn_sums, qkv_given, qkv_held = lax.optimization_barrier(
        (scale_attn_sums, qkv_given, qkv_held)
    )
    qkv_taken = exchange(qkv_given, "dp", 1)
    qkv_scatter = Scatter(qkv_held, qkv_taken, orders[1], 0, 3 * head_cols)
    (out_ready,) = lax.optimization_barrier((out_cuts[0], qkv_given))[:1]
    block_out, gate_ffn_sums = block_result(rank, mod, my_ids, middle, out_grad, [out_ready])

    modulation = in_rank_order(mod)
    modulation = modulation.transpose(1, 0, 2).reshape(clip_count, 4, model_width)
    scale_attn, gate_attn = modulation[:, 0], jnp.tanh(modulation[:, 1])
    scale_ffn, gate_ffn = modulation[:, 2], jnp.tanh(modulation[:, 3])
    clip_mod_grad = jnp.concatenate(
        [
            scale_attn_sums * attn_gain, gate_attn_sums * (1.0 - gate_attn * gate_attn),
            scale_ffn_sums * ffn_gain, gate_ffn_sums * (1.0 - gate_ffn * gate_ffn),
        ],
        axis=1,
    )
    small_parts = (
        jnp.sum(scale_attn_sums * (1.0 + scale_attn), axis=0),
        jnp.sum(scale_ffn_sums * (1.0 + scale_ffn), axis=0),
        jnp.sum(self_sums[:, :, 0], axis=0),
        jnp.sum(self_sums[:, :, 1] + cross_sums[:, :, 0], axis=0),
        lax.dynamic_update_slice_in_dim(
            jnp.zeros((cross_gate.shape[0],), jnp.float32),
            jnp.sum(cross_sums[:, :, 1], axis=1) * (1.0 - gate_tanh * gate_tanh),
            my_rank * local_heads,
            0,
        ),
    )
    share_cols = mod_part.shape[1]
    small = jnp.concatenate(small_parts)
    small = jnp.pad(small, (0, -small.shape[0] % share_cols)).reshape(-1, share_cols)
    step_row = jnp.pad(timesteps.astype(jnp.float32), (0, share_cols - clip_count))[None]
    payloads = shift_ranks(
        [
            jnp.concatenate(
                [
                    lax.dynamic_slice_in_dim(
                        clip_mod_grad, (my_rank + m) % tensor_size * share_cols, share_cols, 1
                    ),
                    small,
                ]
            )
            for m in range(tensor_size)
        ]
    )
    (out_next,) = next_sums([out_scatter])
    qkv_next = next_sums([qkv_scatter])
    payloads, out_next, qkv_next = lax.optimization_barrier((payloads, out_next, qkv_next))
    out_scatter.send(out_next)
    send_all([qkv_scatter], qkv_next)
    summed = jnp.sum(in_rank_order(jnp.stack(payloads)), axis=0)
    mod_grad = summed[:clip_count].astype(jnp.bfloat16).astype(jnp.float32)
    mod_grad = jnp.concatenate([mod_grad, step_row])
    small = summed[clip_count:]
    small_rows = small.shape[0]
    text_next = next_sums(text_scatters)
    mod_grad, text_next = lax.optimization_barrier((mod_grad, text_next))
    send_all(text_scatters, text_next)
    for bit in range(bits):
        arrived = exchange(jnp.concatenate([small, mod_grad]), "dp", 1 << bit)
        if bit == 0:
            for _ in range(bits - 3):
                send_all(ffn_scatters, next_sums(ffn_scatters))
            ffn_terms = lax.optimization_barrier(
                ([scatter.terms[-1][0] for scatter in ffn_scatters], grad_attn_rows)
            )[0]
            for scatter, term in zip(ffn_scatters, ffn_terms):
                scatter.terms[-1] = (term, *scatter.terms[-1][1:])
            width = hidden_cols // 2
            gate_sum, up_sum, *down_sum = sum_stage(
                [
                    ffn_scatters[0].last_job(width, 0, True, False),
                    ffn_scatters[1].last_job(width, 0, True, False),
                    ffn_scatters[0].last_job(width, 2, False, True),
                    ffn_scatters[1].last_job(width, 2, False, True),
                ],
                2,
            )
            arrived, gate_sum, up_sum, down_sum = lax.optimization_barrier(
                (arrived, gate_sum, up_sum, down_sum)
            )
        if bit == 1:
            for _ in range(bits - 3):
                out_scatter.send(next_sums([out_scatter])[0])
            (out_rows,) = next_sums([out_scatter])
            qkv_next = next_sums([qkv_scatter])
            arrived, out_rows, qkv_next = lax.optimization_barrier((arrived, out_rows, qkv_next))
            send_all([qkv_scatter], qkv_next)
            out_pieces = shift_ranks(
                [
                    out_rows[:, m * head_cols : (m + 1) * head_cols].astype(jnp.bfloat16)
                    for m in range(tensor_size)
                ]
            )
        small = small + arrived[:small_rows]
        mod_grad = jnp.concatenate([mod_grad, arrived[small_rows:]])
    mod_grad = mod_grad.reshape(groups, clip_count + 1, share_cols)
    all_steps = mod_grad[:, clip_count, :clip_count].reshape(-1)
    mod_grad = mod_grad[:, :clip_count].reshape(-1, share_cols)
    cond_width = w_ada.shape[0]
    my_condition = time_columns(
        all_steps, my_group * (cond_width // groups), cond_width // groups, cond_width
    )
    finals = text_scatters + [qkv_scatter]
    for _ in range(bits - 3):
        send_all(finals, next_sums(finals))
    text_key_sum, text_value_sum, qkv_sum = next_sums(finals)
    out_sum = total(out_pieces).T
    down_sum = jnp.concatenate(down_sum, axis=0)
    qkv_sums = jnp.split(qkv_sum, 3, axis=1)
    ada_sum = product(my_condition, mod_grad.astype(jnp.bfloat16), ((0,), (0,)))
    small = small.reshape(-1)
    small_sums = []
    start = 0
    for part in small_parts:
        small_sums.append(small[start : start + part.shape[0]])
        start += part.shape[0]
    input_grad = input_result(
        rank, mod, my_ids, attn_gain_row, tokens, grad_middle, grad_attn_rows
    )
    return (
        block_out,
        input_grad,
        *small_sums,
        *qkv_sums,
        out_sum,
        text_key_sum,
        text_value_sum,
        ada_sum,
        gate_sum,
        up_sum,
        down_sum,
    )


def solution(mesh):
    return jax.shard_map(
        on_device,
        mesh=mesh,
        in_specs=(
            P(("dp", "tensor"), None),
            P("dp"),
            P("dp"),
            P("dp"),
            P("dp", None, None),
            P("dp"),
            P(("dp", "tensor"), None),
            P(),
            P(),
            P(),
            P(),
            P(),
            P(None, "tensor"),
            P(None, "tensor"),
            P(None, "tensor"),
            P("tensor", None),
            P(None, "tensor"),
            P(None, "tensor"),
            P(None, "tensor"),
            P(None, "tensor"),
            P(None, "tensor"),
            P("tensor", None),
        ),
        out_specs=(
            P(("dp", "tensor"), None),
            P(("dp", "tensor"), None),
            P(),
            P(),
            P(),
            P(),
            P(),
            P("dp", "tensor"),
            P("dp", "tensor"),
            P("dp", "tensor"),
            P("tensor", "dp"),
            P("dp", "tensor"),
            P("dp", "tensor"),
            P("dp", "tensor"),
            P("dp", "tensor"),
            P("dp", "tensor"),
            P("tensor", "dp"),
        ),
        check_vma=False,
    )
```

time: 760 us -> 540 us (0.71)
  Pallas kernels: 43.8 us -> 197 us
  waiting for transfers between devices: 364 us -> 211 us
  matrix products: 120 us -> 17.3 us
  local copies, waits for them, and re-layouts: 99.2 us -> 33.5 us
  other arithmetic: 55.7 us -> 10.1 us
  blocking collectives: 16.2 us -> 0 us
  starting transfers between devices: 38.4 us -> 46.4 us
    pallas_call x1 -> x26, Pallas kernels: 25.7 us -> 177 us  [the longest x11 34.6 us: sum_stage(): pl.pallas_call(functools.partial(sum_kernel, [(len(job[0]), job[3]) for j...]
    reduce_scatter x4 -> x3, waiting for transfers between devices: 134 us -> 19.2 us  [scatter_rows(): return lax.psum_scatter(values, 'tensor', scatter_dimension=0, tiled=True)]
    dot_general x11 -> x0, matrix products: 74 us -> none  [the longest x1 11.8 us: on_device(): pair_pre = jnp.dot(ffn_all, w_pair, preferred_element_type=jnp.float32)]
    all_gather x1, waiting for transfers between devices: 52.4 us -> 9.32 us  [on_device(): grad_ffn_all = lax.all_gather(grad_ffn_low, 'tensor', axis=0, tiled=True)]
    ppermute x3 -> x18, waiting for transfers between devices: 0.01 us -> 37.1 us  [shift_ranks(): lax.ppermute(pieces[m], 'tensor', [(i, (i + m) % count) for i in range(co...]
    ppermute x36 -> x22, waiting for transfers between devices: 78.1 us -> 42.1 us  [exchange(): lax.ppermute(values, axis_name, [(i, i ^ distance) for i in range(count)])]
    dynamic_slice x4 -> x3, local copies, waits for them, and re-layouts: 35.8 us -> 1.91 us  [the longest x1 1.09 us: on_device(): lax.dynamic_slice_in_dim(w_out, my_group * share_rows, share_rows, 0)]
    dot_general x9 -> x5, matrix products: 43.8 us -> 14.3 us  [product(): lax.dot_general(left, right, (contract, ((), ())), preferred_element_type...]
  transfers between devices with their start and end apart: 47 -> 46, of which waited for: 26 -> 16; matrix products, arithmetic and copies ran while one was open for 24% -> 9% of each run, Pallas kernels for 0% -> 31%
where the time goes in v2:
time: 540 us; the launch traced here: 531 us
  waiting for transfers between devices  211 us (39%)
  Pallas kernels  197 us (36%)
  starting transfers between devices  46.4 us (9%)
  local copies, waits for them, and re-layouts  33.5 us (6%)
  matrix products  17.3 us (3%)
  between operations  15.5 us (3%)
  other arithmetic  10.1 us (2%)
    all_gather x1, waiting for transfers between devices, on_device(): ffn_all = lax.all_gather(ffn_rows, 'tensor', axis=0, tiled=True)  65.1 us
    ppermute x22, waiting for transfers between devices, exchange(): lax.ppermute(values, axis_name, [(i, i ^ distance) for i in range(count)])  42.1 us
    all_gather x1, waiting for transfers between devices, on_device(): tokens_all = lax.all_gather(tokens, 'tensor', axis=0, tiled=True)  37.3 us
    ppermute x18, waiting for transfers between devices, shift_ranks(): lax.ppermute(pieces[m], 'tensor', [(i, (i + m) % count) for i in range(co...  37.1 us
    pallas_call x11, Pallas kernels, sum_stage(): pl.pallas_call(functools.partial(sum_kernel, [(len(job[0]), job[3]) for j...  34.6 us
    pallas_call x1, Pallas kernels, feed_forward(): pl.pallas_call(ffn_kernel, grid=(count // step,), in_specs=[wide, wide, w...  26.2 us
    ppermute x18, starting transfers between devices, shift_ranks(): lax.ppermute(pieces[m], 'tensor', [(i, (i + m) % count) for i in range(co...  25.7 us
    pallas_call x2, Pallas kernels, weight_gradient(): pl.pallas_call(functools.partial(weight_kernel, relative, [len(refs) for...  22.2 us
  transfers between devices with their start and end apart: 46, of which 16 were waited for; matrix products, arithmetic and copies ran while one was open for 9% of the time, Pallas kernels for 31%

profile of v2, /device:TPU:0, one launch (start us, length us, event | category | flops | bytes accessed | tf_op | source)
XLA Modules:
  0.0 530.8 jit_solution(3037001474154506283)
XLA Ops:
  33.4 4.5 collective-permute-done.1
  42.5 37.3 %all-gather.4.cloned.1.call-done.tokens = bf16[1024,1536]{1,0:T(8,128)(2,1)} async-done(((bf16[256,1536]{1,0:T(8,128)(2,1)}), bf16[1024,1536]{1,0:T(8,128)(2,1)}) %all-gather.4.cloned.1.call-update) | async-done | bytes 3145744 | tf_op jit(solution)/shard_map/all_gather | solution.py:1019
  85.2 10.9 %shard_map.342 = (bf16[1024,1536]{1,0:T(8,128)(2,1)}, f32[3,384,1024]{2,1,0:T(8,128)}) custom-call(s32[1]{0:T(128)} %bitcast.rank.ranks, f32[4,3,1536]{2,1,0:T(4,128)} %pad_maximum_fusion.5.mod, s32[1024,1]{1,0:T(8,128)} %copy.53.ids, f32[1,1536]{1,0:T(1,128)} %broadcast_in_dim.126.gain, bf16[1024,1536]{1,0:T(8,128)(2,1)} %all-gather.4.cloned.1.call-done.tokens, ...), custom_call_target="tpu_custom_call" | custom-call | flops 56623104 | bytes 227328 | tf_op jit(solution)/shard_map/pallas_call | solution.py:160
  96.1 19.5 %shard_map.343 = (bf16[4,384,256]{2,1,0:T(8,128)(2,1)}, f32[384,1024]{1,0:T(8,128)}, f32[384,1024]{1,0:T(8,128)}, f32[6,1,1024]{2,1,0:T(1,128)}, f32[6,1,1024]{2,1,0:T(1,128)}) custom-call(s32[1]{0:T(128)} %bitcast.rank.ranks, f32[6]{0:T(128)} %dynamic-slice_tanh_fusion.gates, f32[1152,1024]{1,0:T(8,128)} %bitcast.117, f32[1152,1024]{1,0:T(8,128)} %bitcast.118, ...), custom_call_target="tpu_custom_call" | custom-call | flops 50331648 | bytes 147456 | tf_op jit(solution)/shard_map/pallas_call | solution.py:703
  125.6 5.0 shard_map.344
  132.9 13.7 %collective-permute-done.10.refs_2_ = bf16[384,256]{1,0:T(8,128)(2,1)S(1)} collective-permute-done((bf16[384,256]{1,0:T(8,128)(2,1)S(1)}, bf16[384,256]{1,0:T(8,128)(2,1)S(1)}, u32[]{:S(2)}, u32[]{:S(2)}) %collective-permute-start.10) | collective-permute-done | bytes 196640 | tf_op jit(solution)/shard_map/ppermute | solution.py:943
  147.4 6.7 %shard_map.345 = (f32[256,1536]{1,0:T(8,128)}, f32[256,1536]{1,0:T(8,128)}, bf16[256,1536]{1,0:T(8,128)(2,1)}) custom-call(s32[1]{0:T(128)} %bitcast.rank.ranks, f32[4,3,1536]{2,1,0:T(4,128)} %pad_maximum_fusion.5.mod, s32[256,1]{1,0:T(8,128)} %copy.67.ids, f32[1,1536]{1,0:T(1,128)} %broadcast_in_dim.112.gain, bf16[256,1536]{1,0:T(8,128)(2,1)} %tokens.3, ...), custom_call_target="tpu_custom_call" | custom-call | flops 18874368 | bytes 159744 | tf_op jit(solution)/shard_map/pallas_call | solution.py:227
  154.1 9.3 %all-gather.6.cloned.1.call-done.grads.refs_0_ = bf16[1024,1536]{1,0:T(8,128)(2,1)} async-done(((bf16[256,1536]{1,0:T(8,128)(2,1)}), bf16[1024,1536]{1,0:T(8,128)(2,1)}) %all-gather.6.cloned.1.call-update) | async-done | bytes 3145744 | tf_op jit(solution)/shard_map/all_gather | solution.py:1048
  163.5 65.1 %all-gather.8.cloned.1.call-done.rows.refs_0_ = bf16[1024,1536]{1,0:T(8,128)(2,1)} async-done(((bf16[256,1536]{1,0:T(8,128)(2,1)}), bf16[1024,1536]{1,0:T(8,128)(2,1)}) %all-gather.8.cloned.1.call-update) | async-done | bytes 3145744 | tf_op jit(solution)/shard_map/all_gather | solution.py:1067
  228.5 26.2 %shard_map.346 = (bf16[1024,1024]{1,0:T(8,128)(2,1)}, bf16[1024,1024]{1,0:T(8,128)(2,1)}, bf16[1024,1024]{1,0:T(8,128)(2,1)}, bf16[1024,1536]{1,0:T(8,128)(2,1)}, bf16[1024,1536]{1,0:T(8,128)(2,1)}) custom-call(bf16[1024,1536]{1,0:T(8,128)(2,1)} %all-gather.8.cloned.1.call-done.rows.refs_0_, bf16[1024,1536]{1,0:T(8,128)(2,1)} %all-gather.6.cloned.1.call-done.grads.refs_0_, ...), custom_call_target="tpu_custom_call" | custom-call | flops 301989888 | bytes 344064 | tf_op jit(solution)/shard_map/pallas_call | solution.py:307
  255.6 8.6 %shard_map.347 = (bf16[4,192,3072]{2,1,0:T(8,128)(2,1)}, bf16[4,192,3072]{2,1,0:T(8,128)(2,1)}) custom-call(s32[2]{0:T(128)} %pad_add_fusion.mine, bf16[1024,1536]{1,0:T(8,128)(2,1)} %all-gather.6.cloned.1.call-done.grads.refs_0_, bf16[1024,1024]{1,0:T(8,128)(2,1)} %get-tuple-element.133.refs_1_), custom_call_target="tpu_custom_call" | custom-call | flops 150994944 | bytes 327680 | tf_op jit(solution)/shard_map/pallas_call | solution.py:459
  264.2 13.6 %shard_map.348 = (bf16[4,192,3072]{2,1,0:T(8,128)(2,1)}, bf16[4,192,3072]{2,1,0:T(8,128)(2,1)}) custom-call(s32[2]{0:T(128)} %pad_add_fusion.mine, bf16[1024,1536]{1,0:T(8,128)(2,1)} %all-gather.8.cloned.1.call-done.rows.refs_0_, bf16[1024,1024]{1,0:T(8,128)(2,1)} %get-tuple-element.131.refs_1_, ...), custom_call_target="tpu_custom_call", output_to_operand_aliasing={{0}: (4, {}), {1}: (5, {})} | custom-call | flops 150994944 | bytes 327680 | tf_op jit(solution)/shard_map/pallas_call | solution.py:459
  277.9 8.1 %collective-permute-done.12.refs_1_.refs_3_.refs_4_.refs_5_.refs_9_.refs_13_ = bf16[4,192,3072]{2,1,0:T(8,128)(2,1)S(1)} collective-permute-done((bf16[4,192,3072]{2,1,0:T(8,128)(2,1)}, bf16[4,192,3072]{2,1,0:T(8,128)(2,1)S(1)}, u32[]{:S(2)}, u32[]{:S(2)}) %collective-permute-start.12) | collective-permute-done | bytes 4718624 | tf_op jit(solution)/shard_map/ppermute | solution.py:42
  294.7 19.2 %reduce-scatter.4.cloned.1.call-done.refs_0_ = bf16[256,1536]{1,0:T(8,128)(2,1)} async-done(((bf16[1024,1536]{1,0:T(8,128)(2,1)}), bf16[256,1536]{1,0:T(8,128)(2,1)}) %reduce-scatter.4.cloned.1.call-update) | async-done | bytes 786448 | tf_op jit(solution)/shard_map/reduce_scatter | solution.py:956
  313.9 7.6 %shard_map.350 = (f32[256,1536]{1,0:T(8,128)}, bf16[256,1536]{1,0:T(8,128)(2,1)}, f32[3,1536]{1,0:T(4,128)}, f32[3,1536]{1,0:T(4,128)}, bf16[384,256]{1,0:T(8,12...) custom-call(s32[1]{0:T(128)} %bitcast.rank.ranks, ...), custom_call_target="tpu_custom_call" | custom-call | flops 18874368 | bytes 196608 | tf_op jit(solution)/shard_map/pallas_call | solution.py:270
  332.4 9.2 %collective-permute-done.14.refs_2_ = bf16[384,256]{1,0:T(8,128)(2,1)S(1)} collective-permute-done((bf16[384,256]{1,0:T(8,128)(2,1)}, bf16[384,256]{1,0:T(8,128)(2,1)S(1)}, u32[]{:S(2)}, u32[]{:S(2)}) %collective-permute-start.14) | collective-permute-done | bytes 196640 | tf_op jit(solution)/shard_map/ppermute | solution.py:943
  347.2 10.5 %shard_map.352 = (bf16[2,384,384]{2,1,0:T(8,128)(2,1)}, f32[384,1024]{1,0:T(8,128)}, f32[6,64,128]{2,1,0:T(8,128)}) custom-call(s32[1]{0:T(128)} %bitcast.rank.ranks, f32[6]{0:T(128)} %dynamic-slice_tanh_fusion.gates, f32[1152,1024]{1,0:T(8,128)} %bitcast.120, f32[384,384]{1,0:T(8,128)} %fusion.48.text_key, f32[384,384]{1,0:T(8,128)} %fusion.49.text_value, ...), custom_call_target="tpu_custom_call" | custom-call | flops 14155776 | bytes 86016 | tf_op jit(solution)/shard_map/pallas_call | solution.py:733
  357.6 6.2 %shard_map.353 = bf16[2,384,2048]{2,1,0:T(8,128)(2,1)} custom-call(s32[8]{0:T(128)} %stack.127.places, bf16[2,384,384]{2,1,0:T(8,128)(2,1)} %get-tuple-element.166.grads, bf16[384,4096]{1,0:T(8,128)(2,1)} %bitcast.124, bf16[384,4096]{1,0:T(8,128)(2,1)} %bitcast.125), custom_call_target="tpu_custom_call" | custom-call | flops 18874368 | bytes 49152 | tf_op jit(solution)/shard_map/pallas_call | solution.py:497
  368.5 20.6 %shard_map.355 = (bf16[3,384,1024]{2,1,0:T(8,128)(2,1)}, f32[6,64,128]{2,1,0:T(8,128)}) custom-call(s32[1]{0:T(128)} %bitcast.rank.ranks, f32[1152,1024]{1,0:T(8,128)} %bitcast.121, f32[1152,1024]{1,0:T(8,128)} %bitcast.122, f32[1152,1024]{1,0:T(8,128)} %bitcast.123, f32[2,16,1024]{2,1,0:T(8,128)} %pad_maximum_fusion.4.table, ...), custom_call_target="tpu_custom_call" | custom-call | flops 125829120 | bytes 147456 | tf_op jit(solution)/shard_map/pallas_call | solution.py:751
  389.1 10.6 %shard_map.356 = (bf16[1024,1536]{1,0:T(8,128)(2,1)}, f32[3,1536]{1,0:T(4,128)}) custom-call(s32[1024,1]{1,0:T(8,128)} %copy.53.ids, bf16[1024,1536]{1,0:T(8,128)(2,1)} %all-gather.4.cloned.1.call-done.tokens, bf16[3,384,1024]{2,1,0:T(8,128)(2,1)} %get-tuple-element.170.grad_qkv, bf16[1536,384]{1,0:T(8,128)(2,1)} %w_query.3, bf16[1536,384]{1,0:T(8,128)(2,1)} %w_key.3, ...), custom_call_target="tpu_custom_call" | custom-call | flops 56623104 | bytes 190464 | tf_op jit(solution)/shard_map/pallas_call | solution.py:346
  401.3 6.2 %shard_map.357.refs_0_.refs_2_.refs_3_.refs_4_ = bf16[2,384,2048]{2,1,0:T(8,128)(2,1)} custom-call(s32[8]{0:T(128)} %stack.131.places, bf16[2,384,384]{2,1,0:T(8,128)(2,1)} %get-tuple-element.166.grads, bf16[384,4096]{1,0:T(8,128)(2,1)} %bitcast.126, bf16[384,4096]{1,0:T(8,128)(2,1)} %bitcast.127), custom_call_target="tpu_custom_call" | custom-call | flops 18874368 | bytes 49152 | tf_op jit(solution)/shard_map/pallas_call | solution.py:497
  413.1 6.2 %convolution_convert_fusion = bf16[1536,1152]{1,0:T(8,128)(2,1)S(1)} fusion(bf16[1024,1536]{1,0:T(8,128)(2,1)} %get-tuple-element.164, bf16[1152,1024]{1,0:T(8,128)(2,1)S(1)} %bitcast.135), kind=kOutput, calls=%fused_computation | convolution fusion | flops 3625648128 | bytes 9043968 | tf_op jit(solution)/shard_map/dot_general | solution.py:46
  432.3 10.2 %collective-permute-done.25.refs_2_ = bf16[1,384,1024]{2,1,0:T(8,128)(2,1)S(1)} collective-permute-done((bf16[1,384,1024]{2,1,0:T(8,128)(2,1)}, bf16[1,384,1024]{2,1,0:T(8,128)(2,1)S(1)}, u32[]{:S(2)}, u32[]{:S(2)}) %collective-permute-start.25) | collective-permute-done | bytes 786464 | tf_op jit(solution)/shard_map/ppermute | solution.py:42
  457.8 20.2 %collective-permute-done.31.refs_3_ = bf16[1,192,1536]{2,1,0:T(8,128)(2,1)S(1)} collective-permute-done((bf16[1,192,1536]{2,1,0:T(8,128)(2,1)S(1)}, bf16[1,192,1536]{2,1,0:T(8,128)(2,1)S(1)}, u32[]{:S(2)}, u32[]{:S(2)}) %collective-permute-start.31) | collective-permute-done | bytes 589856 | tf_op jit(solution)/shard_map/ppermute | solution.py:42
  (320 shorter events, 160.1 us)
Async XLA Ops:
  7.2 72.7 %all-gather.4.cloned.1.call-start = ((), (), s32[]{:S(2)}) async-start(), calls=%async_computation.3 | async-start | bytes 3932160 | tf_op jit(solution)/shard_map/all_gather | solution.py:1019
  8.0 155.4 %all-gather.6.cloned.1.call-start = ((), (), s32[]{:S(2)}) async-start(), calls=%async_computation.4 | async-start | bytes 3932160 | tf_op jit(solution)/shard_map/all_gather | solution.py:1048
  31.0 48.9 %collective-permute-start.6 = (bf16[1,4,48,1536]{3,2,1,0:T(8,128)(2,1)S(1)}, bf16[1,4,48,1536]{3,2,1,0:T(8,128)(2,1)S(1)}, u32[]{:S(2)}, u32[]{:S(2)}) collective-permute-start(bf16[1,4,48,1536]{3,2,1,0:T(8,128)(2,1)S(1)} %maximum_bitcast_fusion), channel_id=1, source_target_pairs={{0,16},{4,20},{8,24},{12,28},{16,0},{20,4},{24,8},{28,12},{1,17},{... | collective-permute-start | bytes 1769480 | tf_op jit(solution)/shard_map/ppermute | solution.py:42
  41.2 187.4 %all-gather.8.cloned.1.call-start = ((), (), s32[]{:S(2)}) async-start(), calls=%async_computation.5 | async-start | bytes 3932160 | tf_op jit(solution)/shard_map/all_gather | solution.py:1067
  80.0 35.5 %collective-permute-start.7 = (bf16[2,4,48,1536]{3,2,1,0:T(8,128)(2,1)S(1)}, bf16[2,4,48,1536]{3,2,1,0:T(8,128)(2,1)S(1)}, u32[]{:S(2)}, u32[]{:S(2)}) collective-permute-start(bf16[2,4,48,1536]{3,2,1,0:T(8,128)(2,1)S(1)} %constant_dynamic-update-slice_fusion), channel_id=1, source_target_pairs={{0,8},{4,12},{8,0},{12,4},{16,24},{20,28},{24,16},{28,20},{1,9},{5... | collective-permute-start | bytes 3538952 | tf_op jit(solution)/shard_map/ppermute | solution.py:42
  119.5 27.1 %collective-permute-start.10 = (bf16[384,256]{1,0:T(8,128)(2,1)S(1)}, bf16[384,256]{1,0:T(8,128)(2,1)S(1)}, u32[]{:S(2)}, u32[]{:S(2)}) collective-permute-start(bf16[384,256]{1,0:T(8,128)(2,1)S(1)} %get-tuple-element.264), channel_id=1, source_target_pairs={{0,2},{1,3},{2,0},{3,1},{4,6},{5,7},{6,4},{7,5},{8,10},{9,11},{10,... | collective-permute-start | bytes 589832 | tf_op jit(solution)/shard_map/ppermute | solution.py:943
  163.4 150.5 %reduce-scatter.4.cloned.1.call-start = ((), (), s32[]{:S(2)}) async-start(), calls=%async_computation.6 | async-start | bytes 3932160 | tf_op jit(solution)/shard_map/reduce_scatter | solution.py:956
  254.8 169.0 %reduce-scatter.6.cloned.1.call-start = ((), (), s32[]{:S(2)}) async-start(), calls=%async_computation.7 | async-start | bytes 3932160 | tf_op jit(solution)/shard_map/reduce_scatter | solution.py:956
  291.7 35.5 %collective-permute-start.16 = (bf16[2,192,1536]{2,1,0:T(8,128)(2,1)}, bf16[2,192,1536]{2,1,0:T(8,128)(2,1)S(1)}, u32[]{:S(2)}, u32[]{:S(2)}) collective-permute-start(bf16[2,192,1536]{2,1,0:T(8,128)(2,1)} %get-tuple-element.138), channel_id=1, source_target_pairs={{0,8},{4,12},{8,0},{12,4},{16,24},{20,28},{24,16},{28,20},{1,9},{5... | collective-permute-start | bytes 3538952 | tf_op jit(solution)/shard_map/ppermute | solution.py:42
  293.2 34.0 %collective-permute-start.17 = (bf16[2,192,1536]{2,1,0:T(8,128)(2,1)}, bf16[2,192,1536]{2,1,0:T(8,128)(2,1)S(1)}, u32[]{:S(2)}, u32[]{:S(2)}) collective-permute-start(bf16[2,192,1536]{2,1,0:T(8,128)(2,1)} %get-tuple-element.139), channel_id=1, source_target_pairs={{0,16},{4,20},{8,24},{12,28},{16,0},{20,4},{24,8},{28,12},{1,17},{... | collective-permute-start | bytes 3538952 | tf_op jit(solution)/shard_map/ppermute | solution.py:42
  341.7 144.9 %reduce-scatter.8.cloned.1.call-start = ((), (), s32[]{:S(2)}) async-start(), calls=%async_computation.8 | async-start | bytes 3932160 | tf_op jit(solution)/shard_map/reduce_scatter | solution.py:956
  367.8 39.7 %collective-permute-start.19 = (bf16[2,384,2048]{2,1,0:T(8,128)(2,1)}, bf16[2,384,2048]{2,1,0:T(8,128)(2,1)S(1)}, u32[]{:S(2)}, u32[]{:S(2)}) collective-permute-start(bf16[2,384,2048]{2,1,0:T(8,128)(2,1)} %shard_map.353), channel_id=1, source_target_pairs={{0,4},{4,0},{8,12},{12,8},{16,20},{20,16},{24,28},{28,24},{1,5},{5... | collective-permute-start | bytes 9437192 | tf_op jit(solution)/shard_map/ppermute | solution.py:42
  399.7 29.6 %collective-permute-start.23 = (bf16[2,192,1536]{2,1,0:T(8,128)(2,1)}, bf16[2,192,1536]{2,1,0:T(8,128)(2,1)}, u32[]{:S(2)}, u32[]{:S(2)}) collective-permute-start(bf16[2,192,1536]{2,1,0:T(8,128)(2,1)} %shard_map.354), channel_id=1, source_target_pairs={{0,16},{4,20},{8,24},{12,28},{16,0},{20,4},{24,8},{28,12},{1,17},{... | collective-permute-start | bytes 3538952 | tf_op jit(solution)/shard_map/ppermute | solution.py:42
  421.5 29.0 %collective-permute-start.24 = (bf16[4,192,1152]{2,1,0:T(8,128)(2,1)}, bf16[4,192,1152]{2,1,0:T(8,128)(2,1)S(1)}, u32[]{:S(2)}, u32[]{:S(2)}) collective-permute-start(bf16[4,192,1152]{2,1,0:T(8,128)(2,1)} %get-tuple-element.171), channel_id=1, source_target_pairs={{0,4},{4,0},{8,12},{12,8},{16,20},{20,16},{24,28},{28,24},{1,5},{5... | collective-permute-start | bytes 5308424 | tf_op jit(solution)/shard_map/ppermute | solution.py:42
  423.6 24.0 %collective-permute-start.26 = (bf16[1,384,1024]{2,1,0:T(8,128)(2,1)}, bf16[1,384,1024]{2,1,0:T(8,128)(2,1)}, u32[]{:S(2)}, u32[]{:S(2)}) collective-permute-start(bf16[1,384,1024]{2,1,0:T(8,128)(2,1)} %get-tuple-element.188), channel_id=1, source_target_pairs={{0,16},{4,20},{8,24},{12,28},{16,0},{20,4},{24,8},{28,12},{1,17},{... | collective-permute-start | bytes 2359304 | tf_op jit(solution)/shard_map/ppermute | solution.py:42
  428.4 25.9 %collective-permute-start.22 = (f32[6,1536]{1,0:T(8,128)S(1)}, f32[6,1536]{1,0:T(8,128)S(1)}, u32[]{:S(2)}, u32[]{:S(2)}) collective-permute-start(f32[6,1536]{1,0:T(8,128)S(1)} %get-tuple-element.277), channel_id=1, source_target_pairs={{0,1},{1,2},{2,3},{3,0},{4,5},{5,6},{6,7},{7,4},{8,9},{9,10},{10,1... | collective-permute-start | bytes 110600 | tf_op jit(solution)/shard_map/ppermute | solution.py:943
  429.3 25.0 %collective-permute-start.20 = (f32[6,1536]{1,0:T(8,128)S(1)}, f32[6,1536]{1,0:T(8,128)S(1)}, u32[]{:S(2)}, u32[]{:S(2)}) collective-permute-start(f32[6,1536]{1,0:T(8,128)S(1)} %get-tuple-element.278), channel_id=1, source_target_pairs={{0,3},{1,0},{2,1},{3,2},{4,7},{5,4},{6,5},{7,6},{8,11},{9,8},{10,9... | collective-permute-start | bytes 110600 | tf_op jit(solution)/shard_map/ppermute | solution.py:943
  447.7 38.9 %collective-permute-start.28 = (bf16[1,192,1536]{2,1,0:T(8,128)(2,1)S(1)}, bf16[1,192,1536]{2,1,0:T(8,128)(2,1)S(1)}, u32[]{:S(2)}, u32[]{:S(2)}) collective-permute-start(bf16[1,192,1536]{2,1,0:T(8,128)(2,1)S(1)} %copy-done.56), channel_id=1, source_target_pairs={{0,16},{4,20},{8,24},{12,28},{16,0},{20,4},{24,8},{28,12},{1,17},{... | collective-permute-start | bytes 1769480 | tf_op jit(solution)/shard_map/ppermute | solution.py:42
  450.5 36.0 %collective-permute-start.29 = (bf16[1,192,1536]{2,1,0:T(8,128)(2,1)S(1)}, bf16[1,192,1536]{2,1,0:T(8,128)(2,1)S(1)}, u32[]{:S(2)}, u32[]{:S(2)}) collective-permute-start(bf16[1,192,1536]{2,1,0:T(8,128)(2,1)S(1)} %copy-done.55), channel_id=1, source_target_pairs={{0,8},{4,12},{8,0},{12,4},{16,24},{20,28},{24,16},{28,20},{1,9},{5... | collective-permute-start | bytes 1769480 | tf_op jit(solution)/shard_map/ppermute | solution.py:42
  454.3 23.7 %collective-permute-start.31 = (bf16[1,192,1536]{2,1,0:T(8,128)(2,1)S(1)}, bf16[1,192,1536]{2,1,0:T(8,128)(2,1)S(1)}, u32[]{:S(2)}, u32[]{:S(2)}) collective-permute-start(bf16[1,192,1536]{2,1,0:T(8,128)(2,1)S(1)} %copy-done.29), channel_id=1, source_target_pairs={{0,8},{4,12},{8,0},{12,4},{16,24},{20,28},{24,16},{28,20},{1,9},{5... | collective-permute-start | bytes 1769480 | tf_op jit(solution)/shard_map/ppermute | solution.py:42
  455.6 27.3 %collective-permute-start.32 = (bf16[2,192,1152]{2,1,0:T(8,128)(2,1)}, bf16[2,192,1152]{2,1,0:T(8,128)(2,1)S(1)}, u32[]{:S(2)}, u32[]{:S(2)}) collective-permute-start(bf16[2,192,1152]{2,1,0:T(8,128)(2,1)} %shard_map.362), channel_id=1, source_target_pairs={{0,16},{4,20},{8,24},{12,28},{16,0},{20,4},{24,8},{28,12},{1,17},{... | collective-permute-start | bytes 2654216 | tf_op jit(solution)/shard_map/ppermute | solution.py:42
  457.7 34.3 %collective-permute-start.27 = (f32[7,1536]{1,0:T(8,128)S(1)}, f32[7,1536]{1,0:T(8,128)S(1)}, u32[]{:S(2)}, u32[]{:S(2)}) collective-permute-start(f32[7,1536]{1,0:T(8,128)S(1)} %pad_maximum_fusion.12), channel_id=1, source_target_pairs={{0,4},{4,0},{8,12},{12,8},{16,20},{20,16},{24,28},{28,24},{1,5},{5... | collective-permute-start | bytes 129032 | tf_op jit(solution)/shard_map/ppermute | solution.py:42
  478.0 38.4 %collective-permute-start.34 = (bf16[1,384,512]{2,1,0:T(8,128)(2,1)}, bf16[1,384,512]{2,1,0:T(8,128)(2,1)S(1)}, u32[]{:S(2)}, u32[]{:S(2)}) collective-permute-start(bf16[1,384,512]{2,1,0:T(8,128)(2,1)} %get-tuple-element.202), channel_id=1, source_target_pairs={{0,16},{4,20},{8,24},{12,28},{16,0},{20,4},{24,8},{28,12},{1,17},{... | collective-permute-start | bytes 1179656 | tf_op jit(solution)/shard_map/ppermute | solution.py:42
  483.0 33.5 %collective-permute-start.35 = (bf16[1,384,512]{2,1,0:T(8,128)(2,1)}, bf16[1,384,512]{2,1,0:T(8,128)(2,1)}, u32[]{:S(2)}, u32[]{:S(2)}) collective-permute-start(bf16[1,384,512]{2,1,0:T(8,128)(2,1)} %get-tuple-element.203), channel_id=1, source_target_pairs={{0,8},{4,12},{8,0},{12,4},{16,24},{20,28},{24,16},{28,20},{1,9},{5... | collective-permute-start | bytes 1179656 | tf_op jit(solution)/shard_map/ppermute | solution.py:42
  (80 other events, 882.7 us)
Sparse Core Ops, SparseCore 0:
  9.6 70.2 all-gather.3
  82.0 81.3 all-gather.5
  165.5 62.9 all-gather.7
  254.9 58.8 reduce-scatter.3
  341.8 60.4 reduce-scatter.5
  404.5 63.3 reduce-scatter.7

commit v3 on v2

--- a/solution.py
+++ b/solution.py
@@ -1132,7 +1132,9 @@
     )
     qkv_taken = exchange(qkv_given, "dp", 1)
     qkv_scatter = Scatter(qkv_held, qkv_taken, orders[1], 0, 3 * head_cols)
-    (out_ready,) = lax.optimization_barrier((out_cuts[0], qkv_given))[:1]
+    (out_next,) = next_sums([out_scatter])
+    out_ready, out_next = lax.optimization_barrier((out_cuts[0], out_next))
+    out_scatter.send(out_next)
     block_out, gate_ffn_sums = block_result(rank, mod, my_ids, middle, out_grad, [out_ready])
 
     modulation = in_rank_order(mod)
@@ -1175,10 +1177,8 @@
             for m in range(tensor_size)
         ]
     )
-    (out_next,) = next_sums([out_scatter])
     qkv_next = next_sums([qkv_scatter])
-    payloads, out_next, qkv_next = lax.optimization_barrier((payloads, out_next, qkv_next))
-    out_scatter.send(out_next)
+    payloads, qkv_next = lax.optimization_barrier((payloads, qkv_next))
     send_all([qkv_scatter], qkv_next)
     summed = jnp.sum(in_rank_order(jnp.stack(payloads)), axis=0)
     mod_grad = summed[:clip_count].astype(jnp.bfloat16).astype(jnp.float32)

time: 540 us -> 544 us (level)
    unnamed x132 -> x130, local copies, waits for them, and re-layouts: 14.9 us -> 16 us
  transfers between devices with their start and end apart: 46 -> 46, of which waited for: 16 -> 15; matrix products, arithmetic and copies ran while one was open for 9% -> 8% of each run, Pallas kernels for 31% -> 31%
where the time goes in v3:
time: 544 us; the launch traced here: 534 us
  waiting for transfers between devices  208 us (38%)
  Pallas kernels  197 us (36%)
  starting transfers between devices  51.8 us (10%)
  local copies, waits for them, and re-layouts  34.6 us (6%)
  matrix products  17.3 us (3%)
  between operations  15.4 us (3%)
  other arithmetic  10.1 us (2%)
    all_gather x1, waiting for transfers between devices, on_device(): ffn_all = lax.all_gather(ffn_rows, 'tensor', axis=0, tiled=True)  65.1 us
    ppermute x22, waiting for transfers between devices, exchange(): lax.ppermute(values, axis_name, [(i, i ^ distance) for i in range(count)])  43.5 us
    all_gather x1, waiting for transfers between devices, on_device(): tokens_all = lax.all_gather(tokens, 'tensor', axis=0, tiled=True)  37.3 us
    pallas_call x11, Pallas kernels, sum_stage(): pl.pallas_call(functools.partial(sum_kernel, [(len(job[0]), job[3]) for j...  34.3 us
    ppermute x18, waiting for transfers between devices, shift_ranks(): lax.ppermute(pieces[m], 'tensor', [(i, (i + m) % count) for i in range(co...  33.1 us
    ppermute x18, starting transfers between devices, shift_ranks(): lax.ppermute(pieces[m], 'tensor', [(i, (i + m) % count) for i in range(co...  29.2 us
    pallas_call x1, Pallas kernels, feed_forward(): pl.pallas_call(ffn_kernel, grid=(count // step,), in_specs=[wide, wide, w...  26.2 us
    ppermute x22, starting transfers between devices, exchange(): lax.ppermute(values, axis_name, [(i, i ^ distance) for i in range(count)])  22.1 us
  transfers between devices with their start and end apart: 46, of which 15 were waited for; matrix products, arithmetic and copies ran while one was open for 8% of the time, Pallas kernels for 31%

profile of v3, /device:TPU:0, one launch (start us, length us, event | category | flops | bytes accessed | tf_op | source)
XLA Modules:
  0.0 534.3 jit_solution(12836437846511586736)
XLA Ops:
  42.6 37.3 %all-gather.4.cloned.1.call-done.tokens = bf16[1024,1536]{1,0:T(8,128)(2,1)} async-done(((bf16[256,1536]{1,0:T(8,128)(2,1)}), bf16[1024,1536]{1,0:T(8,128)(2,1)}) %all-gather.4.cloned.1.call-update) | async-done | bytes 3145744 | tf_op jit(solution)/shard_map/all_gather | solution.py:1019
  85.2 10.9 %shard_map.342 = (bf16[1024,1536]{1,0:T(8,128)(2,1)}, f32[3,384,1024]{2,1,0:T(8,128)}) custom-call(s32[1]{0:T(128)} %bitcast.rank.ranks, f32[4,3,1536]{2,1,0:T(4,128)} %pad_maximum_fusion.5.mod, s32[1024,1]{1,0:T(8,128)} %copy.53.ids, f32[1,1536]{1,0:T(1,128)} %broadcast_in_dim.126.gain, bf16[1024,1536]{1,0:T(8,128)(2,1)} %all-gather.4.cloned.1.call-done.tokens, ...), custom_call_target="tpu_custom_call" | custom-call | flops 56623104 | bytes 227328 | tf_op jit(solution)/shard_map/pallas_call | solution.py:160
  96.1 19.4 %shard_map.343 = (bf16[4,384,256]{2,1,0:T(8,128)(2,1)}, f32[384,1024]{1,0:T(8,128)}, f32[384,1024]{1,0:T(8,128)}, f32[6,1,1024]{2,1,0:T(1,128)}, f32[6,1,1024]{2,1,0:T(1,128)}) custom-call(s32[1]{0:T(128)} %bitcast.rank.ranks, f32[6]{0:T(128)} %dynamic-slice_tanh_fusion.gates, f32[1152,1024]{1,0:T(8,128)} %bitcast.117, f32[1152,1024]{1,0:T(8,128)} %bitcast.118, ...), custom_call_target="tpu_custom_call" | custom-call | flops 50331648 | bytes 147456 | tf_op jit(solution)/shard_map/pallas_call | solution.py:703
  125.6 5.0 shard_map.344
  132.9 13.7 %collective-permute-done.10.refs_2_ = bf16[384,256]{1,0:T(8,128)(2,1)S(1)} collective-permute-done((bf16[384,256]{1,0:T(8,128)(2,1)S(1)}, bf16[384,256]{1,0:T(8,128)(2,1)S(1)}, u32[]{:S(2)}, u32[]{:S(2)}) %collective-permute-start.10) | collective-permute-done | bytes 196640 | tf_op jit(solution)/shard_map/ppermute | solution.py:943
  147.4 6.7 %shard_map.345 = (f32[256,1536]{1,0:T(8,128)}, f32[256,1536]{1,0:T(8,128)}, bf16[256,1536]{1,0:T(8,128)(2,1)}) custom-call(s32[1]{0:T(128)} %bitcast.rank.ranks, f32[4,3,1536]{2,1,0:T(4,128)} %pad_maximum_fusion.5.mod, s32[256,1]{1,0:T(8,128)} %copy.62.ids, f32[1,1536]{1,0:T(1,128)} %broadcast_in_dim.112.gain, bf16[256,1536]{1,0:T(8,128)(2,1)} %tokens.3, ...), custom_call_target="tpu_custom_call" | custom-call | flops 18874368 | bytes 159744 | tf_op jit(solution)/shard_map/pallas_call | solution.py:227
  154.1 9.3 %all-gather.6.cloned.1.call-done.grads.refs_0_ = bf16[1024,1536]{1,0:T(8,128)(2,1)} async-done(((bf16[256,1536]{1,0:T(8,128)(2,1)}), bf16[1024,1536]{1,0:T(8,128)(2,1)}) %all-gather.6.cloned.1.call-update) | async-done | bytes 3145744 | tf_op jit(solution)/shard_map/all_gather | solution.py:1048
  163.5 65.1 %all-gather.8.cloned.1.call-done.rows.refs_0_ = bf16[1024,1536]{1,0:T(8,128)(2,1)} async-done(((bf16[256,1536]{1,0:T(8,128)(2,1)}), bf16[1024,1536]{1,0:T(8,128)(2,1)}) %all-gather.8.cloned.1.call-update) | async-done | bytes 3145744 | tf_op jit(solution)/shard_map/all_gather | solution.py:1067
  228.6 26.2 %shard_map.346 = (bf16[1024,1024]{1,0:T(8,128)(2,1)}, bf16[1024,1024]{1,0:T(8,128)(2,1)}, bf16[1024,1024]{1,0:T(8,128)(2,1)}, bf16[1024,1536]{1,0:T(8,128)(2,1)}, bf16[1024,1536]{1,0:T(8,128)(2,1)}) custom-call(bf16[1024,1536]{1,0:T(8,128)(2,1)} %all-gather.8.cloned.1.call-done.rows.refs_0_, bf16[1024,1536]{1,0:T(8,128)(2,1)} %all-gather.6.cloned.1.call-done.grads.refs_0_, ...), custom_call_target="tpu_custom_call" | custom-call | flops 301989888 | bytes 344064 | tf_op jit(solution)/shard_map/pallas_call | solution.py:307
  255.6 8.5 %shard_map.347 = (bf16[4,192,3072]{2,1,0:T(8,128)(2,1)}, bf16[4,192,3072]{2,1,0:T(8,128)(2,1)}) custom-call(s32[2]{0:T(128)} %pad_add_fusion.mine, bf16[1024,1536]{1,0:T(8,128)(2,1)} %all-gather.6.cloned.1.call-done.grads.refs_0_, bf16[1024,1024]{1,0:T(8,128)(2,1)} %get-tuple-element.133.refs_1_), custom_call_target="tpu_custom_call" | custom-call | flops 150994944 | bytes 327680 | tf_op jit(solution)/shard_map/pallas_call | solution.py:459
  264.1 13.6 %shard_map.348 = (bf16[4,192,3072]{2,1,0:T(8,128)(2,1)}, bf16[4,192,3072]{2,1,0:T(8,128)(2,1)}) custom-call(s32[2]{0:T(128)} %pad_add_fusion.mine, bf16[1024,1536]{1,0:T(8,128)(2,1)} %all-gather.8.cloned.1.call-done.rows.refs_0_, bf16[1024,1024]{1,0:T(8,128)(2,1)} %get-tuple-element.131.refs_1_, ...), custom_call_target="tpu_custom_call", output_to_operand_aliasing={{0}: (4, {}), {1}: (5, {})} | custom-call | flops 150994944 | bytes 327680 | tf_op jit(solution)/shard_map/pallas_call | solution.py:459
  277.8 8.1 %collective-permute-done.12.refs_1_.refs_3_.refs_4_.refs_5_.refs_9_.refs_13_ = bf16[4,192,3072]{2,1,0:T(8,128)(2,1)S(1)} collective-permute-done((bf16[4,192,3072]{2,1,0:T(8,128)(2,1)}, bf16[4,192,3072]{2,1,0:T(8,128)(2,1)S(1)}, u32[]{:S(2)}, u32[]{:S(2)}) %collective-permute-start.12) | collective-permute-done | bytes 4718624 | tf_op jit(solution)/shard_map/ppermute | solution.py:42
  294.6 19.3 %reduce-scatter.4.cloned.1.call-done.refs_0_ = bf16[256,1536]{1,0:T(8,128)(2,1)} async-done(((bf16[1024,1536]{1,0:T(8,128)(2,1)}), bf16[256,1536]{1,0:T(8,128)(2,1)}) %reduce-scatter.4.cloned.1.call-update) | async-done | bytes 786448 | tf_op jit(solution)/shard_map/reduce_scatter | solution.py:956
  313.9 7.6 %shard_map.350 = (f32[256,1536]{1,0:T(8,128)}, bf16[256,1536]{1,0:T(8,128)(2,1)}, f32[3,1536]{1,0:T(4,128)}, f32[3,1536]{1,0:T(4,128)}, bf16[384,256]{1,0:T(8,12...) custom-call(s32[1]{0:T(128)} %bitcast.rank.ranks, ...), custom_call_target="tpu_custom_call" | custom-call | flops 18874368 | bytes 196608 | tf_op jit(solution)/shard_map/pallas_call | solution.py:270
  332.5 9.2 %collective-permute-done.14.refs_2_ = bf16[384,256]{1,0:T(8,128)(2,1)S(1)} collective-permute-done((bf16[384,256]{1,0:T(8,128)(2,1)}, bf16[384,256]{1,0:T(8,128)(2,1)S(1)}, u32[]{:S(2)}, u32[]{:S(2)}) %collective-permute-start.14) | collective-permute-done | bytes 196640 | tf_op jit(solution)/shard_map/ppermute | solution.py:943
  347.1 10.5 %shard_map.352 = (bf16[2,384,384]{2,1,0:T(8,128)(2,1)}, f32[384,1024]{1,0:T(8,128)}, f32[6,64,128]{2,1,0:T(8,128)}) custom-call(s32[1]{0:T(128)} %bitcast.rank.ranks, f32[6]{0:T(128)} %dynamic-slice_tanh_fusion.gates, f32[1152,1024]{1,0:T(8,128)} %bitcast.120, f32[384,384]{1,0:T(8,128)} %fusion.48.text_key, f32[384,384]{1,0:T(8,128)} %fusion.49.text_value, ...), custom_call_target="tpu_custom_call" | custom-call | flops 14155776 | bytes 86016 | tf_op jit(solution)/shard_map/pallas_call | solution.py:733
  357.6 6.2 %shard_map.353 = bf16[2,384,2048]{2,1,0:T(8,128)(2,1)} custom-call(s32[8]{0:T(128)} %stack.127.places, bf16[2,384,384]{2,1,0:T(8,128)(2,1)} %get-tuple-element.170.grads, bf16[384,4096]{1,0:T(8,128)(2,1)} %bitcast.124, bf16[384,4096]{1,0:T(8,128)(2,1)} %bitcast.125), custom_call_target="tpu_custom_call" | custom-call | flops 18874368 | bytes 49152 | tf_op jit(solution)/shard_map/pallas_call | solution.py:497
  368.5 20.6 %shard_map.357 = (bf16[3,384,1024]{2,1,0:T(8,128)(2,1)}, f32[6,64,128]{2,1,0:T(8,128)}) custom-call(s32[1]{0:T(128)} %bitcast.rank.ranks, f32[1152,1024]{1,0:T(8,128)} %bitcast.121, f32[1152,1024]{1,0:T(8,128)} %bitcast.122, f32[1152,1024]{1,0:T(8,128)} %bitcast.123, f32[2,16,1024]{2,1,0:T(8,128)} %pad_maximum_fusion.4.table, ...), custom_call_target="tpu_custom_call" | custom-call | flops 125829120 | bytes 147456 | tf_op jit(solution)/shard_map/pallas_call | solution.py:751
  389.1 10.6 %shard_map.358 = (bf16[1024,1536]{1,0:T(8,128)(2,1)}, f32[3,1536]{1,0:T(4,128)}) custom-call(s32[1024,1]{1,0:T(8,128)} %copy.53.ids, bf16[1024,1536]{1,0:T(8,128)(2,1)} %all-gather.4.cloned.1.call-done.tokens, bf16[3,384,1024]{2,1,0:T(8,128)(2,1)} %get-tuple-element.174.grad_qkv, bf16[1536,384]{1,0:T(8,128)(2,1)} %w_query.3, bf16[1536,384]{1,0:T(8,128)(2,1)} %w_key.3, ...), custom_call_target="tpu_custom_call" | custom-call | flops 56623104 | bytes 190464 | tf_op jit(solution)/shard_map/pallas_call | solution.py:346
  401.3 6.2 %shard_map.360.refs_0_.refs_2_.refs_3_.refs_4_ = bf16[2,384,2048]{2,1,0:T(8,128)(2,1)} custom-call(s32[8]{0:T(128)} %stack.131.places, bf16[2,384,384]{2,1,0:T(8,128)(2,1)} %get-tuple-element.170.grads, bf16[384,4096]{1,0:T(8,128)(2,1)} %bitcast.126, bf16[384,4096]{1,0:T(8,128)(2,1)} %bitcast.127), custom_call_target="tpu_custom_call" | custom-call | flops 18874368 | bytes 49152 | tf_op jit(solution)/shard_map/pallas_call | solution.py:497
  413.1 6.2 %convolution_convert_fusion = bf16[1536,1152]{1,0:T(8,128)(2,1)S(1)} fusion(bf16[1024,1536]{1,0:T(8,128)(2,1)} %get-tuple-element.169, bf16[1152,1024]{1,0:T(8,128)(2,1)S(1)} %bitcast.135), kind=kOutput, calls=%fused_computation | convolution fusion | flops 3625648128 | bytes 9043968 | tf_op jit(solution)/shard_map/dot_general | solution.py:46
  422.2 5.7 %collective-permute-done.19.refs_2_ = bf16[2,192,1536]{2,1,0:T(8,128)(2,1)S(1)} collective-permute-done((bf16[2,192,1536]{2,1,0:T(8,128)(2,1)}, bf16[2,192,1536]{2,1,0:T(8,128)(2,1)S(1)}, u32[]{:S(2)}, u32[]{:S(2)}) %collective-permute-start.19) | collective-permute-done | bytes 1179680 | tf_op jit(solution)/shard_map/ppermute | solution.py:42
  443.0 7.4 %collective-permute-done.25.refs_2_ = bf16[1,384,1024]{2,1,0:T(8,128)(2,1)S(1)} collective-permute-done((bf16[1,384,1024]{2,1,0:T(8,128)(2,1)}, bf16[1,384,1024]{2,1,0:T(8,128)(2,1)S(1)}, u32[]{:S(2)}, u32[]{:S(2)}) %collective-permute-start.25) | collective-permute-done | bytes 786464 | tf_op jit(solution)/shard_map/ppermute | solution.py:42
  463.5 20.0 %collective-permute-done.31.refs_3_ = bf16[1,192,1536]{2,1,0:T(8,128)(2,1)S(1)} collective-permute-done((bf16[1,192,1536]{2,1,0:T(8,128)(2,1)S(1)}, bf16[1,192,1536]{2,1,0:T(8,128)(2,1)S(1)}, u32[]{:S(2)}, u32[]{:S(2)}) %collective-permute-start.31) | collective-permute-done | bytes 589856 | tf_op jit(solution)/shard_map/ppermute | solution.py:42
  (318 shorter events, 165.5 us)
Async XLA Ops:
  7.2 72.7 %all-gather.4.cloned.1.call-start = ((), (), s32[]{:S(2)}) async-start(), calls=%async_computation.3 | async-start | bytes 3932160 | tf_op jit(solution)/shard_map/all_gather | solution.py:1019
  8.0 155.4 %all-gather.6.cloned.1.call-start = ((), (), s32[]{:S(2)}) async-start(), calls=%async_computation.4 | async-start | bytes 3932160 | tf_op jit(solution)/shard_map/all_gather | solution.py:1048
  31.0 48.9 %collective-permute-start.6 = (bf16[1,4,48,1536]{3,2,1,0:T(8,128)(2,1)S(1)}, bf16[1,4,48,1536]{3,2,1,0:T(8,128)(2,1)S(1)}, u32[]{:S(2)}, u32[]{:S(2)}) collective-permute-start(bf16[1,4,48,1536]{3,2,1,0:T(8,128)(2,1)S(1)} %maximum_bitcast_fusion), channel_id=1, source_target_pairs={{0,16},{4,20},{8,24},{12,28},{16,0},{20,4},{24,8},{28,12},{1,17},{... | collective-permute-start | bytes 1769480 | tf_op jit(solution)/shard_map/ppermute | solution.py:42
  41.2 187.4 %all-gather.8.cloned.1.call-start = ((), (), s32[]{:S(2)}) async-start(), calls=%async_computation.5 | async-start | bytes 3932160 | tf_op jit(solution)/shard_map/all_gather | solution.py:1067
  80.0 35.5 %collective-permute-start.7 = (bf16[2,4,48,1536]{3,2,1,0:T(8,128)(2,1)S(1)}, bf16[2,4,48,1536]{3,2,1,0:T(8,128)(2,1)S(1)}, u32[]{:S(2)}, u32[]{:S(2)}) collective-permute-start(bf16[2,4,48,1536]{3,2,1,0:T(8,128)(2,1)S(1)} %constant_dynamic-update-slice_fusion), channel_id=1, source_target_pairs={{0,8},{4,12},{8,0},{12,4},{16,24},{20,28},{24,16},{28,20},{1,9},{5... | collective-permute-start | bytes 3538952 | tf_op jit(solution)/shard_map/ppermute | solution.py:42
  119.5 27.1 %collective-permute-start.10 = (bf16[384,256]{1,0:T(8,128)(2,1)S(1)}, bf16[384,256]{1,0:T(8,128)(2,1)S(1)}, u32[]{:S(2)}, u32[]{:S(2)}) collective-permute-start(bf16[384,256]{1,0:T(8,128)(2,1)S(1)} %get-tuple-element.264), channel_id=1, source_target_pairs={{0,2},{1,3},{2,0},{3,1},{4,6},{5,7},{6,4},{7,5},{8,10},{9,11},{10,... | collective-permute-start | bytes 589832 | tf_op jit(solution)/shard_map/ppermute | solution.py:943
  123.2 23.5 %collective-permute-start.9 = (bf16[384,256]{1,0:T(8,128)(2,1)S(1)}, bf16[384,256]{1,0:T(8,128)(2,1)S(1)}, u32[]{:S(2)}, u32[]{:S(2)}) collective-permute-start(bf16[384,256]{1,0:T(8,128)(2,1)S(1)} %get-tuple-element.265), channel_id=1, source_target_pairs={{0,3},{1,0},{2,1},{3,2},{4,7},{5,4},{6,5},{7,6},{8,11},{9,8},{10,9... | collective-permute-start | bytes 589832 | tf_op jit(solution)/shard_map/ppermute | solution.py:943
  163.4 150.5 %reduce-scatter.4.cloned.1.call-start = ((), (), s32[]{:S(2)}) async-start(), calls=%async_computation.6 | async-start | bytes 3932160 | tf_op jit(solution)/shard_map/reduce_scatter | solution.py:956
  254.8 179.6 %reduce-scatter.6.cloned.1.call-start = ((), (), s32[]{:S(2)}) async-start(), calls=%async_computation.7 | async-start | bytes 3932160 | tf_op jit(solution)/shard_map/reduce_scatter | solution.py:956
  291.6 35.6 %collective-permute-start.16 = (bf16[2,192,1536]{2,1,0:T(8,128)(2,1)}, bf16[2,192,1536]{2,1,0:T(8,128)(2,1)S(1)}, u32[]{:S(2)}, u32[]{:S(2)}) collective-permute-start(bf16[2,192,1536]{2,1,0:T(8,128)(2,1)} %get-tuple-element.138), channel_id=1, source_target_pairs={{0,8},{4,12},{8,0},{12,4},{16,24},{20,28},{24,16},{28,20},{1,9},{5... | collective-permute-start | bytes 3538952 | tf_op jit(solution)/shard_map/ppermute | solution.py:42
  293.1 34.2 %collective-permute-start.17 = (bf16[2,192,1536]{2,1,0:T(8,128)(2,1)}, bf16[2,192,1536]{2,1,0:T(8,128)(2,1)S(1)}, u32[]{:S(2)}, u32[]{:S(2)}) collective-permute-start(bf16[2,192,1536]{2,1,0:T(8,128)(2,1)} %get-tuple-element.139), channel_id=1, source_target_pairs={{0,16},{4,20},{8,24},{12,28},{16,0},{20,4},{24,8},{28,12},{1,17},{... | collective-permute-start | bytes 3538952 | tf_op jit(solution)/shard_map/ppermute | solution.py:42
  341.7 149.7 %reduce-scatter.8.cloned.1.call-start = ((), (), s32[]{:S(2)}) async-start(), calls=%async_computation.8 | async-start | bytes 3932160 | tf_op jit(solution)/shard_map/reduce_scatter | solution.py:956
  367.9 39.7 %collective-permute-start.20 = (bf16[2,384,2048]{2,1,0:T(8,128)(2,1)}, bf16[2,384,2048]{2,1,0:T(8,128)(2,1)S(1)}, u32[]{:S(2)}, u32[]{:S(2)}) collective-permute-start(bf16[2,384,2048]{2,1,0:T(8,128)(2,1)} %shard_map.353), channel_id=1, source_target_pairs={{0,4},{4,0},{8,12},{12,8},{16,20},{20,16},{24,28},{28,24},{1,5},{5... | collective-permute-start | bytes 9437192 | tf_op jit(solution)/shard_map/ppermute | solution.py:42
  399.7 28.2 %collective-permute-start.19 = (bf16[2,192,1536]{2,1,0:T(8,128)(2,1)}, bf16[2,192,1536]{2,1,0:T(8,128)(2,1)S(1)}, u32[]{:S(2)}, u32[]{:S(2)}) collective-permute-start(bf16[2,192,1536]{2,1,0:T(8,128)(2,1)} %shard_map.354), channel_id=1, source_target_pairs={{0,16},{4,20},{8,24},{12,28},{16,0},{20,4},{24,8},{28,12},{1,17},{... | collective-permute-start | bytes 3538952 | tf_op jit(solution)/shard_map/ppermute | solution.py:42
  421.5 36.0 %collective-permute-start.24 = (bf16[4,192,1152]{2,1,0:T(8,128)(2,1)}, bf16[4,192,1152]{2,1,0:T(8,128)(2,1)S(1)}, u32[]{:S(2)}, u32[]{:S(2)}) collective-permute-start(bf16[4,192,1152]{2,1,0:T(8,128)(2,1)} %get-tuple-element.182), channel_id=1, source_target_pairs={{0,4},{4,0},{8,12},{12,8},{16,20},{20,16},{24,28},{28,24},{1,5},{5... | collective-permute-start | bytes 5308424 | tf_op jit(solution)/shard_map/ppermute | solution.py:42
  439.1 22.3 %collective-permute-start.23 = (f32[6,1536]{1,0:T(8,128)S(1)}, f32[6,1536]{1,0:T(8,128)S(1)}, u32[]{:S(2)}, u32[]{:S(2)}) collective-permute-start(f32[6,1536]{1,0:T(8,128)S(1)} %get-tuple-element.277), channel_id=1, source_target_pairs={{0,1},{1,2},{2,3},{3,0},{4,5},{5,6},{6,7},{7,4},{8,9},{9,10},{10,1... | collective-permute-start | bytes 110600 | tf_op jit(solution)/shard_map/ppermute | solution.py:943
  439.6 23.1 %collective-permute-start.21 = (f32[6,1536]{1,0:T(8,128)S(1)}, f32[6,1536]{1,0:T(8,128)S(1)}, u32[]{:S(2)}, u32[]{:S(2)}) collective-permute-start(f32[6,1536]{1,0:T(8,128)S(1)} %get-tuple-element.278), channel_id=1, source_target_pairs={{0,3},{1,0},{2,1},{3,2},{4,7},{5,4},{6,5},{7,6},{8,11},{9,8},{10,9... | collective-permute-start | bytes 110600 | tf_op jit(solution)/shard_map/ppermute | solution.py:943
  453.2 38.2 %collective-permute-start.28 = (bf16[1,192,1536]{2,1,0:T(8,128)(2,1)}, bf16[1,192,1536]{2,1,0:T(8,128)(2,1)S(1)}, u32[]{:S(2)}, u32[]{:S(2)}) collective-permute-start(bf16[1,192,1536]{2,1,0:T(8,128)(2,1)} %get-tuple-element.147), channel_id=1, source_target_pairs={{0,16},{4,20},{8,24},{12,28},{16,0},{20,4},{24,8},{28,12},{1,17},{... | collective-permute-start | bytes 1769480 | tf_op jit(solution)/shard_map/ppermute | solution.py:42
  457.5 33.9 %collective-permute-start.29 = (bf16[1,192,1536]{2,1,0:T(8,128)(2,1)S(1)}, bf16[1,192,1536]{2,1,0:T(8,128)(2,1)S(1)}, u32[]{:S(2)}, u32[]{:S(2)}) collective-permute-start(bf16[1,192,1536]{2,1,0:T(8,128)(2,1)S(1)} %copy-done.55), channel_id=1, source_target_pairs={{0,8},{4,12},{8,0},{12,4},{16,24},{20,28},{24,16},{28,20},{1,9},{5... | collective-permute-start | bytes 1769480 | tf_op jit(solution)/shard_map/ppermute | solution.py:42
  461.4 22.0 %collective-permute-start.31 = (bf16[1,192,1536]{2,1,0:T(8,128)(2,1)S(1)}, bf16[1,192,1536]{2,1,0:T(8,128)(2,1)S(1)}, u32[]{:S(2)}, u32[]{:S(2)}) collective-permute-start(bf16[1,192,1536]{2,1,0:T(8,128)(2,1)S(1)} %copy-done.30), channel_id=1, source_target_pairs={{0,8},{4,12},{8,0},{12,4},{16,24},{20,28},{24,16},{28,20},{1,9},{5... | collective-permute-start | bytes 1769480 | tf_op jit(solution)/shard_map/ppermute | solution.py:42
  462.7 24.9 %collective-permute-start.32 = (bf16[2,192,1152]{2,1,0:T(8,128)(2,1)}, bf16[2,192,1152]{2,1,0:T(8,128)(2,1)S(1)}, u32[]{:S(2)}, u32[]{:S(2)}) collective-permute-start(bf16[2,192,1152]{2,1,0:T(8,128)(2,1)} %shard_map.362), channel_id=1, source_target_pairs={{0,16},{4,20},{8,24},{12,28},{16,0},{20,4},{24,8},{28,12},{1,17},{... | collective-permute-start | bytes 2654216 | tf_op jit(solution)/shard_map/ppermute | solution.py:42
  463.4 33.5 %collective-permute-start.27 = (f32[7,1536]{1,0:T(8,128)S(1)}, f32[7,1536]{1,0:T(8,128)S(1)}, u32[]{:S(2)}, u32[]{:S(2)}) collective-permute-start(f32[7,1536]{1,0:T(8,128)S(1)} %pad_maximum_fusion.12), channel_id=1, source_target_pairs={{0,4},{4,0},{8,12},{12,8},{16,20},{20,16},{24,28},{28,24},{1,5},{5... | collective-permute-start | bytes 129032 | tf_op jit(solution)/shard_map/ppermute | solution.py:42
  487.2 33.5 %collective-permute-start.34 = (bf16[1,384,512]{2,1,0:T(8,128)(2,1)}, bf16[1,384,512]{2,1,0:T(8,128)(2,1)}, u32[]{:S(2)}, u32[]{:S(2)}) collective-permute-start(bf16[1,384,512]{2,1,0:T(8,128)(2,1)} %get-tuple-element.202), channel_id=1, source_target_pairs={{0,16},{4,20},{8,24},{12,28},{16,0},{20,4},{24,8},{28,12},{1,17},{... | collective-permute-start | bytes 1179656 | tf_op jit(solution)/shard_map/ppermute | solution.py:42
  487.7 33.0 %collective-permute-start.35 = (bf16[1,384,512]{2,1,0:T(8,128)(2,1)}, bf16[1,384,512]{2,1,0:T(8,128)(2,1)}, u32[]{:S(2)}, u32[]{:S(2)}) collective-permute-start(bf16[1,384,512]{2,1,0:T(8,128)(2,1)} %get-tuple-element.203), channel_id=1, source_target_pairs={{0,8},{4,12},{8,0},{12,4},{16,24},{20,28},{24,16},{28,20},{1,9},{5... | collective-permute-start | bytes 1179656 | tf_op jit(solution)/shard_map/ppermute | solution.py:42
  (79 other events, 877.0 us)
Sparse Core Ops, SparseCore 0:
  9.6 70.2 all-gather.3
  82.0 81.3 all-gather.5
  165.5 62.9 all-gather.7
  254.9 58.8 reduce-scatter.3
  341.8 60.4 reduce-scatter.5
  404.5 63.3 reduce-scatter.7
